TPU v7x, 32 devices: a whole 2x2x4 slice. The times are simulated.
32 devices in a mesh: seq: 8 (over z, core), tp: 4 (over y, x).
Axes of the slice: x: 2, y: 2, z: 4, core: 2. Of those that a mesh axis runs over, the one named last changes fastest.
Arguments:
- tokens: bfloat16 [24, 1024, 1600], P('seq', 'tp'), may hold values from -6 to 6
- positions: int32 [24, 1024], P('seq'), may hold values from 0 to 1023, as said below
- ln1_gain: bfloat16 [1600], replicated, may hold values from 0.25 to 1.75
- ln1_bias: bfloat16 [1600], replicated, may hold values from -1.5 to 1.5
- query_key_value_weight: bfloat16 [1600, 4800], P('seq', 'tp'), may hold values from -0.15625 to 0.15625
- qv_bias: bfloat16 [2, 1600], replicated, may hold values from -3 to 3
- attention_output_weight: bfloat16 [1600, 1600], P('seq', 'tp'), may hold values from -0.625 to 0.625
- attention_output_bias: bfloat16 [1600], replicated, may hold values from -1.5 to 1.5
- ln2_gain: bfloat16 [1600], replicated, may hold values from 0.25 to 1.75
- ln2_bias: bfloat16 [1600], replicated, may hold values from -1.5 to 1.5
- expand_weight: bfloat16 [1600, 6400], P('seq', 'tp'), may hold values from -0.15625 to 0.15625
- expand_bias: bfloat16 [6400], replicated, may hold values from -3 to 3
- contract_weight: bfloat16 [6400, 1600], P('tp', 'seq'), may hold values from -0.078125 to 0.078125
- contract_bias: bfloat16 [1600], replicated, may hold values from -1.5 to 1.5
- cotangent: bfloat16 [24, 1024, 1600], P('seq', 'tp'), may hold values from -6 to 6
Outputs:
- layer_out: bfloat16 [24, 1024, 1600], P('seq', 'tp')
- input_grad: bfloat16 [24, 1024, 1600], P('seq', 'tp')
- ln1_gain_grad: float32 [1600], replicated
- ln1_bias_grad: float32 [1600], replicated
- qkv_weight_grad: float32 [1600, 4800], P('seq', 'tp')
- qv_bias_grad: float32 [2, 1600], replicated
- out_weight_grad: float32 [1600, 1600], P('seq', 'tp')
- out_bias_grad: float32 [1600], replicated
- ln2_gain_grad: float32 [1600], replicated
- ln2_bias_grad: float32 [1600], replicated
- fc_weight_grad: float32 [1600, 6400], P('seq', 'tp')
- fc_bias_grad: float32 [6400], replicated
- proj_weight_grad: float32 [6400, 1600], P('tp', 'seq')
- proj_bias_grad: float32 [1600], replicated
Inputs may be any that keep to these rules, and one draw needn't show every extreme that they name: `positions`: each row is a permutation of the places 0 to 1023. With n the devices of tp, the places fall into 2 n blocks of 128; the 1024 / n stored tokens that tp index t holds are, in order, all of some block b and then all of block 2 n - 1 - b, ascending within each; b differs between the indices of tp and is drawn for each sequence.
All inputs are finite; a program needn't handle non-finite values.
Results may differ from a plain program's by a relative error of at most 0.0095.
Values may be sent and summed in bfloat16 or wider, within the bound.
A program may use at most 384 MiB of HBM per device.

v0:
```python
import jax
import jax.numpy as jnp
from jax import lax
from jax.sharding import PartitionSpec as P

HEADS = 25
HEAD = 64


epsilon = 1e-05


def layer_norm(values, norm_gain, norm_shift):
    centred = values - jnp.mean(values, -1, keepdims=True)
    spread = jnp.mean(centred * centred, -1, keepdims=True)
    return centred * lax.rsqrt(spread + epsilon) * norm_gain + norm_shift


def assemble(blocks, row_parts, col_parts):
    inner_rows, inner_cols = (blocks.shape[1], blocks.shape[2])
    stacked = blocks.reshape(row_parts, col_parts, inner_rows, inner_cols).transpose(0, 2, 1, 3)
    return stacked.reshape(row_parts * inner_rows, col_parts * inner_cols)


def split_blocks(matrix, row_parts, col_parts):
    inner_rows = matrix.shape[0] // row_parts
    inner_cols = matrix.shape[1] // col_parts
    stacked = matrix.reshape(row_parts, inner_rows, col_parts, inner_cols).transpose(0, 2, 1, 3)
    return stacked.reshape(row_parts * col_parts, inner_rows, inner_cols)


def masked_scores(q_heads, k_heads, query_pos, key_pos):
    scores = jnp.einsum(
        "qhe,khe->hqk", q_heads, k_heads, preferred_element_type=jnp.float32
    ) * HEAD ** (-0.5)
    visible = key_pos[None, None, :] <= query_pos[None, :, None]
    return jnp.where(visible, scores, -1e30)


def attend_forward(inputs):
    queries, keys_all, values_all, query_pos, key_pos = inputs
    q_heads = queries.reshape(queries.shape[0], HEADS, HEAD)
    k_heads = keys_all.reshape(keys_all.shape[0], HEADS, HEAD)
    v_heads = values_all.reshape(values_all.shape[0], HEADS, HEAD)
    scores = masked_scores(q_heads, k_heads, query_pos, key_pos)
    row_max = jnp.max(scores, -1, keepdims=True)
    exponent = jnp.exp(scores - row_max)
    row_total = jnp.sum(exponent, -1, keepdims=True)
    rounded = (exponent / row_total).astype(jnp.bfloat16)
    mixed = jnp.einsum("hqk,khe->qhe", rounded, v_heads, preferred_element_type=jnp.float32)
    log_total = row_max[..., 0] + jnp.log(row_total[..., 0])
    return (mixed.reshape(queries.shape[0], HEADS * HEAD), log_total)


def attend_backward(inputs):
    queries, keys_all, values_all, query_pos, key_pos, log_total, heads_grad = inputs
    q_heads = queries.reshape(queries.shape[0], HEADS, HEAD)
    k_heads = keys_all.reshape(keys_all.shape[0], HEADS, HEAD)
    v_heads = values_all.reshape(values_all.shape[0], HEADS, HEAD)
    o_grad = heads_grad.reshape(heads_grad.shape[0], HEADS, HEAD)
    scores = masked_scores(q_heads, k_heads, query_pos, key_pos)
    weights = jnp.exp(scores - log_total[..., None])
    rounded = weights.astype(jnp.bfloat16)
    prob_grad = jnp.einsum("qhe,khe->hqk", o_grad, v_heads, preferred_element_type=jnp.float32)
    value_grad = jnp.einsum("hqk,qhe->khe", rounded, o_grad, preferred_element_type=jnp.float32)
    inner = jnp.sum(weights * prob_grad, -1, keepdims=True)
    score_grad = (weights * (prob_grad - inner)).astype(jnp.bfloat16)
    query_grad = jnp.einsum(
        "hqk,khe->qhe", score_grad, k_heads, preferred_element_type=jnp.float32
    ) * HEAD ** (-0.5)
    key_grad = jnp.einsum(
        "hqk,qhe->khe", score_grad, q_heads, preferred_element_type=jnp.float32
    ) * HEAD ** (-0.5)
    key_rows = keys_all.shape[0]
    return (
        key_grad.reshape(key_rows, HEADS * HEAD),
        value_grad.reshape(key_rows, HEADS * HEAD),
        query_grad.reshape(queries.shape[0], HEADS * HEAD),
    )


def body(
    tokens,
    positions,
    ln1_gain,
    ln1_bias,
    query_key_value_weight,
    qv_bias,
    attention_output_weight,
    attention_output_bias,
    ln2_gain,
    ln2_bias,
    expand_weight,
    expand_bias,
    contract_weight,
    contract_bias,
    cotangent,
):
    seq_count = lax.axis_size("seq")
    tp_count = lax.axis_size("tp")
    tp_index = lax.axis_index("tp")
    local_len = tokens.shape[1]
    model_width = tokens.shape[2]
    inputs = tokens.astype(jnp.float32)
    gain_one = ln1_gain.astype(jnp.float32)
    shift_one = ln1_bias.astype(jnp.float32)
    gain_two = ln2_gain.astype(jnp.float32)
    shift_two = ln2_bias.astype(jnp.float32)
    first_normalized = layer_norm(inputs, gain_one, shift_one).astype(jnp.bfloat16)
    qkv_blocks, out_blocks = (
        lax.all_gather(query_key_value_weight[None], ("seq", "tp"), axis=0, tiled=True),
        lax.all_gather(attention_output_weight[None], ("seq", "tp"), axis=0, tiled=True),
    )
    query_key_value_gathered = assemble(qkv_blocks, seq_count, tp_count)
    gathered_output = assemble(out_blocks, seq_count, tp_count)
    contracted_output = jnp.einsum(
        "wjv,vp->wjp",
        first_normalized,
        query_key_value_gathered,
        preferred_element_type=jnp.float32,
    )
    queries = (contracted_output[..., :model_width] + qv_bias[0]).astype(jnp.bfloat16)
    keys_local = contracted_output[..., model_width : 2 * model_width].astype(jnp.bfloat16)
    values_local = (contracted_output[..., 2 * model_width :] + qv_bias[1]).astype(jnp.bfloat16)
    keys_all, values_all = (
        lax.all_gather(keys_local, "tp", axis=1, tiled=True),
        lax.all_gather(values_local, "tp", axis=1, tiled=True),
    )
    query_pos = lax.dynamic_slice_in_dim(positions, tp_index * local_len, local_len, 1)
    mixed, log_total = lax.map(
        attend_forward, (queries, keys_all, values_all, query_pos, positions)
    )
    attention_head_rows = mixed.astype(jnp.bfloat16)
    residual = (
        inputs
        + jnp.einsum(
            "wjv,vp->wjp", attention_head_rows, gathered_output, preferred_element_type=jnp.float32
        )
        + attention_output_bias
    )
    second_normalized = layer_norm(residual, gain_two, shift_two).astype(jnp.bfloat16)
    token_group_rows = lax.all_gather(second_normalized, "tp", axis=1, tiled=True)
    expand_columns, contract_rows = (
        lax.all_gather(expand_weight, "seq", axis=0, tiled=True),
        lax.all_gather(contract_weight, "seq", axis=1, tiled=True),
    )
    hidden_width = expand_columns.shape[1]
    bias_cols = lax.dynamic_slice_in_dim(expand_bias, tp_index * hidden_width, hidden_width)
    preactivation = (
        jnp.einsum(
            "iyg,gn->iyn", token_group_rows, expand_columns, preferred_element_type=jnp.float32
        )
        + bias_cols
    )
    activated_hidden = jax.nn.gelu(preactivation, approximate=True).astype(jnp.bfloat16)
    partial_out = jnp.einsum(
        "btj,jn->btn", activated_hidden, contract_rows, preferred_element_type=jnp.float32
    )
    feed_out = (
        lax.psum_scatter(
            partial_out.astype(jnp.bfloat16), "tp", scatter_dimension=1, tiled=True
        ).astype(jnp.float32)
        + contract_bias
    )
    layer_out = (residual + feed_out).astype(jnp.bfloat16)
    output_rows_local = lax.all_gather(cotangent, "tp", axis=1, tiled=True)
    activation_gradient = jnp.einsum(
        "mtb,yb->mty", output_rows_local, contract_rows, preferred_element_type=jnp.float32
    )
    gelu_value, gelu_pull = jax.vjp(
        lambda argument: jax.nn.gelu(argument, approximate=True), preactivation
    )
    preactivation_gradient = gelu_pull(activation_gradient)[0].astype(jnp.bfloat16)
    contract_gradient_term = jnp.einsum(
        "keo,keg->og", activated_hidden, output_rows_local, preferred_element_type=jnp.float32
    )
    expand_gradient_term = jnp.einsum(
        "ajo,aju->ou", token_group_rows, preactivation_gradient, preferred_element_type=jnp.float32
    )
    fc_bias_part = jnp.sum(preactivation_gradient, axis=(0, 1), dtype=jnp.float32)
    norm_gradient_term = jnp.einsum(
        "gzj,mj->gzm", preactivation_gradient, expand_columns, preferred_element_type=jnp.float32
    )
    norm_two_grad = lax.psum_scatter(norm_gradient_term, "tp", scatter_dimension=1, tiled=True)
    norm_value, norm_two_pull = jax.vjp(layer_norm, residual, gain_two, shift_two)
    resid_from_norm, gain_two_grad, shift_two_grad = norm_two_pull(norm_two_grad)
    resid_grad = cotangent.astype(jnp.float32) + resid_from_norm
    branch_gradient = resid_grad.astype(jnp.bfloat16)
    heads_grad = jnp.einsum(
        "knb,jb->knj", branch_gradient, gathered_output, preferred_element_type=jnp.float32
    ).astype(jnp.bfloat16)
    key_terms, value_terms, query_grad = lax.map(
        attend_backward,
        (queries, keys_all, values_all, query_pos, positions, log_total, heads_grad),
    )
    key_grad, value_grad = (
        lax.psum_scatter(key_terms, "tp", scatter_dimension=1, tiled=True),
        lax.psum_scatter(value_terms, "tp", scatter_dimension=1, tiled=True),
    )
    query_key_value_gradient = jnp.concatenate(
        [
            query_grad.astype(jnp.bfloat16),
            key_grad.astype(jnp.bfloat16),
            value_grad.astype(jnp.bfloat16),
        ],
        axis=-1,
    )
    norm_one_grad = jnp.einsum(
        "knb,jb->knj",
        query_key_value_gradient,
        query_key_value_gathered,
        preferred_element_type=jnp.float32,
    )
    input_value, norm_one_pull = jax.vjp(layer_norm, inputs, gain_one, shift_one)
    input_from_norm, gain_one_grad, shift_one_grad = norm_one_pull(norm_one_grad)
    input_grad = (resid_grad + input_from_norm).astype(jnp.bfloat16)
    query_key_value_term = jnp.einsum(
        "knz,kni->zi",
        first_normalized,
        query_key_value_gradient,
        preferred_element_type=jnp.float32,
    )
    out_term = jnp.einsum(
        "knz,kni->zi", attention_head_rows, branch_gradient, preferred_element_type=jnp.float32
    )
    qkv_parts, out_parts = (
        lax.psum_scatter(
            split_blocks(query_key_value_term, seq_count, tp_count),
            ("seq", "tp"),
            scatter_dimension=0,
            tiled=True,
        ),
        lax.psum_scatter(
            split_blocks(out_term, seq_count, tp_count),
            ("seq", "tp"),
            scatter_dimension=0,
            tiled=True,
        ),
    )
    qkv_weight_grad = qkv_parts[0]
    out_weight_grad = out_parts[0]
    fc_weight_grad, proj_weight_grad = (
        lax.psum_scatter(expand_gradient_term, "seq", scatter_dimension=0, tiled=True),
        lax.psum_scatter(contract_gradient_term, "seq", scatter_dimension=1, tiled=True),
    )
    qv_part = jnp.stack(
        [
            jnp.sum(query_key_value_gradient[..., :model_width], axis=(0, 1), dtype=jnp.float32),
            jnp.sum(
                query_key_value_gradient[..., 2 * model_width :], axis=(0, 1), dtype=jnp.float32
            ),
        ]
    )
    out_bias_part = jnp.sum(branch_gradient, axis=(0, 1), dtype=jnp.float32)
    proj_bias_part = jnp.sum(cotangent, axis=(0, 1), dtype=jnp.float32)
    fc_bias_full = lax.dynamic_update_slice_in_dim(
        jnp.zeros(expand_bias.shape, jnp.float32), fc_bias_part, tp_index * hidden_width, 0
    )
    summed = lax.psum(
        (
            gain_one_grad,
            shift_one_grad,
            qv_part,
            out_bias_part,
            gain_two_grad,
            shift_two_grad,
            fc_bias_full,
            proj_bias_part,
        ),
        ("seq", "tp"),
    )
    return (
        layer_out,
        input_grad,
        summed[0],
        summed[1],
        qkv_weight_grad,
        summed[2],
        out_weight_grad,
        summed[3],
        summed[4],
        summed[5],
        fc_weight_grad,
        summed[6],
        proj_weight_grad,
        summed[7],
    )


def solution(mesh):
    in_specs = (
        P("seq", "tp", None),
        P("seq", None),
        P(),
        P(),
        P("seq", "tp"),
        P(),
        P("seq", "tp"),
        P(),
        P(),
        P(),
        P("seq", "tp"),
        P(),
        P("tp", "seq"),
        P(),
        P("seq", "tp", None),
    )
    out_specs = (
        P("seq", "tp", None),
        P("seq", "tp", None),
        P(),
        P(),
        P("seq", "tp"),
        P(),
        P("seq", "tp"),
        P(),
        P(),
        P(),
        P("seq", "tp"),
        P(),
        P("tp", "seq"),
        P(),
    )
    return jax.shard_map(body, mesh=mesh, in_specs=in_specs, out_specs=out_specs, check_vma=False)
```

profile of v0, /device:TPU:0, one launch (start us, length us, event | category | flops | bytes accessed | tf_op | source)
XLA Modules:
  0.0 3215.7 jit_solution(5160385244400729876)
XLA Ops:
  16.0 110.8 %all-gather.23.cloned.1.call-done = bf16[6400,1200]{1,0:T(8,128)(2,1)} async-done(((bf16[200,1200]{1,0:T(8,128)(2,1)}), bf16[6400,1200]{1,0:T(8,128)(2,1)}) %all-gather.23.cloned.1.call-update) | async-done | bytes 15360016 | tf_op jit(solution)/shard_map/all_gather | solution.py:111
  126.7 13.2 copy.42
  139.9 29.1 reshape.280
  169.1 20.6 fusion.49
  203.2 14.4 copy.35
  229.5 69.4 %all-gather.11.cloned.1.call-done = bf16[3,1024,1600]{1,2,0:T(8,128)(2,1)} async-done(((bf16[3,256,1600]{1,2,0:T(8,128)(2,1)}), bf16[3,1024,1600]{1,2,0:T(8,128)(2,1)}) %all-gather.11.cloned.1.call-update) | async-done | bytes 9830416 | tf_op jit(solution)/shard_map/all_gather | solution.py:127
  298.9 101.8 %all-gather.13.cloned.1.call-done = bf16[3,1024,1600]{1,2,0:T(8,128)(2,1)} async-done(((bf16[3,256,1600]{1,2,0:T(8,128)(2,1)}), bf16[3,1024,1600]{1,2,0:T(8,128)(2,1)}) %all-gather.13.cloned.1.call-update) | async-done | bytes 9830416 | tf_op jit(solution)/shard_map/all_gather | solution.py:126
  402.2 144.4 %while.26 = (s32[]{:T(128)}, bf16[3,256,1600]{1,2,0:T(8,128)(2,1)}, f32[3,25,256]{2,1,0:T(8,128)}, bf16[3,1024,1600]{1,2,0:T(8,128)(2,1)}, s32[3,1024]{1,0:T(4,1...) while((s32[]{:T(128)}, bf16[3,256,1600]{1,2,0:T(8,128)(2,1)}, ...), condition=%wide.region_5.6_spmd, body=%wide.region_2.5_spmd.sunk | while | flops 1756620544 | bytes 104611984 | solution.py:130
  419.9 13.9 fusion.103
  433.8 13.2 fusion.104
  468.1 13.8 fusion.103
  481.9 12.9 fusion.104
  516.0 13.8 fusion.103
  529.8 12.9 fusion.104
  562.7 97.7 %all-gather.15.cloned.1.call-done = bf16[3,1024,1600]{1,2,0:T(8,128)(2,1)} async-done(((bf16[3,256,1600]{1,2,0:T(8,128)(2,1)}), bf16[3,1024,1600]{1,2,0:T(8,128)(2,1)}) %all-gather.15.cloned.1.call-update) | async-done | bytes 9830416 | tf_op jit(solution)/shard_map/all_gather | solution.py:142
  660.4 24.6 fusion.26
  685.0 33.8 %all-gather.19.cloned.1.call-done = bf16[1600,1600]{0,1:T(8,128)(2,1)} async-done(((bf16[1600,200]{0,1:T(8,128)(2,1)}), bf16[1600,1600]{0,1:T(8,128)(2,1)}) %all-gather.19.cloned.1.call-update) | async-done | bytes 5120016 | tf_op jit(solution)/shard_map/all_gather | solution.py:145
  718.8 100.1 %all-gather.21.cloned.1.call-done = bf16[3,1024,1600]{1,2,0:T(8,128)(2,1)} async-done(((bf16[3,256,1600]{1,2,0:T(8,128)(2,1)}), bf16[3,1024,1600]{1,2,0:T(8,128)(2,1)}) %all-gather.21.cloned.1.call-update) | async-done | bytes 9830416 | tf_op jit(solution)/shard_map/all_gather | solution.py:166
  818.9 39.5 %convert_reduce_fusion = (f32[1600]{0:T(1024)}, bf16[3,1024,1600]{1,2,0:T(8,128)(2,1)}) fusion(f32[3,1024,1600]{1,2,0:T(8,128)} %fusion.26, f32[1600]{0:T(1024)S(1)} %dynamic-slice_convert_fusion, bf16[3,1024,1600]{1,2,0:T(8,128)(2,1)} %all-gather.21.cloned.1.call-done, bf16[1600,1600]{0,1:T(8,128)(2,1)} %all-gather.19.cloned.1.call-done), kind=kOutput, calls=%fused_computation.44 | convolution fusion | flops 15841687552 | bytes 44454400 | tf_op jit(solution)/shard_map/mtb,yb->mty/dot_general | solution.py:167
  858.4 24.3 fusion.24
  882.8 25.9 convolution_convert_fusion
  921.8 138.3 %reduce-scatter.15.cloned.1.call-done = f32[3,256,1600]{1,2,0:T(8,128)} async-done(((f32[3,1024,1600]{1,2,0:T(8,128)}), f32[3,256,1600]{1,2,0:T(8,128)}) %reduce-scatter.15.cloned.1.call-update) | async-done | bytes 4915216 | tf_op jit(solution)/shard_map/reduce_scatter | solution.py:184
  1066.3 95.3 %reduce-scatter.13.cloned.1.call-done = bf16[3,256,1600]{1,2,0:T(8,128)(2,1)} async-done(((bf16[3,1024,1600]{1,2,0:T(8,128)(2,1)}), bf16[3,256,1600]{1,2,0:T(8,128)(2,1)}) %reduce-scatter.13.cloned.1.call-update) | async-done | bytes 2457616 | tf_op jit(solution)/shard_map/reduce_scatter | solution.py:160
  1179.9 324.0 %while.27 = (s32[]{:T(128)}, f32[3,1024,1600]{1,2,0:T(8,128)}, f32[3,1024,1600]{1,2,0:T(8,128)}, bf16[3,256,1600]{1,2,0:T(8,128)(2,1)}, bf16[3,256,1600]{1,2,0:T...) while((s32[]{:T(128)}, f32[3,1024,1600]{1,2,0:T(8,128)}, ...), condition=%wide.region_14.15_spmd, body=%wide.region_12.14_spmd.sunk | while | flops 4255999744 | bytes 298037536 | solution.py:192
  1200.6 19.8 multiply_reduce_fusion.5
  1220.3 21.9 multiply_convert_fusion.5
  1242.2 13.6 fusion.116
  1308.4 19.8 multiply_reduce_fusion.5
  1328.2 21.9 multiply_convert_fusion.5
  1350.1 13.6 fusion.116
  1383.3 12.5 constant_dynamic-update-slice_fusion.8
  1416.4 19.8 multiply_reduce_fusion.5
  1436.1 21.9 multiply_convert_fusion.5
  1458.0 13.6 fusion.116
  1504.6 29.6 convolution_bitcast_fusion.1
  1534.3 25.1 convolution_bitcast_fusion.2
  1571.2 18.9 reshape.272
  1590.1 13.9 copy.38
  1606.2 75.1 %reduce-scatter.19.cloned.1.call-done = f32[3,256,1600]{1,2,0:T(8,128)} async-done(((f32[3,1024,1600]{1,2,0:T(8,128)}), f32[3,256,1600]{1,2,0:T(8,128)}) %reduce-scatter.19.cloned.1.call-update) | async-done | bytes 4915216 | tf_op jit(solution)/shard_map/reduce_scatter | solution.py:198
  1685.4 176.0 %reduce-scatter.17.cloned.1.call-done = f32[3,256,1600]{1,2,0:T(8,128)} async-done(((f32[3,1024,1600]{1,2,0:T(8,128)}), f32[3,256,1600]{1,2,0:T(8,128)}) %reduce-scatter.17.cloned.1.call-update) | async-done | bytes 4915216 | tf_op jit(solution)/shard_map/reduce_scatter | solution.py:197
  1865.8 22.0 fusion.51
  1895.6 22.2 convolution_bitcast_fusion
  1917.9 42.1 %reshape.270 = f32[8,200,4,1200]{3,2,1,0:T(4,128)} reshape(f32[1600,4800]{1,0:T(8,128)} %convolution_bitcast_fusion) | data formatting | bytes 61440000 | tf_op jit(solution)/shard_map/reshape | solution.py:28
  1959.9 27.7 copy.37
  1987.7 100.4 %reduce-scatter.25.cloned.1.call-done = f32[200,1600]{1,0:T(8,128)} async-done(((f32[1600,1600]{1,0:T(8,128)}), f32[200,1600]{1,0:T(8,128)}) %reduce-scatter.25.cloned.1.call-update) | async-done | bytes 1280016
  2088.1 282.3 %reduce-scatter.23.cloned.1.call-done = f32[1,200,400]{2,1,0:T(8,128)} async-done(((f32[32,200,400]{2,1,0:T(8,128)}), f32[1,200,400]{2,1,0:T(8,128)}) %reduce-scatter.23.cloned.1.call-update) | async-done | bytes 320016 | tf_op jit(solution)/shard_map/reduce_scatter | solution.py:233
  2370.4 132.7 %all-reduce.5.cloned.1.call-done = (f32[1600]{0:T(1024)}, f32[1600]{0:T(1024)}, f32[2,1600]{1,0:T(2,128)}, f32[1600]{0:T(1024)}, f32[1600]{0:T(1024)}, /*index=5*/f32[1600]{0:T(1024)}, f32[6400]{0:T(1024)}, f32[1600]{0:T(1024)}) async-done(((f32[1600]{0:T(1024)}, f32[1600]{0:T(1024)}, f32[2,1600]{1,0:T(2,128)}, f32[1600]{0:T(1024)}, f32[1600]{0:T(1024)}, /*index=5*/f32[1600]{0:T(1024)}, f32[6400]{0:T(1024)}, ...) | async-done | bytes 76816 | tf_op jit(solution)/shard_map/psum | solution.py:259
  2503.2 695.3 %reduce-scatter.21.cloned.1.call-done = f32[1,200,1200]{2,1,0:T(8,128)} async-done(((f32[32,200,1200]{2,1,0:T(8,128)}), f32[1,200,1200]{2,1,0:T(8,128)}) %reduce-scatter.21.cloned.1.call-update) | async-done | bytes 960016 | tf_op jit(solution)/shard_map/reduce_scatter | solution.py:227
  (279 shorter events, 339.2 us)
Async XLA Ops:
  7.2 119.6 %all-gather.23.cloned.1.call-start = ((), (), s32[]{:S(2)}) async-start(), calls=%async_computation.20 | async-start | bytes 16896000 | tf_op jit(solution)/shard_map/all_gather | solution.py:111
  7.9 195.3 %all-gather.25.cloned.1.call-start = ((), (), s32[]{:S(2)}) async-start(), calls=%async_computation.21 | async-start | bytes 6758400 | tf_op jit(solution)/shard_map/all_gather | solution.py:112
  8.7 290.2 %all-gather.11.cloned.1.call-start = ((), (), s32[]{:S(2)}) async-start(), calls=%async_computation.8 | async-start | bytes 12288000 | tf_op jit(solution)/shard_map/all_gather | solution.py:127
  9.4 159.7 %copy-start.22 = (f32[1600]{0:T(1024)}, f32[1600]{0:T(1024)S(1)}, u32[]{:S(2)}) copy-start(f32[1600]{0:T(1024)S(1)} %convert_element_type.119) | copy-start | bytes 19204
  10.1 159.0 %copy-start.37 = (f32[1600]{0:T(1024)}, f32[1600]{0:T(1024)S(1)}, u32[]{:S(2)}) copy-start(f32[1600]{0:T(1024)S(1)} %convert_element_type.120) | copy-start | bytes 19204
  13.0 156.1 %copy-start.24 = (f32[3,256]{1,0:T(4,128)}, f32[3,256]{1,0:T(4,128)S(1)}, u32[]{:S(2)}) copy-start(f32[3,256]{1,0:T(4,128)S(1)} %broadcast_multiply_fusion.2) | copy-start | bytes 9220
  15.9 153.1 %copy-start.28 = (f32[3,256]{1,0:T(4,128)}, f32[3,256]{1,0:T(4,128)S(1)}, u32[]{:S(2)}) copy-start(f32[3,256]{1,0:T(4,128)S(1)} %fusion.44) | copy-start | bytes 9220
  139.9 29.2 copy-start.5
  195.6 205.0 %all-gather.13.cloned.1.call-start = ((), (), s32[]{:S(2)}) async-start(), calls=%async_computation.9 | async-start | bytes 12288000 | tf_op jit(solution)/shard_map/all_gather | solution.py:126
  200.0 362.7 %all-gather.17.cloned.1.call-start = ((), (), s32[]{:S(2)}) async-start(), calls=%async_computation.11 | async-start | bytes 5990400 | tf_op jit(solution)/shard_map/all_gather | solution.py:144
  200.5 459.8 %all-gather.15.cloned.1.call-start = ((), (), s32[]{:S(2)}) async-start(), calls=%async_computation.10 | async-start | bytes 12288000 | tf_op jit(solution)/shard_map/all_gather | solution.py:142
  546.6 11.7 copy-start.16
  546.6 11.6 copy-start.36
  560.4 158.4 %all-gather.19.cloned.1.call-start = ((), (), s32[]{:S(2)}) async-start(), calls=%async_computation.12 | async-start | bytes 5990400 | tf_op jit(solution)/shard_map/all_gather | solution.py:145
  561.1 257.7 %all-gather.21.cloned.1.call-start = ((), (), s32[]{:S(2)}) async-start(), calls=%async_computation.14 | async-start | bytes 12288000 | tf_op jit(solution)/shard_map/all_gather | solution.py:166
  561.9 498.2 %reduce-scatter.15.cloned.1.call-start = ((), (), s32[]{:S(2)}) async-start(), calls=%async_computation.15 | async-start | bytes 24576000 | tf_op jit(solution)/shard_map/reduce_scatter | solution.py:184
  562.7 320.1 %copy-start.40 = (f32[1600]{0:T(1024)}, f32[1600]{0:T(1024)S(1)}, u32[]{:S(2)}) copy-start(f32[1600]{0:T(1024)S(1)} %dynamic-slice_convert_fusion) | copy-start | bytes 19204
  882.7 278.9 %reduce-scatter.13.cloned.1.call-start = ((), (), s32[]{:S(2)}) async-start(), calls=%async_computation.13 | async-start | bytes 12288000 | tf_op jit(solution)/shard_map/reduce_scatter | solution.py:160
  908.7 772.5 %reduce-scatter.19.cloned.1.call-start = ((), (), s32[]{:S(2)}) async-start(), calls=%async_computation.17 | async-start | bytes 24576000 | tf_op jit(solution)/shard_map/reduce_scatter | solution.py:198
  909.4 150.7 %copy-start.17 = (f32[1600]{0:T(1024)S(1)}, f32[1600]{0:T(1024)}, u32[]{:S(2)}) copy-start(f32[1600]{0:T(1024)} %convert_element_type.130) | copy-start | bytes 19204
  909.4 150.7 %copy-start.21 = (f32[3,256]{1,0:T(4,128)S(1)}, f32[3,256]{1,0:T(4,128)}, u32[]{:S(2)}) copy-start(f32[3,256]{1,0:T(4,128)} %copy-done.20) | copy-start | bytes 9220
  909.4 150.7 %copy-start.27 = (f32[3,256]{1,0:T(4,128)S(1)}, f32[3,256]{1,0:T(4,128)}, u32[]{:S(2)}) copy-start(f32[3,256]{1,0:T(4,128)} %copy-done.26) | copy-start | bytes 9220
  921.8 144.5 %copy-start.35 = (f32[3,256]{1,0:T(4,128)S(1)}, f32[3,256]{1,0:T(4,128)}, u32[]{:S(2)}) copy-start(f32[3,256]{1,0:T(4,128)} %copy-done.34) | copy-start | bytes 9220
  1066.3 101.9 %copy-start.7 = (bf16[3,256,1600]{1,2,0:T(8,128)(2,1)S(1)}, bf16[3,256,1600]{1,2,0:T(8,128)(2,1)}, u32[]{:S(2)}) copy-start(bf16[3,256,1600]{1,2,0:T(8,128)(2,1)} %param.33) | copy-start | bytes 7372804
  1168.2 10.0 copy-start.4
  1168.2 10.0 copy-start.30
  1220.3 21.9 copy-start.1
  1255.8 8.9 copy-start.2
  1275.5 12.4 copy-start.13
  1328.2 21.9 copy-start.1
  1363.7 8.9 copy-start.2
  1383.3 12.5 copy-start.13
  1436.1 21.9 copy-start.1
  1491.3 12.4 copy-start.13
  1503.9 357.6 %reduce-scatter.17.cloned.1.call-start = ((), (), s32[]{:S(2)}) async-start(), calls=%async_computation.16 | async-start | bytes 24576000 | tf_op jit(solution)/shard_map/reduce_scatter | solution.py:197
  1504.4 483.2 %reduce-scatter.27.cloned.1.call-start = ((), (), s32[]{:S(2)}) async-start(), calls=%async_computation.23 | async-start | bytes 11980800
  1534.3 553.9 %reduce-scatter.25.cloned.1.call-start = ((), (), s32[]{:S(2)}) async-start(), calls=%async_computation.22 | async-start | bytes 11980800
  1559.4 811.0 %reduce-scatter.23.cloned.1.call-start = ((), (), s32[]{:S(2)}) async-start(), calls=%async_computation.19 | async-start | bytes 13516800 | tf_op jit(solution)/shard_map/reduce_scatter | solution.py:233
  1604.1 899.1 %all-reduce.5.cloned.1.call-start = ((), (), s32[]{:S(2)}) async-start(), calls=%async_computation.24 | async-start | bytes 182272 | tf_op jit(solution)/shard_map/psum | solution.py:259
  1605.2 260.5 %copy-start.19 = (f32[6400]{0:T(1024)}, f32[6400]{0:T(1024)S(1)}, u32[]{:S(2)}) copy-start(f32[6400]{0:T(1024)S(1)} %dynamic_update_slice.21) | copy-start | bytes 76804
  1685.4 180.4 %copy-start.6 = (bf16[3,256,1600]{1,2,0:T(8,128)(2,1)S(1)}, bf16[3,256,1600]{1,2,0:T(8,128)(2,1)}, u32[]{:S(2)}) copy-start(bf16[3,256,1600]{1,2,0:T(8,128)(2,1)} %param.19) | copy-start | bytes 7372804
  1685.4 180.4 %copy-start.23 = (f32[1600]{0:T(1024)S(1)}, f32[1600]{0:T(1024)}, u32[]{:S(2)}) copy-start(f32[1600]{0:T(1024)} %copy-done.22) | copy-start | bytes 19204
  1685.4 180.4 %copy-start.25 = (f32[3,256]{1,0:T(4,128)S(1)}, f32[3,256]{1,0:T(4,128)}, u32[]{:S(2)}) copy-start(f32[3,256]{1,0:T(4,128)} %copy-done.24) | copy-start | bytes 9220
  1865.7 25.4 slice-start
  1865.8 22.0 copy-start.33
  1865.8 22.0 copy-start.29
  1865.8 25.4 slice-start.1
  1895.6 1302.9 %reduce-scatter.21.cloned.1.call-start = ((), (), s32[]{:S(2)}) async-start(), calls=%async_computation.18 | async-start | bytes 33792000 | tf_op jit(solution)/shard_map/reduce_scatter | solution.py:227
  (31 other events, 126.1 us)
Sparse Core Ops, SparseCore 0:
  10.9 115.7 all-gather.22
  129.6 68.7 all-gather.24
  200.9 97.9 all-gather.10
  301.1 99.4 all-gather.12
  402.1 56.7 all-gather.16
  560.5 99.8 all-gather.14
  662.0 56.7 all-gather.18
  720.6 98.2 all-gather.20
  882.9 177.1 reduce-scatter.14
  1063.4 98.1 reduce-scatter.12
  1504.0 177.2 reduce-scatter.18
  1684.2 177.1 reduce-scatter.16
  1864.4 111.2 reduce-scatter.26
  1978.5 109.5 reduce-scatter.24
  2090.9 279.4 reduce-scatter.22
  2377.8 125.2 all-reduce.4
  2506.0 692.3 reduce-scatter.20
where the time goes:
time: 3230 us; the launch traced here: 3220 us
  waiting for transfers between devices  2210 us (68%)
  matrix products  518 us (16%)
  local copies, waits for them, and re-layouts  308 us (10%)
  other arithmetic  161 us (5%)
    reduce_scatter x1, waiting for transfers between devices, body(): lax.psum_scatter(split_blocks(query_key_value_term, seq_count, tp_count),...  695 us
    reduce_scatter x1, waiting for transfers between devices, body(): lax.psum_scatter(split_blocks(out_term, seq_count, tp_count), ('seq', 'tp...  282 us
    reduce_scatter x1, waiting for transfers between devices, body(): lax.psum_scatter(key_terms, 'tp', scatter_dimension=1, tiled=True)  176 us
    reduce_scatter x1, waiting for transfers between devices, body(): lax.psum_scatter(norm_gradient_term, 'tp', scatter_dimension=1, tiled=True)  138 us
    psum x1, waiting for transfers between devices, body(): lax.psum((gain_one_grad, shift_one_grad, qv_part, out_bias_part, gain_two...  133 us
    all_gather x1, waiting for transfers between devices, body(): lax.all_gather(query_key_value_weight[None], ('seq', 'tp'), axis=0, tiled...  111 us
    unnamed x19, waiting for transfers between devices  104 us
    all_gather x1, waiting for transfers between devices, body(): lax.all_gather(keys_local, 'tp', axis=1, tiled=True)  102 us
  transfers between devices with their start and end apart: 17, of which 14 were waited for; matrix products, arithmetic and copies ran while one was open for 17% of the time, Pallas kernels for 0%

commit v1 on v0

v1 whole, which is shorter than its diff:
```python
import functools
import jax
import jax.numpy as jnp
from jax import lax
from jax.experimental import pallas as pl
from jax.experimental.pallas import tpu as pltpu
from jax.sharding import PartitionSpec as P

HEADS = 25
HEAD = 64
LANES = 128
TILE = 256
epsilon = 1e-05
F32 = jnp.float32
BF16 = jnp.bfloat16
NN = (((1,), (0,)), ((), ()))
NT = (((1,), (1,)), ((), ()))
TN = (((0,), (0,)), ((), ()))


def dot(left, right, dims=NN):
    return lax.dot_general(left, right, dims, preferred_element_type=F32)


def load_blocks(place_ref, span, count, source, target):
    for n in range(count):
        rows = pl.ds(pl.multiple_of(place_ref[n] * span, span), span)
        target[rows, :] = source(n)


def attend_forward(span, pieces, odd, place_ref, qkv_ref, *refs):
    out_refs, lse_ref = refs[:pieces], refs[pieces]
    queries, keys, values, mixed = refs[pieces + 1 :]
    pair, pairs = pl.program_id(0), pl.num_programs(0)
    for part, target in enumerate((queries, keys, values)):
        columns = slice(part * LANES, (part + 1) * LANES)
        load_blocks(
            place_ref, span, 2 * pieces, lambda n: qkv_ref[n * span : (n + 1) * span, columns], target
        )
    length = queries.shape[0]

    def one_head(head):
        lane = lax.broadcasted_iota(jnp.int32, (TILE, LANES), 1)
        mine = (lane // HEAD) == head
        for first in range(0, length, TILE):
            last = first + TILE
            query = jnp.where(mine, queries[first:last, :] * BF16(HEAD**-0.5), BF16(0))
            scores = dot(query, keys[0:last, :], NT)
            row = lax.broadcasted_iota(jnp.int32, (TILE, TILE), 0)
            column = lax.broadcasted_iota(jnp.int32, (TILE, TILE), 1)
            corner = jnp.where(column <= row, scores[:, first:last], -1e30)
            scores = corner if first == 0 else jnp.concatenate([scores[:, :first], corner], axis=1)
            row_max = jnp.max(scores, 1, keepdims=True)
            weights = jnp.exp(scores - row_max)
            total = jnp.sum(weights, 1, keepdims=True)
            part = dot(weights.astype(BF16), values[0:last, :]) / total
            lse_ref[0, head, first:last] = (row_max + jnp.log(total))[:, 0]
            if head == 0:
                mixed[first:last, :] = jnp.where(mine, part, 0.0).astype(BF16)
            else:
                mixed[first:last, :] = jnp.where(mine, part.astype(BF16), mixed[first:last, :])

    one_head(0)
    if odd:
        pl.when(pair < pairs - 1)(lambda: one_head(1))
    else:
        one_head(1)
    for piece in range(pieces):
        for half in range(2):
            rows = pl.ds(pl.multiple_of(place_ref[2 * piece + half] * span, span), span)
            out_refs[piece][half * span : (half + 1) * span, :] = mixed[rows, :]


def attend_backward(span, pieces, odd, place_ref, qkv_ref, *refs):
    grad_refs, lse_ref, out_ref = refs[:pieces], refs[pieces], refs[pieces + 1]
    queries, keys, values, grads, query_grad, key_sum, value_sum = refs[pieces + 2 :]
    pair, pairs = pl.program_id(0), pl.num_programs(0)
    for part, target in enumerate((queries, keys, values)):
        columns = slice(part * LANES, (part + 1) * LANES)
        load_blocks(
            place_ref, span, 2 * pieces, lambda n: qkv_ref[n * span : (n + 1) * span, columns], target
        )
    load_blocks(
        place_ref,
        span,
        2 * pieces,
        lambda n: grad_refs[n // 2][(n % 2) * span : (n % 2 + 1) * span, :],
        grads,
    )
    length = queries.shape[0]

    def one_head(head):
        lane = lax.broadcasted_iota(jnp.int32, (TILE, LANES), 1)
        mine = (lane // HEAD) == head
        for first in reversed(range(0, length, TILE)):
            last = first + TILE
            query = jnp.where(mine, queries[first:last, :] * BF16(HEAD**-0.5), BF16(0))
            grad = jnp.where(mine, grads[first:last, :], BF16(0))
            scores = dot(query, keys[0:last, :], NT)
            row = lax.broadcasted_iota(jnp.int32, (TILE, TILE), 0)
            column = lax.broadcasted_iota(jnp.int32, (TILE, TILE), 1)
            corner = jnp.where(column <= row, scores[:, first:last], -1e30)
            scores = corner if first == 0 else jnp.concatenate([scores[:, :first], corner], axis=1)
            weights = jnp.exp(scores - lse_ref[0, head, first:last][:, None])
            prob_grad = dot(grad, values[0:last, :], NT)
            product = weights * prob_grad
            inner = jnp.sum(product, 1, keepdims=True)
            score_grad = (product - weights * inner).astype(BF16)
            rounded = weights.astype(BF16)
            part = (dot(score_grad, keys[0:last, :]) * HEAD**-0.5).astype(BF16)
            key_part = dot(query, score_grad, TN)
            value_part = dot(grad, rounded, TN)
            if head == 0 and last == length:
                key_sum[...] = key_part
                value_sum[...] = value_part
            else:
                key_sum[:, 0:last] += key_part
                value_sum[:, 0:last] += value_part
            if head == 0:
                query_grad[first:last, :] = jnp.where(mine, part, BF16(0))
            else:
                query_grad[first:last, :] = jnp.where(mine, part, query_grad[first:last, :])

    one_head(0)
    if odd:
        pl.when(pair < pairs - 1)(lambda: one_head(1))
    else:
        one_head(1)
    keys[...] = key_sum[...].T.astype(BF16)
    values[...] = value_sum[...].T.astype(BF16)
    for n in range(2 * pieces):
        rows = pl.ds(pl.multiple_of(place_ref[n] * span, span), span)
        target = slice(n * span, (n + 1) * span)
        out_ref[target, 0:LANES] = query_grad[rows, :]
        out_ref[target, LANES : 2 * LANES] = keys[rows, :]
        out_ref[target, 2 * LANES :] = values[rows, :]


def call_forward(places, qkv, span, heads):
    length, width = qkv.shape
    pairs, pieces = width // (3 * LANES), length // (2 * span)
    return pl.pallas_call(
        functools.partial(attend_forward, span, pieces, heads % 2 == 1),
        grid_spec=pltpu.PrefetchScalarGridSpec(
            num_scalar_prefetch=1,
            grid=(pairs,),
            in_specs=[pl.BlockSpec((length, 3 * LANES), lambda j, p: (0, j))],
            out_specs=[pl.BlockSpec((2 * span, LANES), lambda j, p: (0, j))] * pieces
            + [pl.BlockSpec((1, 2, length), lambda j, p: (j, 0, 0))],
            scratch_shapes=[pltpu.VMEM((length, LANES), BF16)] * 4,
        ),
        out_shape=[jax.ShapeDtypeStruct((2 * span, pairs * LANES), BF16)] * pieces
        + [jax.ShapeDtypeStruct((pairs, 2, length), F32)],
        compiler_params=pltpu.CompilerParams(vmem_limit_bytes=40 * 2**20),
        cost_estimate=pl.CostEstimate(
            flops=heads * length * length * 5 * 256,
            bytes_accessed=4 * length * width,
            transcendentals=heads * length * length,
        ),
        name="attend_forward",
    )(places, qkv)


def call_backward(places, qkv, grads, lse, span, heads):
    length, width = qkv.shape
    pairs, pieces = width // (3 * LANES), length // (2 * span)
    return pl.pallas_call(
        functools.partial(attend_backward, span, pieces, heads % 2 == 1),
        grid_spec=pltpu.PrefetchScalarGridSpec(
            num_scalar_prefetch=1,
            grid=(pairs,),
            in_specs=[pl.BlockSpec((length, 3 * LANES), lambda j, p: (0, j))]
            + [pl.BlockSpec((2 * span, LANES), lambda j, p: (0, j))] * pieces
            + [pl.BlockSpec((1, 2, length), lambda j, p: (j, 0, 0))],
            out_specs=pl.BlockSpec((length, 3 * LANES), lambda j, p: (0, j)),
            scratch_shapes=[pltpu.VMEM((length, LANES), BF16)] * 5
            + [pltpu.VMEM((LANES, length), F32)] * 2,
        ),
        out_shape=jax.ShapeDtypeStruct(qkv.shape, BF16),
        compiler_params=pltpu.CompilerParams(vmem_limit_bytes=40 * 2**20),
        cost_estimate=pl.CostEstimate(
            flops=heads * length * length * 8 * 256,
            bytes_accessed=6 * length * width,
            transcendentals=heads * length * length,
        ),
        name="attend_backward",
    )(places, qkv, *grads, lse)


def statistics(values):
    centred = values - jnp.mean(values, -1, keepdims=True)
    spread = jnp.mean(centred * centred, -1, keepdims=True)
    inverse = lax.rsqrt(spread + epsilon)
    return centred * inverse, inverse


def norm_forward(values, gain, shift):
    return (statistics(values)[0] * gain + shift).astype(BF16)


def norm_backward(values, gain, grad):
    normal, inverse = statistics(values)
    scaled = grad * gain
    spread = jnp.mean(scaled * normal, -1, keepdims=True)
    result = inverse * (scaled - jnp.mean(scaled, -1, keepdims=True) - normal * spread)
    return result, jnp.sum(grad * normal, 0), jnp.sum(grad, 0)


def gelu_pair(u):
    scale = 0.7978845608028654
    inner = jnp.tanh(scale * (u + 0.044715 * (u * u * u)))
    value = 0.5 * u * (1.0 + inner)
    slope = 0.5 * (1.0 + inner) + 0.5 * u * (1.0 - inner * inner) * scale * (1.0 + 0.134145 * (u * u))
    return value, slope


def body(
    seq_count,
    tp_count,
    tokens,
    positions,
    ln1_gain,
    ln1_bias,
    query_key_value_weight,
    qv_bias,
    attention_output_weight,
    attention_output_bias,
    ln2_gain,
    ln2_bias,
    expand_weight,
    expand_bias,
    contract_weight,
    contract_bias,
    cotangent,
):
    devices = seq_count * tp_count
    both = ("seq", "tp")
    t = lax.axis_index("tp")
    core = lax.axis_index("seq") % 2
    core_bit = tp_count
    tp_bits = [1 << k for k in range(tp_count.bit_length() - 1)]
    high = tp_bits[-1]
    ff_bits = tp_bits[:-1] + [core_bit]
    chunks, rows, width = tokens.shape
    span = rows // 2
    length = rows * tp_count
    group_heads = -(-HEADS // tp_count)
    group = group_heads * HEAD
    pairs = -(-group_heads // 2)
    padded = pairs * LANES
    hidden = expand_weight.shape[1]
    peers = t ^ jnp.arange(tp_count)

    def swap(value, mask):
        return lax.ppermute(value, both, [(i, i ^ mask) for i in range(devices)])

    def gather_tp(value):
        if tp_count != 4:
            pieces = [value]
            for bit in tp_bits:
                pieces += [swap(piece, bit) for piece in pieces]
            return jnp.concatenate(pieces, 0)
        one, two = swap(value, 1), swap(value, 2)
        return jnp.concatenate([value, one, two, swap(one[:span], 2), swap(two[span:], 1)], 0)

    def sum_tp(partial):
        pieces = [partial[r * rows : (r + 1) * rows] for r in range(tp_count)]
        if tp_count != 4:
            for bit in reversed(tp_bits):
                pieces = [
                    piece + swap(other.astype(BF16), bit)
                    for piece, other in zip(pieces[:bit], pieces[bit:], strict=True)
                ]
            return pieces[0]
        upper = swap(pieces[3][:span].astype(BF16), 2)
        lower = swap(pieces[3][span:].astype(BF16), 1)
        one = jnp.concatenate([pieces[1][:span] + upper, pieces[1][span:]], 0)
        two = jnp.concatenate([pieces[2][:span], pieces[2][span:] + lower], 0)
        return pieces[0] + swap(one.astype(BF16), 1) + swap(two.astype(BF16), 2)

    def gather_ff(value):
        pieces = [value]
        for bit in ff_bits:
            pieces += [swap(piece, bit) for piece in pieces]
        return jnp.concatenate(pieces, 0)

    def sum_ff(partial):
        count = len(partial) // rows
        pieces = [partial[r * rows : (r + 1) * rows] for r in range(count)]
        while len(pieces) > 1:
            half = len(pieces) // 2
            bit = ff_bits[half.bit_length() - 1]
            pieces = [
                piece + swap(other.astype(BF16), bit)
                for piece, other in zip(pieces[:half], pieces[half:], strict=True)
            ]
        return pieces[0]

    def sum_all(value):
        for k in range(devices.bit_length() - 1):
            value = value + swap(value, 1 << k)
        return value

    def wanted(owner):
        index = lax.broadcasted_iota(jnp.int32, (1, 3 * padded), 1)
        within = index // (3 * LANES) * LANES + index % LANES
        feature = owner * group + within
        valid = (within < group) & (feature < width)
        return jnp.where(valid, index // LANES % 3 * width + feature, -1)

    columns = query_key_value_weight.shape[1]
    shard_index = lax.broadcasted_iota(jnp.int32, (columns, 1), 0)
    pick = jnp.concatenate(
        [(shard_index + columns * (t ^ r) == wanted(t)).astype(BF16) for r in range(tp_count)], 0
    )
    qkv_shards = [query_key_value_weight] + [swap(query_key_value_weight, r) for r in range(1, tp_count)]
    qkv_rows = dot(jnp.concatenate(qkv_shards, 1), pick).astype(BF16)
    qkv_weight = lax.all_gather(qkv_rows, "seq", axis=0, tiled=True)

    inputs = tokens.astype(F32)
    gain_one, shift_one = ln1_gain.astype(F32), ln1_bias.astype(F32)
    gain_two, shift_two = ln2_gain.astype(F32), ln2_bias.astype(F32)

    def head_columns(vector):
        whole = jnp.pad(vector, (0, tp_count * group - width))
        mine = lax.dynamic_slice_in_dim(whole, t * group, group)
        return jnp.pad(mine, (0, padded - group)).reshape(pairs, LANES)

    query_bias, value_bias = head_columns(qv_bias[0]), head_columns(qv_bias[1])
    qkv_bias = jnp.stack([query_bias, jnp.zeros_like(query_bias), value_bias], 1).reshape(-1)

    place = positions.reshape(chunks, tp_count, 2, span)[:, :, :, 0] // span
    places = jnp.take(place, peers, axis=1).reshape(chunks, 2 * tp_count)

    normal_one = [None] * chunks
    qkv, lse, own_out = [None] * chunks, [None] * chunks, [None] * chunks
    for c in range(chunks):
        normal_one[c] = gather_tp(norm_forward(inputs[c], gain_one, shift_one))

    out_row = [attention_output_weight] + [swap(attention_output_weight, r) for r in range(1, tp_count)]
    out_row = jnp.stack(out_row, 0)
    out_row = jnp.take(out_row, peers, axis=0).transpose(1, 0, 2).reshape(-1, width)
    out_whole = lax.all_gather(out_row, "seq", axis=0, tiled=True)
    out_whole = jnp.pad(out_whole, ((0, tp_count * group - width), (0, 0)))
    out_weight = [
        jnp.pad(
            lax.dynamic_slice_in_dim(out_whole, (t ^ r) * group, group, 0), ((0, padded - group), (0, 0))
        )
        for r in range(tp_count)
    ]

    stays = core == t // high
    block = t % high + core * high
    send = [
        (s * tp_count + i, s * tp_count + (i ^ high))
        for s in range(seq_count)
        for i in range(tp_count)
        if s % 2 == i // high
    ]

    def gather_block(shard):
        whole = lax.all_gather(shard, "seq", axis=0, tiled=True)
        return jnp.where(stays, whole, lax.ppermute(whole, both, send))

    expand = gather_block(expand_weight)
    contract = gather_block(contract_weight.T)
    hidden_bias = lax.dynamic_slice_in_dim(expand_bias, block * hidden, hidden).astype(F32)

    for c in range(chunks):
        qkv[c] = (dot(normal_one[c], qkv_weight) + qkv_bias).astype(BF16)
        *own_out[c], lse[c] = call_forward(places[c], qkv[c], span, group_heads)

    mixed, residual = [None] * chunks, [None] * chunks
    normal_two, output_rows = [None] * chunks, [None] * chunks
    for c in range(chunks):
        pieces = own_out[c]
        mixed[c] = jnp.concatenate([pieces[0]] + [swap(pieces[r], r) for r in range(1, tp_count)], 1)
        residual[c] = inputs[c] + dot(mixed[c], jnp.concatenate(out_weight, 0)) + attention_output_bias
        normal_two[c] = gather_ff(norm_forward(residual[c], gain_two, shift_two))
        output_rows[c] = gather_ff(cotangent[c])

    layer_out = []
    expand_grad = contract_grad = hidden_bias_grad = 0.0
    gain_two_grad = shift_two_grad = 0.0
    resid_grad, branch = [None] * chunks, [None] * chunks
    head_grads = [None] * chunks
    for c in range(chunks):
        activation_grad = dot(output_rows[c], contract)
        hidden_in = dot(normal_two[c], expand) + hidden_bias
        value, slope = gelu_pair(hidden_in)
        value = value.astype(BF16)
        hidden_grad = (activation_grad * slope).astype(BF16)
        feed = sum_ff(dot(value, contract, NT))
        layer_out.append((residual[c] + feed + contract_bias).astype(BF16))
        expand_grad = expand_grad + dot(normal_two[c], hidden_grad, TN)
        contract_grad = contract_grad + dot(output_rows[c], value, TN)
        hidden_bias_grad = hidden_bias_grad + jnp.sum(hidden_grad, 0, dtype=F32)
        norm_grad = sum_ff(dot(hidden_grad, expand, NT))
        from_norm, gain_part, shift_part = norm_backward(residual[c], gain_two, norm_grad)
        gain_two_grad, shift_two_grad = gain_two_grad + gain_part, shift_two_grad + shift_part
        resid_grad[c] = cotangent[c].astype(F32) + from_norm
        branch[c] = resid_grad[c].astype(BF16)
        pieces = [dot(branch[c], out_weight[r], NT).astype(BF16) for r in range(tp_count)]
        head_grads[c] = [pieces[0]] + [swap(pieces[r], r) for r in range(1, tp_count)]

    def sum_block(partial):
        rounded = partial.astype(BF16)
        other = lax.ppermute(rounded, both, [(b, a) for a, b in send])
        mine = jnp.where(stays, partial + other, 0.0).astype(BF16)
        return lax.psum_scatter(mine, "seq", scatter_dimension=0, tiled=True).astype(F32)

    fc_weight_grad = sum_block(expand_grad)
    proj_weight_grad = sum_block(contract_grad).T

    all_mixed, all_branch = jnp.concatenate(mixed, 0), jnp.concatenate(branch, 0)
    out_grad = dot(all_mixed, all_branch, TN).reshape(tp_count, padded, width)
    out_grad = out_grad[:, :group].astype(BF16)
    out_grad = jnp.take(out_grad, peers, axis=0).reshape(tp_count * group, width)[:width]
    out_grad = lax.psum_scatter(out_grad, "seq", scatter_dimension=0, tiled=True)
    out_grad = out_grad.reshape(-1, tp_count, width // tp_count).transpose(1, 0, 2)
    out_grad = jnp.take(out_grad, peers, axis=0)
    out_weight_grad = out_grad[0].astype(F32)
    for r in range(1, tp_count):
        out_weight_grad = out_weight_grad + swap(out_grad[r], r)

    qkv_grad, qkv_bias_grad = 0.0, 0.0
    gain_one_grad = shift_one_grad = 0.0
    input_grad = []
    for c in range(chunks):
        grads = call_backward(places[c], qkv[c], head_grads[c], lse[c], span, group_heads)
        norm_grad = sum_tp(dot(grads, qkv_weight, NT))
        qkv_grad = qkv_grad + dot(normal_one[c], grads, TN)
        qkv_bias_grad = qkv_bias_grad + jnp.sum(grads, 0, dtype=F32)
        from_norm, gain_part, shift_part = norm_backward(inputs[c], gain_one, norm_grad)
        gain_one_grad, shift_one_grad = gain_one_grad + gain_part, shift_one_grad + shift_part
        input_grad.append((resid_grad[c] + from_norm).astype(BF16))

    summed = lax.psum_scatter(qkv_grad.astype(BF16), "seq", scatter_dimension=0, tiled=True)
    spread = jnp.concatenate([summed] + [swap(summed, r) for r in range(1, tp_count)], 1)
    shard_column = lax.broadcasted_iota(jnp.int32, (1, columns), 1) + columns * t
    place_back = jnp.concatenate(
        [
            (wanted(t ^ r).reshape(-1, 1) == shard_column).astype(BF16)
            for r in range(tp_count)
        ],
        0,
    )
    qkv_weight_grad = dot(spread, place_back)

    qkv_bias_grad = qkv_bias_grad.reshape(pairs, 3, LANES)

    def whole_bias(part):
        mine = qkv_bias_grad[:, part].reshape(-1)[:group]
        whole = jnp.zeros((tp_count * group,), F32)
        return lax.dynamic_update_slice_in_dim(whole, mine, t * group, 0)[:width]

    hidden_whole = lax.dynamic_update_slice_in_dim(
        jnp.zeros(expand_bias.shape, F32), hidden_bias_grad, block * hidden, 0
    )
    out_bias_part = jnp.sum(all_branch, 0, dtype=F32)
    proj_bias_part = jnp.sum(cotangent, axis=(0, 1), dtype=F32)
    early = sum_all(
        jnp.concatenate([gain_two_grad, shift_two_grad, out_bias_part, proj_bias_part, hidden_whole])
    )
    late = sum_all(jnp.concatenate([gain_one_grad, shift_one_grad, whole_bias(0), whole_bias(2)]))

    def part(vector, index):
        return vector[index * width : (index + 1) * width]

    return (
        jnp.stack(layer_out),
        jnp.stack(input_grad),
        part(late, 0),
        part(late, 1),
        qkv_weight_grad,
        late[2 * width :].reshape(2, width),
        out_weight_grad,
        part(early, 2),
        part(early, 0),
        part(early, 1),
        fc_weight_grad,
        early[4 * width :],
        proj_weight_grad,
        part(early, 3),
    )


def solution(mesh):
    in_specs = (
        P("seq", "tp", None),
        P("seq", None),
        P(),
        P(),
        P("seq", "tp"),
        P(),
        P("seq", "tp"),
        P(),
        P(),
        P(),
        P("seq", "tp"),
        P(),
        P("tp", "seq"),
        P(),
        P("seq", "tp", None),
    )
    out_specs = (
        P("seq", "tp", None),
        P("seq", "tp", None),
        P(),
        P(),
        P("seq", "tp"),
        P(),
        P("seq", "tp"),
        P(),
        P(),
        P(),
        P("seq", "tp"),
        P(),
        P("tp", "seq"),
        P(),
    )
    placed = functools.partial(body, mesh.shape["seq"], mesh.shape["tp"])
    return jax.shard_map(placed, mesh=mesh, in_specs=in_specs, out_specs=out_specs, check_vma=False)
```

time: 3230 us -> 1090 us (0.34)
  waiting for transfers between devices: 2210 us -> 310 us
  local copies, waits for them, and re-layouts: 308 us -> 82.1 us
  matrix products: 518 us -> 336 us
  starting transfers between devices: 0.89 us -> 114 us
  Pallas kernels: 0 us -> 103 us
  other arithmetic: 161 us -> 115 us
    reduce_scatter x6 -> x1, waiting for transfers between devices: 1460 us -> 0.01 us  [body(): lax.psum_scatter(qkv_grad.astype(BF16), 'seq', scatter_dimension=0, tiled...]
    all_gather x8 -> x4, waiting for transfers between devices: 513 us -> 0.03 us  [the longest x1 0.02 us: body(): qkv_weight = lax.all_gather(qkv_rows, 'seq', axis=0, tiled=True)]
    ppermute x0 -> x104, waiting for transfers between devices: none -> 309 us  [the longest x100 309 us: swap(): return lax.ppermute(value, both, [(i, i ^ mask) for i in range(devices)])]
    dot_general x33 -> x45, matrix products: 518 us -> 336 us  [dot(): return lax.dot_general(left, right, dims, preferred_element_type=F32)]
    psum x1 -> x0, waiting for transfers between devices: 133 us -> none  [body(): lax.psum((gain_one_grad, shift_one_grad, qv_part, out_bias_part, gain_two...]
    reshape x7 -> x5, local copies, waits for them, and re-layouts: 142 us -> 16.5 us  [the longest x1 9.59 us: body(): out_grad = dot(all_mixed, all_branch, TN).reshape(tp_count, padded, width)]
    ppermute x0 -> x104, starting transfers between devices: none -> 114 us  [the longest x100 101 us: swap(): return lax.ppermute(value, both, [(i, i ^ mask) for i in range(devices)])]
    unnamed x19 -> x11, waiting for transfers between devices: 104 us -> 0.8 us
  transfers between devices with their start and end apart: 17 -> 112, of which waited for: 14 -> 37; matrix products, arithmetic and copies ran while one was open for 17% -> 47% of each run, Pallas kernels for 0% -> 8%
where the time goes in v1:
time: 1090 us; the launch traced here: 1080 us
  matrix products  336 us (31%)
  waiting for transfers between devices  310 us (28%)
  other arithmetic  115 us (11%)
  starting transfers between devices  114 us (10%)
  Pallas kernels  103 us (9%)
  local copies, waits for them, and re-layouts  82.1 us (8%)
  between operations  17.3 us (2%)
    dot_general x45, matrix products, dot(): return lax.dot_general(left, right, dims, preferred_element_type=F32)  336 us
    ppermute x100, waiting for transfers between devices, swap(): return lax.ppermute(value, both, [(i, i ^ mask) for i in range(devices)])  309 us
    ppermute x100, starting transfers between devices, swap(): return lax.ppermute(value, both, [(i, i ^ mask) for i in range(devices)])  101 us
    pallas_call x3, Pallas kernels, call_backward(): pl.pallas_call(functools.partial(attend_backward, span, pieces, heads % 2...  62.1 us
    pallas_call x3, Pallas kernels, call_forward(): pl.pallas_call(functools.partial(attend_forward, span, pieces, heads % 2...  41.4 us
    unnamed x380, local copies, waits for them, and re-layouts  23.6 us
  transfers between devices with their start and end apart: 112, of which 37 were waited for; matrix products, arithmetic and copies ran while one was open for 47% of the time, Pallas kernels for 8%

profile of v1, /device:TPU:0, one launch (start us, length us, event | category | flops | bytes accessed | tf_op | source)
XLA Modules:
  0.0 1079.2 jit_solution(505753056111586552)
XLA Ops:
  23.7 11.6 %collective-permute-done.5 = bf16[200,1200]{1,0:T(8,128)(2,1)S(1)} collective-permute-done((bf16[200,1200]{1,0:T(8,128)(2,1)}, bf16[200,1200]{1,0:T(8,128)(2,1)S(1)}, u32[]{:S(2)}, u32[]{:S(2)}) %collective-permute-start.5) | collective-permute-done | bytes 480032 | tf_op jit(solution)/shard_map/ppermute | solution.py:255
  72.6 14.9 %collective-permute-done.34 = bf16[256,1600]{0,1:T(8,128)(2,1)} collective-permute-done((bf16[256,1600]{0,1:T(8,128)(2,1)}, bf16[256,1600]{0,1:T(8,128)(2,1)}, u32[]{:S(2)}, u32[]{:S(2)}) %collective-permute-start.34) | collective-permute-done | bytes 819232 | tf_op jit(solution)/shard_map/ppermute | solution.py:255
  92.9 12.1 %collective-permute-done.21 = bf16[256,1600]{0,1:T(8,128)(2,1)S(1)} collective-permute-done((bf16[256,1600]{0,1:T(8,128)(2,1)}, bf16[256,1600]{0,1:T(8,128)(2,1)S(1)}, u32[]{:S(2)}, u32[]{:S(2)}) %collective-permute-start.21) | collective-permute-done | bytes 819232 | tf_op jit(solution)/shard_map/ppermute | solution.py:255
  107.2 15.3 %collective-permute-done = bf16[256,1600]{0,1:T(8,128)(2,1)S(1)} collective-permute-done((bf16[256,1600]{0,1:T(8,128)(2,1)}, bf16[256,1600]{0,1:T(8,128)(2,1)S(1)}, u32[]{:S(2)}, u32[]{:S(2)}) %collective-permute-start) | collective-permute-done | bytes 819232 | tf_op jit(solution)/shard_map/ppermute | solution.py:255
  153.9 9.1 add_convert_fusion.1.qkv_ref
  163.1 13.7 %attend_forward.5 = (bf16[256,512]{1,0:T(8,128)(2,1)S(1)}, bf16[256,512]{1,0:T(8,128)(2,1)S(1)}, bf16[256,512]{1,0:T(8,128)(2,1)S(1)}, bf16[256,512]{1,0:T(8,128)(2,1)S(1)}, f32[4,2,1024]{2,1,0:T(2,128)S(1)}) custom-call(s32[8]{0:T(128)S(1)} %squeeze.66.place_ref, bf16[1024,1536]{1,0:T(8,128)(2,1)S(1)} %add_convert_fusion.1.qkv_ref), custom_call_target="tpu_custom_call" | custom-call | flops 9395240960 | bytes 6291456 | tf_op jit(solution)/shard_map/attend_forward/pallas_call | solution.py:142
  187.3 13.8 %attend_forward.4 = (bf16[256,512]{1,0:T(8,128)(2,1)S(1)}, bf16[256,512]{1,0:T(8,128)(2,1)S(1)}, bf16[256,512]{1,0:T(8,128)(2,1)S(1)}, bf16[256,512]{1,0:T(8,128)(2,1)S(1)}, f32[4,2,1024]{2,1,0:T(2,128)S(1)}) custom-call(s32[8]{0:T(128)S(1)} %squeeze.64.place_ref, bf16[1024,1536]{1,0:T(8,128)(2,1)S(1)} %add_convert_fusion.2.qkv_ref), custom_call_target="tpu_custom_call" | custom-call | flops 9395240960 | bytes 6291456 | tf_op jit(solution)/shard_map/attend_forward/pallas_call | solution.py:142
  202.5 7.6 add_convert_fusion.3.qkv_ref
  210.1 13.9 %attend_forward.3 = (bf16[256,512]{1,0:T(8,128)(2,1)S(1)}, bf16[256,512]{1,0:T(8,128)(2,1)S(1)}, bf16[256,512]{1,0:T(8,128)(2,1)S(1)}, bf16[256,512]{1,0:T(8,128)(2,1)S(1)}, f32[4,2,1024]{2,1,0:T(2,128)S(1)}) custom-call(s32[8]{0:T(128)S(1)} %squeeze.60.place_ref, bf16[1024,1536]{1,0:T(8,128)(2,1)S(1)} %add_convert_fusion.3.qkv_ref), custom_call_target="tpu_custom_call" | custom-call | flops 9395240960 | bytes 6291456 | tf_op jit(solution)/shard_map/attend_forward/pallas_call | solution.py:142
  272.0 12.2 %collective-permute-done.28 = bf16[256,1600]{0,1:T(8,128)(2,1)} collective-permute-done((bf16[256,1600]{0,1:T(8,128)(2,1)}, bf16[256,1600]{0,1:T(8,128)(2,1)}, u32[]{:S(2)}, u32[]{:S(2)}) %collective-permute-start.28) | collective-permute-done | bytes 819232 | tf_op jit(solution)/shard_map/ppermute | solution.py:255
  289.1 23.0 %collective-permute-done.41 = bf16[256,1600]{0,1:T(8,128)(2,1)S(1)} collective-permute-done((bf16[256,1600]{0,1:T(8,128)(2,1)}, bf16[256,1600]{0,1:T(8,128)(2,1)S(1)}, u32[]{:S(2)}, u32[]{:S(2)}) %collective-permute-start.41) | collective-permute-done | bytes 819232 | tf_op jit(solution)/shard_map/ppermute | solution.py:255
  312.6 9.9 fusion.90
  324.7 10.0 fusion.88
  334.7 25.9 %collective-permute-done.13 = bf16[256,1600]{0,1:T(8,128)(2,1)} collective-permute-done((bf16[256,1600]{0,1:T(8,128)(2,1)S(1)}, bf16[256,1600]{0,1:T(8,128)(2,1)}, u32[]{:S(2)}, u32[]{:S(2)}) %collective-permute-start.13) | collective-permute-done | bytes 819232 | tf_op jit(solution)/shard_map/ppermute | solution.py:255
  366.2 11.6 %fusion.92 = f32[1024,1600]{0,1:T(8,128)} fusion(bf16[1600,1600]{1,0:T(8,128)(2,1)} %copy-done.42, bf16[256,1600]{0,1:T(8,128)(2,1)} %collective-permute-done.15, bf16[256,1600]{0,1:T(8,128)(2,1)S(1)} %collective-permute-done.14, bf16[256,1600]{0,1:T(8,128)(2,1)} %collective-permute-done.13, bf16[256,1600]{0,1:T(8,128)(2,1)S(1)} %copy-done.63), kind=kOutput, calls=%fused_computation.244 | convolution fusion | flops 5255987200 | bytes 14950400 | tf_op jit(solution)/shard_map/dot_general | solution.py:22
  377.8 8.8 fusion.171
  390.5 15.3 %convert_reduce_fusion.1 = (f32[1600]{0:T(1024)}, bf16[1024,1600]{0,1:T(8,128)(2,1)}) fusion(f32[1024,1600]{0,1:T(8,128)} %fusion.90, f32[1600]{0:T(1024)S(1)} %dynamic-slice_convert_fusion, bf16[1600,1600]{1,0:T(8,128)(2,1)S(1)} %broadcast_select_fusion, bf16[256,1600]{0,1:T(8,128)(2,1)} %copy-done.167, bf16[256,1600]{0,1:T(8,128)(2,1)} %collective-permute-done.61, ...), kind=kOutput, calls=%fused_computation.49 | convolution fusion | flops 5290392064 | bytes 18240000 | tf_op jit(solution)/shard_map/dot_general | solution.py:22
  405.8 9.4 fusion.170
  418.0 15.0 %convert_reduce_fusion = (f32[1600]{0:T(1024)}, bf16[1024,1600]{0,1:T(8,128)(2,1)}) fusion(f32[1024,1600]{0,1:T(8,128)} %fusion.88, f32[1600]{0:T(1024)S(1)} %dynamic-slice_convert_fusion, bf16[1600,1600]{1,0:T(8,128)(2,1)S(1)} %broadcast_select_fusion, bf16[256,1600]{0,1:T(8,128)(2,1)} %collective-permute-done.75, bf16[256,1600]{0,1:T(8,128)(2,1)} %copy-done.168, ...), kind=kOutput, calls=%fused_computation.48 | convolution fusion | flops 5290392064 | bytes 18240000 | tf_op jit(solution)/shard_map/dot_general | solution.py:22
  433.0 9.4 fusion.169
  444.4 15.2 %convert_reduce_fusion.2 = (f32[1600]{0:T(1024)}, bf16[1024,1600]{0,1:T(8,128)(2,1)}) fusion(f32[1024,1600]{0,1:T(8,128)} %fusion.92, f32[1600]{0:T(1024)S(1)} %dynamic-slice_convert_fusion, bf16[1600,1600]{1,0:T(8,128)(2,1)S(1)} %broadcast_select_fusion, bf16[256,1600]{0,1:T(8,128)(2,1)} %collective-permute-done.49, ...), kind=kOutput, calls=%fused_computation.50 | convolution fusion | flops 5290392064 | bytes 18240000 | tf_op jit(solution)/shard_map/dot_general | solution.py:22
  459.6 8.0 fusion.167
  480.8 12.0 %collective-permute-done.65 = bf16[256,1600]{0,1:T(8,128)(2,1)S(1)} collective-permute-done((bf16[256,1600]{0,1:T(8,128)(2,1)S(1)}, bf16[256,1600]{0,1:T(8,128)(2,1)S(1)}, u32[]{:S(2)}, u32[]{:S(2)}) %collective-permute-start.65) | collective-permute-done | bytes 819232 | tf_op jit(solution)/shard_map/ppermute | solution.py:255
  494.1 16.2 %collective-permute-done.78 = bf16[256,1600]{0,1:T(8,128)(2,1)S(1)} collective-permute-done((bf16[256,1600]{0,1:T(8,128)(2,1)S(1)}, bf16[256,1600]{0,1:T(8,128)(2,1)S(1)}, u32[]{:S(2)}, u32[]{:S(2)}) %collective-permute-start.78) | collective-permute-done | bytes 819232 | tf_op jit(solution)/shard_map/ppermute | solution.py:255
  515.4 12.5 %collective-permute-done.33 = bf16[256,1600]{0,1:T(8,128)(2,1)S(1)} collective-permute-done((bf16[256,1600]{0,1:T(8,128)(2,1)S(1)}, bf16[256,1600]{0,1:T(8,128)(2,1)S(1)}, u32[]{:S(2)}, u32[]{:S(2)}) %collective-permute-start.33) | collective-permute-done | bytes 819232 | tf_op jit(solution)/shard_map/ppermute | solution.py:255
  566.9 20.8 %attend_backward.4 = bf16[1024,1536]{1,0:T(8,128)(2,1)S(1)} custom-call(s32[8]{0:T(128)S(1)} %squeeze.64.place_ref, bf16[1024,1536]{1,0:T(8,128)(2,1)S(1)} %copy-done.11, bf16[256,512]{1,0:T(8,128)(2,1)S(1)} %convolution_convert_fusion.8.refs_0_, bf16[256,512]{1,0:T(8,128)(2,1)S(1)} %collective-permute-done.66.refs_1_, ...), custom_call_target="tpu_custom_call" | custom-call | flops 15032385536 | bytes 9437184 | tf_op jit(solution)/shard_map/attend_backward/pallas_call | solution.py:167
  596.4 20.6 %attend_backward.3 = bf16[1024,1536]{1,0:T(8,128)(2,1)S(1)} custom-call(s32[8]{0:T(128)S(1)} %squeeze.60.place_ref, bf16[1024,1536]{1,0:T(8,128)(2,1)S(1)} %copy-done.9, bf16[256,512]{1,0:T(8,128)(2,1)S(1)} %convolution_convert_fusion.12.refs_0_, bf16[256,512]{1,0:T(8,128)(2,1)S(1)} %collective-permute-done.53.refs_1_, ...), custom_call_target="tpu_custom_call" | custom-call | flops 15032385536 | bytes 9437184 | tf_op jit(solution)/shard_map/attend_backward/pallas_call | solution.py:167
  617.0 11.6 %fusion.190 = f32[1600,1536]{1,0:T(8,128)} fusion(bf16[1024,1600]{0,1:T(8,128)(2,1)} %constant_dynamic-update-slice_fusion, bf16[1024,1536]{1,0:T(8,128)(2,1)S(1)} %attend_backward.3), kind=kOutput, calls=%fused_computation.438 | convolution fusion | flops 5033164800 | bytes 16252928 | tf_op jit(solution)/shard_map/dot_general | solution.py:22
  628.7 20.6 %attend_backward.5 = bf16[1024,1536]{1,0:T(8,128)(2,1)S(1)} custom-call(s32[8]{0:T(128)S(1)} %squeeze.66.place_ref, bf16[1024,1536]{1,0:T(8,128)(2,1)S(1)} %copy-done.7, bf16[256,512]{1,0:T(8,128)(2,1)S(1)} %convolution_convert_fusion.4.refs_0_, bf16[256,512]{1,0:T(8,128)(2,1)S(1)} %collective-permute-done.79.refs_1_, ...), custom_call_target="tpu_custom_call" | custom-call | flops 15032385536 | bytes 9437184 | tf_op jit(solution)/shard_map/attend_backward/pallas_call | solution.py:167
  650.9 10.8 %add_convert_fusion = bf16[1600,1536]{1,0:T(8,128)(2,1)} fusion(f32[1600,1536]{1,0:T(8,128)} %fusion.190, f32[1600,1536]{1,0:T(8,128)} %fusion.191, bf16[1024,1600]{0,1:T(8,128)(2,1)S(1)} %copy-done.73, bf16[1024,1536]{1,0:T(8,128)(2,1)S(1)} %attend_backward.5), kind=kOutput, calls=%fused_computation.12 | convolution fusion | flops 5040537600 | bytes 30998528 | tf_op jit(solution)/shard_map/dot_general | solution.py:22
  669.2 14.4 %fusion.85 = f32[1600,1600]{1,0:T(8,128)} fusion(bf16[256,1600]{0,1:T(8,128)(2,1)} %copy-done.167, bf16[256,1600]{0,1:T(8,128)(2,1)} %collective-permute-done.61, bf16[256,1600]{0,1:T(8,128)(2,1)} %collective-permute-done.60, bf16[256,1600]{0,1:T(8,128)(2,1)} %get-tuple-element.137, f32[1024,1600]{0,1:T(8,128)} %fusion.90, ...), kind=kOutput, calls=%fused_computation.237 | convolution fusion | flops 5272371200 | bytes 20076800 | tf_op jit(solution)/shard_map/dot_general | solution.py:22
  683.6 14.8 %fusion.86 = f32[1600,1600]{1,0:T(8,128)} fusion(bf16[256,1600]{0,1:T(8,128)(2,1)} %collective-permute-done.49, bf16[256,1600]{0,1:T(8,128)(2,1)} %collective-permute-done.48, bf16[256,1600]{0,1:T(8,128)(2,1)} %collective-permute-done.47, bf16[256,1600]{0,1:T(8,128)(2,1)S(1)} %copy-done.59, f32[1024,1600]{0,1:T(8,128)} %fusion.92, ...), kind=kOutput, calls=%fused_computation.238 | convolution fusion | flops 5272371200 | bytes 20076800 | tf_op jit(solution)/shard_map/dot_general | solution.py:22
  698.4 17.1 %fusion.177 = (bf16[1600,1600]{1,0:T(8,128)(2,1)}, f32[1600,1600]{1,0:T(8,128)}) fusion(f32[1024,1600]{0,1:T(8,128)} %fusion.88, f32[1600]{0:T(1024)S(1)} %dynamic-slice_convert_fusion, bf16[256,1600]{0,1:T(8,128)(2,1)} %collective-permute-done.75, bf16[256,1600]{0,1:T(8,128)(2,1)S(1)} %copy-done.169, bf16[256,1600]{0,1:T(8,128)(2,1)} %collective-permute-done.73, ...), kind=kOutput, calls=%fused_computation.425 | convolution fusion | flops 5280051200 | bytes 45676800 | tf_op jit(solution)/shard_map/dot_general | solution.py:22
  717.1 12.7 %fusion.175 = (bf16[1024,1600]{0,1:T(8,128)(2,1)}, f32[1024,1600]{0,1:T(8,128)}) fusion(bf16[1600,1600]{1,0:T(8,128)(2,1)} %copy-done.41, f32[1024,1600]{0,1:T(8,128)} %fusion.92, f32[1600]{0:T(1024)S(1)} %dynamic-slice_convert_fusion), kind=kOutput, calls=%fused_computation.423 | convolution fusion | flops 5260902400 | bytes 21510400 | tf_op jit(solution)/shard_map/dot_general | solution.py:22
  737.2 9.6 copy.59
  771.1 12.2 %fusion.174 = (bf16[1024,1600]{0,1:T(8,128)(2,1)S(1)}, f32[1024,1600]{0,1:T(8,128)}) fusion(bf16[1600,1600]{1,0:T(8,128)(2,1)} %copy-done.41, f32[1024,1600]{0,1:T(8,128)} %fusion.88, f32[1600]{0:T(1024)S(1)} %dynamic-slice_convert_fusion), kind=kOutput, calls=%fused_computation.422 | convolution fusion | flops 5260902400 | bytes 21510400 | tf_op jit(solution)/shard_map/dot_general | solution.py:22
  786.1 11.6 %fusion.89 = f32[1600,1600]{1,0:T(8,128)} fusion(bf16[1024,1600]{0,1:T(8,128)(2,1)} %get-tuple-element.200, bf16[256,1600]{0,1:T(8,128)(2,1)} %copy-done.164, bf16[256,1600]{0,1:T(8,128)(2,1)} %copy-done.162, bf16[256,1600]{0,1:T(8,128)(2,1)} %collective-permute-done.28, bf16[256,1600]{0,1:T(8,128)(2,1)} %get-tuple-element.154), kind=kOutput, calls=%fused_computation.241 | convolution fusion | flops 5255987200 | bytes 16793600 | tf_op jit(solution)/shard_map/dot_general | solution.py:22
  800.0 9.8 fusion.91
  810.0 15.4 %fusion.176 = (bf16[1600,1600]{1,0:T(8,128)(2,1)}, f32[1600,1600]{1,0:T(8,128)}) fusion(bf16[1024,1600]{0,1:T(8,128)(2,1)} %get-tuple-element.196, bf16[256,1600]{0,1:T(8,128)(2,1)} %copy-done.163, bf16[256,1600]{0,1:T(8,128)(2,1)} %copy-done.161, bf16[256,1600]{0,1:T(8,128)(2,1)} %copy-done.160, bf16[256,1600]{0,1:T(8,128)(2,1)S(1)} %copy-done.62, ...), kind=kOutput, calls=%fused_computation.424 | convolution fusion | flops 5263667200 | bytes 42393600 | tf_op jit(solution)/shard_map/dot_general | solution.py:22
  837.1 9.1 select_convert_fusion
  883.8 17.3 %collective-permute-done.82 = bf16[128,1600]{0,1:T(8,128)(2,1)S(1)} collective-permute-done((bf16[128,1600]{0,1:T(8,128)(2,1)}, bf16[128,1600]{0,1:T(8,128)(2,1)S(1)}, u32[]{:S(2)}, u32[]{:S(2)}) %collective-permute-start.82) | collective-permute-done | bytes 409632 | tf_op jit(solution)/shard_map/ppermute | solution.py:255
  919.4 9.2 select_convert_fusion.1
  935.6 13.2 %collective-permute-done.70 = bf16[256,1600]{0,1:T(8,128)(2,1)} collective-permute-done((bf16[256,1600]{0,1:T(8,128)(2,1)S(1)}, bf16[256,1600]{0,1:T(8,128)(2,1)}, u32[]{:S(2)}, u32[]{:S(2)}) %collective-permute-start.70) | collective-permute-done | bytes 819232 | tf_op jit(solution)/shard_map/ppermute | solution.py:255
  954.4 12.0 %collective-permute-done.57 = bf16[256,1600]{0,1:T(8,128)(2,1)} collective-permute-done((bf16[256,1600]{0,1:T(8,128)(2,1)}, bf16[256,1600]{0,1:T(8,128)(2,1)}, u32[]{:S(2)}, u32[]{:S(2)}) %collective-permute-start.57) | collective-permute-done | bytes 819232 | tf_op jit(solution)/shard_map/ppermute | solution.py:255
  967.5 8.8 multiply_reduce_fusion.3
  988.9 11.4 %collective-permute-done.46 = bf16[256,1600]{0,1:T(8,128)(2,1)} collective-permute-done((bf16[256,1600]{0,1:T(8,128)(2,1)}, bf16[256,1600]{0,1:T(8,128)(2,1)}, u32[]{:S(2)}, u32[]{:S(2)}) %collective-permute-start.46) | collective-permute-done | bytes 819232 | tf_op jit(solution)/shard_map/ppermute | solution.py:255
  1033.1 17.1 %collective-permute-done.94 = bf16[200,400]{1,0:T(8,128)(2,1)S(1)} collective-permute-done((bf16[200,400]{1,0:T(8,128)(2,1)}, bf16[200,400]{1,0:T(8,128)(2,1)S(1)}, u32[]{:S(2)}, u32[]{:S(2)}) %collective-permute-start.94) | collective-permute-done | bytes 160032 | tf_op jit(solution)/shard_map/ppermute | solution.py:255
  1058.0 9.7 fusion
  (797 shorter events, 425.5 us)
Async XLA Ops:
  7.2 140.3 %all-gather.9.cloned.1.call-start = ((), (), s32[]{:S(2)}) async-start(), calls=%async_computation.6 | async-start | bytes 5990400 | tf_op jit(solution)/shard_map/all_gather | solution.py:362
  7.9 146.0 %all-gather.5.cloned.1.call-start = ((), (), s32[]{:S(2)}) async-start(), calls=%async_computation.4 | async-start | bytes 5529600 | tf_op jit(solution)/shard_map/all_gather | solution.py:318
  45.7 179.0 %all-gather.7.cloned.1.call-start = ((), (), s32[]{:S(2)}) async-start(), calls=%async_computation.5 | async-start | bytes 5990400 | tf_op jit(solution)/shard_map/all_gather | solution.py:343
  60.1 203.8 %all-gather.11.cloned.1.call-start = ((), (), s32[]{:S(2)}) async-start(), calls=%async_computation.7 | async-start | bytes 5990400 | tf_op jit(solution)/shard_map/all_gather | solution.py:362
  68.1 36.9 %collective-permute-start.21 = (bf16[256,1600]{0,1:T(8,128)(2,1)}, bf16[256,1600]{0,1:T(8,128)(2,1)S(1)}, u32[]{:S(2)}, u32[]{:S(2)}) collective-permute-start(bf16[256,1600]{0,1:T(8,128)(2,1)} %get-tuple-element.107), channel_id=1, source_target_pairs={{0,1},{1,0},{2,3},{3,2},{4,5},{5,4},{6,7},{7,6},{8,9},{9,8},{10,11... | collective-permute-start | bytes 2457608 | tf_op jit(solution)/shard_map/ppermute | solution.py:255
  68.7 36.9 %collective-permute-start.22 = (bf16[256,1600]{0,1:T(8,128)(2,1)}, bf16[256,1600]{0,1:T(8,128)(2,1)S(1)}, u32[]{:S(2)}, u32[]{:S(2)}) collective-permute-start(bf16[256,1600]{0,1:T(8,128)(2,1)} %get-tuple-element.107), channel_id=1, source_target_pairs={{0,2},{1,3},{2,0},{3,1},{4,6},{5,7},{6,4},{7,5},{8,10},{9,11},{10,... | collective-permute-start | bytes 2457608 | tf_op jit(solution)/shard_map/ppermute | solution.py:255
  70.1 52.5 %collective-permute-start = (bf16[256,1600]{0,1:T(8,128)(2,1)}, bf16[256,1600]{0,1:T(8,128)(2,1)S(1)}, u32[]{:S(2)}, u32[]{:S(2)}) collective-permute-start(bf16[256,1600]{0,1:T(8,128)(2,1)} %get-tuple-element.91), channel_id=1, source_target_pairs={{0,1},{1,0},{2,3},{3,2},{4,5},{5,4},{6,7},{7,6},{8,9},{9,8},{10,11... | collective-permute-start | bytes 2457608 | tf_op jit(solution)/shard_map/ppermute | solution.py:255
  70.7 946.2 %reduce-scatter.11.cloned.1.call-start = ((), (), s32[]{:S(2)}) async-start(), calls=%async_computation.8 | async-start | bytes 5529600 | tf_op jit(solution)/shard_map/reduce_scatter | solution.py:438
  87.5 38.7 %collective-permute-start.1 = (bf16[256,1600]{0,1:T(8,128)(2,1)}, bf16[256,1600]{0,1:T(8,128)(2,1)S(1)}, u32[]{:S(2)}, u32[]{:S(2)}) collective-permute-start(bf16[256,1600]{0,1:T(8,128)(2,1)} %get-tuple-element.91), channel_id=1, source_target_pairs={{0,2},{1,3},{2,0},{3,1},{4,6},{5,7},{6,4},{7,5},{8,10},{9,11},{10,... | collective-permute-start | bytes 2457608 | tf_op jit(solution)/shard_map/ppermute | solution.py:255
  91.4 40.5 %collective-permute-start.36 = (bf16[128,1600]{0,1:T(8,128)(2,1)S(1)}, bf16[128,1600]{0,1:T(8,128)(2,1)S(1)}, u32[]{:S(2)}, u32[]{:S(2)}) collective-permute-start(bf16[128,1600]{0,1:T(8,128)(2,1)S(1)} %slice.437), channel_id=1, source_target_pairs={{0,2},{1,3},{2,0},{3,1},{4,6},{5,7},{6,4},{7,5},{8,10},{9,11},{10,... | collective-permute-start | bytes 1228808 | tf_op jit(solution)/shard_map/ppermute | solution.py:255
  147.5 137.9 %collective-permute-start.16 = (bf16[1600,1600]{1,0:T(8,128)(2,1)}, bf16[1600,1600]{1,0:T(8,128)(2,1)}, u32[]{:S(2)}, u32[]{:S(2)}) collective-permute-start(bf16[1600,1600]{1,0:T(8,128)(2,1)} %all-gather.9.cloned.1.call-done), channel_id=1, source_target_pairs={{0,2},{1,3},{6,4},{7,5},{8,10},{9,11},{14,12},{15,13},{16,18},{17,... | collective-permute-start | bytes 15360008 | tf_op jit(solution)/shard_map/ppermute | solution.py:363
  177.5 53.8 %collective-permute-start.38 = (bf16[256,512]{1,0:T(8,128)(2,1)S(1)}, bf16[256,512]{1,0:T(8,128)(2,1)}, u32[]{:S(2)}, u32[]{:S(2)}) collective-permute-start(bf16[256,512]{1,0:T(8,128)(2,1)S(1)} %get-tuple-element.39), channel_id=1, source_target_pairs={{0,1},{1,0},{2,3},{3,2},{4,5},{5,4},{6,7},{7,6},{8,9},{9,8},{10,11... | collective-permute-start | bytes 786440 | tf_op jit(solution)/shard_map/ppermute | solution.py:255
  178.1 55.1 %collective-permute-start.39 = (bf16[256,512]{1,0:T(8,128)(2,1)S(1)}, bf16[256,512]{1,0:T(8,128)(2,1)S(1)}, u32[]{:S(2)}, u32[]{:S(2)}) collective-permute-start(bf16[256,512]{1,0:T(8,128)(2,1)S(1)} %get-tuple-element.40), channel_id=1, source_target_pairs={{0,2},{1,3},{2,0},{3,1},{4,6},{5,7},{6,4},{7,5},{8,10},{9,11},{10,... | collective-permute-start | bytes 786440 | tf_op jit(solution)/shard_map/ppermute | solution.py:255
  178.1 57.3 %collective-permute-start.40 = (bf16[256,512]{1,0:T(8,128)(2,1)S(1)}, bf16[256,512]{1,0:T(8,128)(2,1)S(1)}, u32[]{:S(2)}, u32[]{:S(2)}) collective-permute-start(bf16[256,512]{1,0:T(8,128)(2,1)S(1)} %get-tuple-element.41), channel_id=1, source_target_pairs={{0,3},{1,2},{2,1},{3,0},{4,7},{5,6},{6,5},{7,4},{8,11},{9,10},{10,... | collective-permute-start | bytes 786440 | tf_op jit(solution)/shard_map/ppermute | solution.py:255
  201.9 37.2 %collective-permute-start.25 = (bf16[256,512]{1,0:T(8,128)(2,1)S(1)}, bf16[256,512]{1,0:T(8,128)(2,1)S(1)}, u32[]{:S(2)}, u32[]{:S(2)}) collective-permute-start(bf16[256,512]{1,0:T(8,128)(2,1)S(1)} %get-tuple-element.35), channel_id=1, source_target_pairs={{0,1},{1,0},{2,3},{3,2},{4,5},{5,4},{6,7},{7,6},{8,9},{9,8},{10,11... | collective-permute-start | bytes 786440 | tf_op jit(solution)/shard_map/ppermute | solution.py:255
  263.9 96.7 %collective-permute-start.17 = (bf16[1600,1600]{1,0:T(8,128)(2,1)}, bf16[1600,1600]{1,0:T(8,128)(2,1)}, u32[]{:S(2)}, u32[]{:S(2)}) collective-permute-start(bf16[1600,1600]{1,0:T(8,128)(2,1)} %all-gather.11.cloned.1.call-done), channel_id=1, source_target_pairs={{0,2},{1,3},{6,4},{7,5},{8,10},{9,11},{14,12},{15,13},{16,18},{17,... | collective-permute-start | bytes 15360008 | tf_op jit(solution)/shard_map/ppermute | solution.py:363
  269.1 92.6 %collective-permute-start.60 = (bf16[256,1600]{0,1:T(8,128)(2,1)}, bf16[256,1600]{0,1:T(8,128)(2,1)}, u32[]{:S(2)}, u32[]{:S(2)}) collective-permute-start(bf16[256,1600]{0,1:T(8,128)(2,1)} %get-tuple-element.137), channel_id=1, source_target_pairs={{0,1},{1,0},{2,3},{3,2},{4,5},{5,4},{6,7},{7,6},{8,9},{9,8},{10,11... | collective-permute-start | bytes 2457608 | tf_op jit(solution)/shard_map/ppermute | solution.py:255
  288.6 99.1 %collective-permute-start.61 = (bf16[256,1600]{0,1:T(8,128)(2,1)}, bf16[256,1600]{0,1:T(8,128)(2,1)}, u32[]{:S(2)}, u32[]{:S(2)}) collective-permute-start(bf16[256,1600]{0,1:T(8,128)(2,1)} %get-tuple-element.137), channel_id=1, source_target_pairs={{0,4},{1,5},{2,6},{3,7},{4,0},{5,1},{6,2},{7,3},{8,12},{9,13},{10,... | collective-permute-start | bytes 2457608 | tf_op jit(solution)/shard_map/ppermute | solution.py:255
  322.5 66.5 %collective-permute-start.47 = (bf16[256,1600]{0,1:T(8,128)(2,1)S(1)}, bf16[256,1600]{0,1:T(8,128)(2,1)}, u32[]{:S(2)}, u32[]{:S(2)}) collective-permute-start(bf16[256,1600]{0,1:T(8,128)(2,1)S(1)} %copy-done.58), channel_id=1, source_target_pairs={{0,1},{1,0},{2,3},{3,2},{4,5},{5,4},{6,7},{7,6},{8,9},{9,8},{10,11... | collective-permute-start | bytes 2457608 | tf_op jit(solution)/shard_map/ppermute | solution.py:255
  324.3 36.3 %collective-permute-start.13 = (bf16[256,1600]{0,1:T(8,128)(2,1)S(1)}, bf16[256,1600]{0,1:T(8,128)(2,1)}, u32[]{:S(2)}, u32[]{:S(2)}) collective-permute-start(bf16[256,1600]{0,1:T(8,128)(2,1)S(1)} %copy-done.63), channel_id=1, source_target_pairs={{0,1},{1,0},{2,3},{3,2},{4,5},{5,4},{6,7},{7,6},{8,9},{9,8},{10,11... | collective-permute-start | bytes 2457608 | tf_op jit(solution)/shard_map/ppermute | solution.py:255
  361.8 82.1 %collective-permute-start.48 = (bf16[256,1600]{0,1:T(8,128)(2,1)S(1)}, bf16[256,1600]{0,1:T(8,128)(2,1)}, u32[]{:S(2)}, u32[]{:S(2)}) collective-permute-start(bf16[256,1600]{0,1:T(8,128)(2,1)S(1)} %copy-done.58), channel_id=1, source_target_pairs={{0,4},{1,5},{2,6},{3,7},{4,0},{5,1},{6,2},{7,3},{8,12},{9,13},{10,... | collective-permute-start | bytes 2457608 | tf_op jit(solution)/shard_map/ppermute | solution.py:255
  389.0 54.8 %collective-permute-start.49 = (bf16[256,1600]{0,1:T(8,128)(2,1)}, bf16[256,1600]{0,1:T(8,128)(2,1)}, u32[]{:S(2)}, u32[]{:S(2)}) collective-permute-start(bf16[256,1600]{0,1:T(8,128)(2,1)} %collective-permute-done.47), channel_id=1, source_target_pairs={{0,4},{1,5},{2,6},{3,7},{4,0},{5,1},{6,2},{7,3},{8,12},{9,13},{10,... | collective-permute-start | bytes 2457608 | tf_op jit(solution)/shard_map/ppermute | solution.py:255
  390.5 84.4 %collective-permute-start.32 = (bf16[256,1600]{0,1:T(8,128)(2,1)S(1)}, bf16[256,1600]{0,1:T(8,128)(2,1)}, u32[]{:S(2)}, u32[]{:S(2)}) collective-permute-start(bf16[256,1600]{0,1:T(8,128)(2,1)S(1)} %get-tuple-element.131), channel_id=1, source_target_pairs={{0,4},{1,5},{2,6},{3,7},{4,0},{5,1},{6,2},{7,3},{8,12},{9,13},{10,... | collective-permute-start | bytes 2457608 | tf_op jit(solution)/shard_map/ppermute | solution.py:255
  416.6 51.2 %collective-permute-start.64 = (bf16[256,1600]{0,1:T(8,128)(2,1)}, bf16[256,1600]{0,1:T(8,128)(2,1)}, u32[]{:S(2)}, u32[]{:S(2)}) collective-permute-start(bf16[256,1600]{0,1:T(8,128)(2,1)} %get-tuple-element.121), channel_id=1, source_target_pairs={{0,4},{1,5},{2,6},{3,7},{4,0},{5,1},{6,2},{7,3},{8,12},{9,13},{10,... | collective-permute-start | bytes 2457608 | tf_op jit(solution)/shard_map/ppermute | solution.py:255
  417.5 60.6 %collective-permute-start.63 = (bf16[256,1600]{0,1:T(8,128)(2,1)}, bf16[256,1600]{0,1:T(8,128)(2,1)S(1)}, u32[]{:S(2)}, u32[]{:S(2)}) collective-permute-start(bf16[256,1600]{0,1:T(8,128)(2,1)} %get-tuple-element.120), channel_id=1, source_target_pairs={{0,4},{1,5},{2,6},{3,7},{4,0},{5,1},{6,2},{7,3},{8,12},{9,13},{10,... | collective-permute-start | bytes 2457608 | tf_op jit(solution)/shard_map/ppermute | solution.py:255
  477.7 37.7 %collective-permute-start.31 = (bf16[256,1600]{0,1:T(8,128)(2,1)}, bf16[256,1600]{0,1:T(8,128)(2,1)S(1)}, u32[]{:S(2)}, u32[]{:S(2)}) collective-permute-start(bf16[256,1600]{0,1:T(8,128)(2,1)} %get-tuple-element.130), channel_id=1, source_target_pairs={{0,4},{1,5},{2,6},{3,7},{4,0},{5,1},{6,2},{7,3},{8,12},{9,13},{10,... | collective-permute-start | bytes 2457608 | tf_op jit(solution)/shard_map/ppermute | solution.py:255
  479.0 59.2 %collective-permute-start.50 = (bf16[256,1600]{0,1:T(8,128)(2,1)S(1)}, bf16[256,1600]{0,1:T(8,128)(2,1)S(1)}, u32[]{:S(2)}, u32[]{:S(2)}) collective-permute-start(bf16[256,1600]{0,1:T(8,128)(2,1)S(1)} %get-tuple-element.126), channel_id=1, source_target_pairs={{0,4},{1,5},{2,6},{3,7},{4,0},{5,1},{6,2},{7,3},{8,12},{9,13},{10,... | collective-permute-start | bytes 2457608 | tf_op jit(solution)/shard_map/ppermute | solution.py:255
  479.5 48.4 %collective-permute-start.33 = (bf16[256,1600]{0,1:T(8,128)(2,1)S(1)}, bf16[256,1600]{0,1:T(8,128)(2,1)S(1)}, u32[]{:S(2)}, u32[]{:S(2)}) collective-permute-start(bf16[256,1600]{0,1:T(8,128)(2,1)S(1)} %fusion.59), channel_id=1, source_target_pairs={{0,1},{1,0},{2,3},{3,2},{4,5},{5,4},{6,7},{7,6},{8,9},{9,8},{10,11... | collective-permute-start | bytes 2457608 | tf_op jit(solution)/shard_map/ppermute | solution.py:255
  492.8 52.0 %collective-permute-start.52 = (bf16[256,1600]{0,1:T(8,128)(2,1)S(1)}, bf16[256,1600]{0,1:T(8,128)(2,1)S(1)}, u32[]{:S(2)}, u32[]{:S(2)}) collective-permute-start(bf16[256,1600]{0,1:T(8,128)(2,1)S(1)} %fusion.52), channel_id=1, source_target_pairs={{0,1},{1,0},{2,3},{3,2},{4,5},{5,4},{6,7},{7,6},{8,9},{9,8},{10,11... | collective-permute-start | bytes 2457608 | tf_op jit(solution)/shard_map/ppermute | solution.py:255
  554.3 74.3 %collective-permute-start.79 = (bf16[256,512]{1,0:T(8,128)(2,1)S(1)}, bf16[256,512]{1,0:T(8,128)(2,1)S(1)}, u32[]{:S(2)}, u32[]{:S(2)}) collective-permute-start(bf16[256,512]{1,0:T(8,128)(2,1)S(1)} %convolution_convert_fusion.3), channel_id=1, source_target_pairs={{0,1},{1,0},{2,3},{3,2},{4,5},{5,4},{6,7},{7,6},{8,9},{9,8},{10,11... | collective-permute-start | bytes 786440 | tf_op jit(solution)/shard_map/ppermute | solution.py:255
  555.7 72.9 %collective-permute-start.80 = (bf16[256,512]{1,0:T(8,128)(2,1)S(1)}, bf16[256,512]{1,0:T(8,128)(2,1)S(1)}, u32[]{:S(2)}, u32[]{:S(2)}) collective-permute-start(bf16[256,512]{1,0:T(8,128)(2,1)S(1)} %convolution_convert_fusion.2), channel_id=1, source_target_pairs={{0,2},{1,3},{2,0},{3,1},{4,6},{5,7},{6,4},{7,5},{8,10},{9,11},{10,... | collective-permute-start | bytes 786440 | tf_op jit(solution)/shard_map/ppermute | solution.py:255
  661.8 358.6 %reduce-scatter.13.cloned.1.call-start = ((), (), s32[]{:S(2)}) async-start(), calls=%async_computation.9 | async-start | bytes 5990400
  715.5 121.5 %collective-permute-start.103 = (bf16[1600,1600]{1,0:T(8,128)(2,1)}, bf16[1600,1600]{1,0:T(8,128)(2,1)}, u32[]{:S(2)}, u32[]{:S(2)}) collective-permute-start(bf16[1600,1600]{1,0:T(8,128)(2,1)} %get-tuple-element.203), channel_id=1, source_target_pairs={{2,0},{3,1},{4,6},{5,7},{10,8},{11,9},{12,14},{13,15},{18,16},{19,... | collective-permute-start | bytes 15360008 | tf_op jit(solution)/shard_map/ppermute | solution.py:408
  765.3 302.5 %reduce-scatter.17.cloned.1.call-start = ((), (), s32[]{:S(2)}) async-start(), calls=%async_computation.11 | async-start | bytes 5990400
  768.0 61.2 %collective-permute-start.19 = (bf16[256,1600]{0,1:T(8,128)(2,1)}, bf16[256,1600]{0,1:T(8,128)(2,1)}, u32[]{:S(2)}, u32[]{:S(2)}) collective-permute-start(bf16[256,1600]{0,1:T(8,128)(2,1)} %get-tuple-element.129), channel_id=1, source_target_pairs={{0,4},{1,5},{2,6},{3,7},{4,0},{5,1},{6,2},{7,3},{8,12},{9,13},{10,... | collective-permute-start | bytes 2457608 | tf_op jit(solution)/shard_map/ppermute | solution.py:255
  784.3 49.7 %collective-permute-start.45 = (bf16[256,1600]{0,1:T(8,128)(2,1)S(1)}, bf16[256,1600]{0,1:T(8,128)(2,1)}, u32[]{:S(2)}, u32[]{:S(2)}) collective-permute-start(bf16[256,1600]{0,1:T(8,128)(2,1)S(1)} %get-tuple-element.133), channel_id=1, source_target_pairs={{0,4},{1,5},{2,6},{3,7},{4,0},{5,1},{6,2},{7,3},{8,12},{9,13},{10,... | collective-permute-start | bytes 2457608 | tf_op jit(solution)/shard_map/ppermute | solution.py:255
  825.3 94.1 %collective-permute-start.102 = (bf16[1600,1600]{1,0:T(8,128)(2,1)}, bf16[1600,1600]{1,0:T(8,128)(2,1)}, u32[]{:S(2)}, u32[]{:S(2)}) collective-permute-start(bf16[1600,1600]{1,0:T(8,128)(2,1)} %get-tuple-element.201), channel_id=1, source_target_pairs={{2,0},{3,1},{4,6},{5,7},{10,8},{11,9},{12,14},{13,15},{18,16},{19,... | collective-permute-start | bytes 15360008 | tf_op jit(solution)/shard_map/ppermute | solution.py:408
  846.2 223.8 %reduce-scatter.15.cloned.1.call-start = ((), (), s32[]{:S(2)}) async-start(), calls=%async_computation.10 | async-start | bytes 5990400
  856.3 44.8 %collective-permute-start.82 = (bf16[128,1600]{0,1:T(8,128)(2,1)}, bf16[128,1600]{0,1:T(8,128)(2,1)S(1)}, u32[]{:S(2)}, u32[]{:S(2)}) collective-permute-start(bf16[128,1600]{0,1:T(8,128)(2,1)} %get-tuple-element.110), channel_id=1, source_target_pairs={{0,2},{1,3},{2,0},{3,1},{4,6},{5,7},{6,4},{7,5},{8,10},{9,11},{10,... | collective-permute-start | bytes 1228808 | tf_op jit(solution)/shard_map/ppermute | solution.py:255
  861.3 39.9 %collective-permute-start.84 = (bf16[128,1600]{0,1:T(8,128)(2,1)S(1)}, bf16[128,1600]{0,1:T(8,128)(2,1)S(1)}, u32[]{:S(2)}, u32[]{:S(2)}) collective-permute-start(bf16[128,1600]{0,1:T(8,128)(2,1)S(1)} %get-tuple-element.111), channel_id=1, source_target_pairs={{0,1},{1,0},{2,3},{3,2},{4,5},{5,4},{6,7},{7,6},{8,9},{9,8},{10,11... | collective-permute-start | bytes 1228808 | tf_op jit(solution)/shard_map/ppermute | solution.py:255
  869.8 39.4 %collective-permute-start.69 = (bf16[128,1600]{0,1:T(8,128)(2,1)S(1)}, bf16[128,1600]{0,1:T(8,128)(2,1)S(1)}, u32[]{:S(2)}, u32[]{:S(2)}) collective-permute-start(bf16[128,1600]{0,1:T(8,128)(2,1)S(1)} %get-tuple-element.116), channel_id=1, source_target_pairs={{0,2},{1,3},{2,0},{3,1},{4,6},{5,7},{6,4},{7,5},{8,10},{9,11},{10,... | collective-permute-start | bytes 1228808 | tf_op jit(solution)/shard_map/ppermute | solution.py:255
  872.0 38.4 %collective-permute-start.71 = (bf16[128,1600]{0,1:T(8,128)(2,1)S(1)}, bf16[128,1600]{0,1:T(8,128)(2,1)S(1)}, u32[]{:S(2)}, u32[]{:S(2)}) collective-permute-start(bf16[128,1600]{0,1:T(8,128)(2,1)S(1)} %get-tuple-element.117), channel_id=1, source_target_pairs={{0,1},{1,0},{2,3},{3,2},{4,5},{5,4},{6,7},{7,6},{8,9},{9,8},{10,11... | collective-permute-start | bytes 1228808 | tf_op jit(solution)/shard_map/ppermute | solution.py:255
  929.6 36.7 %collective-permute-start.57 = (bf16[256,1600]{0,1:T(8,128)(2,1)}, bf16[256,1600]{0,1:T(8,128)(2,1)}, u32[]{:S(2)}, u32[]{:S(2)}) collective-permute-start(bf16[256,1600]{0,1:T(8,128)(2,1)} %pad_maximum_fusion.12), channel_id=1, source_target_pairs={{0,1},{1,0},{2,3},{3,2},{4,5},{5,4},{6,7},{7,6},{8,9},{9,8},{10,11... | collective-permute-start | bytes 2457608 | tf_op jit(solution)/shard_map/ppermute | solution.py:255
  935.6 41.7 %collective-permute-start.18 = (bf16[256,1600]{0,1:T(8,128)(2,1)}, bf16[256,1600]{0,1:T(8,128)(2,1)}, u32[]{:S(2)}, u32[]{:S(2)}) collective-permute-start(bf16[256,1600]{0,1:T(8,128)(2,1)} %get-tuple-element.128), channel_id=1, source_target_pairs={{0,4},{1,5},{2,6},{3,7},{4,0},{5,1},{6,2},{7,3},{8,12},{9,13},{10,... | collective-permute-start | bytes 2457608 | tf_op jit(solution)/shard_map/ppermute | solution.py:255
  948.9 40.0 %collective-permute-start.44 = (bf16[256,1600]{0,1:T(8,128)(2,1)}, bf16[256,1600]{0,1:T(8,128)(2,1)}, u32[]{:S(2)}, u32[]{:S(2)}) collective-permute-start(bf16[256,1600]{0,1:T(8,128)(2,1)} %get-tuple-element.132), channel_id=1, source_target_pairs={{0,4},{1,5},{2,6},{3,7},{4,0},{5,1},{6,2},{7,3},{8,12},{9,13},{10,... | collective-permute-start | bytes 2457608 | tf_op jit(solution)/shard_map/ppermute | solution.py:255
  1016.9 41.1 %collective-permute-start.91 = (bf16[200,1536]{1,0:T(8,128)(2,1)}, bf16[200,1536]{1,0:T(8,128)(2,1)}, u32[]{:S(2)}, u32[]{:S(2)}) collective-permute-start(bf16[200,1536]{1,0:T(8,128)(2,1)} %reduce-scatter.11.cloned.1.call-done), channel_id=1, source_target_pairs={{0,1},{1,0},{2,3},{3,2},{4,5},{5,4},{6,7},{7,6},{8,9},{9,8},{10,11... | collective-permute-start | bytes 1843208 | tf_op jit(solution)/shard_map/ppermute | solution.py:255
  1017.9 40.1 %collective-permute-start.92 = (bf16[200,1536]{1,0:T(8,128)(2,1)}, bf16[200,1536]{1,0:T(8,128)(2,1)}, u32[]{:S(2)}, u32[]{:S(2)}) collective-permute-start(bf16[200,1536]{1,0:T(8,128)(2,1)} %reduce-scatter.11.cloned.1.call-done), channel_id=1, source_target_pairs={{0,2},{1,3},{2,0},{3,1},{4,6},{5,7},{6,4},{7,5},{8,10},{9,11},{10,... | collective-permute-start | bytes 1843208 | tf_op jit(solution)/shard_map/ppermute | solution.py:255
  1018.2 39.8 %collective-permute-start.93 = (bf16[200,1536]{1,0:T(8,128)(2,1)}, bf16[200,1536]{1,0:T(8,128)(2,1)}, u32[]{:S(2)}, u32[]{:S(2)}) collective-permute-start(bf16[200,1536]{1,0:T(8,128)(2,1)} %reduce-scatter.11.cloned.1.call-done), channel_id=1, source_target_pairs={{0,3},{1,2},{2,1},{3,0},{4,7},{5,6},{6,5},{7,4},{8,11},{9,10},{10,... | collective-permute-start | bytes 1843208 | tf_op jit(solution)/shard_map/ppermute | solution.py:255
  (245 other events, 4178.5 us)
Sparse Core Ops, SparseCore 0:
  9.7 59.4 all-gather.8
  70.8 52.0 all-gather.4
  125.1 55.5 all-gather.6
  182.2 55.4 all-gather.10
  661.9 57.6 reduce-scatter.10
  765.4 65.6 reduce-scatter.12
  846.3 65.0 reduce-scatter.16
  928.8 62.6 reduce-scatter.14

commit v2 on v1

v2 whole, which is shorter than its diff:
```python
import functools
import jax
import jax.numpy as jnp
from jax import lax
from jax.experimental import pallas as pl
from jax.experimental.pallas import tpu as pltpu
from jax.sharding import PartitionSpec as P

HEADS = 25
HEAD = 64
LANES = 128
TILE = 256
epsilon = 1e-05
F32 = jnp.float32
BF16 = jnp.bfloat16
NN = (((1,), (0,)), ((), ()))
NT = (((1,), (1,)), ((), ()))
TN = (((0,), (0,)), ((), ()))
MIB = 2**20
VMEM = pl.BlockSpec(memory_space=pltpu.VMEM)
SMEM = pl.BlockSpec(memory_space=pltpu.SMEM)
FAR = pl.BlockSpec(memory_space=pl.ANY)


def dot(left, right, dims=NN):
    return lax.dot_general(left, right, dims, preferred_element_type=F32)


def peer_id(count, mask):
    if mask < count:
        return {"tp": lax.axis_index("tp") ^ mask}
    return {"seq": lax.axis_index("seq") ^ 1}


def meet(count, masks):
    barrier = pltpu.get_barrier_semaphore()
    for mask in masks:
        pl.semaphore_signal(barrier, inc=1, device_id=peer_id(count, mask), device_id_type=pl.DeviceIdType.MESH)
    pl.semaphore_wait(barrier, len(masks))


def remote(count, source, target, send, recv, mask):
    return pltpu.make_async_remote_copy(
        src_ref=source,
        dst_ref=target,
        send_sem=send,
        recv_sem=recv,
        device_id=peer_id(count, mask),
        device_id_type=pl.DeviceIdType.MESH,
    )


def gather_kernel(count, tokens, own_ref, rows_ref, send_sems, recv_sems, local_sems):
    chunks = rows_ref.shape[0]
    span = tokens // 2
    direct_peers = (1, 2) if count == 4 else tuple(range(1, count))
    meet(count, direct_peers)

    def own(c):
        return pltpu.make_async_copy(
            own_ref.at[pl.ds(c * tokens, tokens)], rows_ref.at[c, pl.ds(0, tokens)], local_sems.at[c]
        )

    def direct(c, r):
        return remote(
            count,
            own_ref.at[pl.ds(c * tokens, tokens)],
            rows_ref.at[c, pl.ds(r * tokens, tokens)],
            send_sems.at[c, r],
            recv_sems.at[c, r],
            r,
        )

    def passed(c, half):
        start = (tokens, 2 * tokens + span)[half]
        return remote(
            count,
            rows_ref.at[c, pl.ds(start, span)],
            rows_ref.at[c, pl.ds(3 * tokens + half * span, span)],
            send_sems.at[c, 3 * half],
            recv_sems.at[c, 3 * half],
            2 - half,
        )

    for c in range(chunks):
        own(c).start()
        for r in direct_peers:
            direct(c, r).start()
    for c in range(chunks):
        for r in direct_peers:
            direct(c, r).wait_recv()
        if count == 4:
            passed(c, 0).start()
            passed(c, 1).start()
    for c in range(chunks):
        own(c).wait()
        for r in direct_peers:
            direct(c, r).wait_send()
        if count == 4:
            passed(c, 0).wait()
            passed(c, 1).wait()


def gather_rows(own, chunks, count):
    tokens = own.shape[0] // chunks
    return pl.pallas_call(
        functools.partial(gather_kernel, count, tokens),
        in_specs=[FAR],
        out_specs=FAR,
        out_shape=jax.ShapeDtypeStruct((chunks, tokens * count, own.shape[1]), BF16),
        scratch_shapes=[pltpu.SemaphoreType.DMA((chunks, count))] * 2 + [pltpu.SemaphoreType.DMA((chunks,))],
        compiler_params=pltpu.CompilerParams(collective_id=1, has_side_effects=True),
        cost_estimate=pl.CostEstimate(flops=0, bytes_accessed=120 * MIB, transcendentals=0),
        name="gather_rows",
    )(own)


def pick_one(index, options):
    result = options(0)
    for n in range(1, index[1]):
        result = lax.select(index[0] == n, options(n), result)
    return result


def to_places(count, span, holder, turned, source, target):
    for p in range(count):
        piece = pick_one((holder(p), count), source)
        first, second = piece[:span], piece[span:]
        swap = turned(p) == 1
        high = 2 * count - 1 - p
        target[p * span : (p + 1) * span, :] = lax.select(swap, second, first)
        target[high * span : (high + 1) * span, :] = lax.select(swap, first, second)


def from_places(count, span, pair, turned, source, store):
    for r in range(count):
        low = pick_one((pair(r), count), lambda p: source[p * span : (p + 1) * span, :])
        high = pick_one(
            (pair(r), count),
            lambda p: source[(2 * count - 1 - p) * span : (2 * count - p) * span, :],
        )
        swap = turned(r) == 1
        store(r, 0, lax.select(swap, high, low))
        store(r, 1, lax.select(swap, low, high))


def group_route(d):
    bit = d.bit_length() - 1
    return d - (1 << bit), bit


def forward_kernel(
    count,
    span,
    odd,
    masks,
    order_ref,
    place_ref,
    rows_ref,
    weight_ref,
    bias_ref,
    grad_ref,
    qkv_ref,
    mixed_ref,
    lse_ref,
    group_ref,
    rows,
    projected,
    outgoing,
    queries,
    keys,
    values,
    mixed,
    out_send,
    out_recv,
    group_send,
    group_recv,
    local_sems,
):
    chunks, length, _ = rows.shape
    pairs = weight_ref.shape[1] // (3 * LANES)
    tokens = 2 * span
    pieces = 1 << len(masks)

    def load_rows(c):
        return pltpu.make_async_copy(rows_ref.at[c], rows.at[c], local_sems.at[0, c])

    def save_qkv(c):
        return pltpu.make_async_copy(projected.at[c % 2], qkv_ref.at[c], local_sems.at[1, c])

    def keep(c):
        return pltpu.make_async_copy(
            outgoing.at[c, 0], mixed_ref.at[0, pl.ds(c * tokens, tokens)], local_sems.at[2, c]
        )

    def keep_grad(c):
        return pltpu.make_async_copy(
            grad_ref.at[pl.ds(c * tokens, tokens)], group_ref.at[0, c], local_sems.at[3, c]
        )

    def outward(c, r):
        return remote(
            count,
            outgoing.at[c, r],
            mixed_ref.at[r, pl.ds(c * tokens, tokens)],
            out_send.at[c, r],
            out_recv.at[c, r],
            r,
        )

    def grouped(c, d):
        origin, bit = group_route(d)
        source = grad_ref.at[pl.ds(c * tokens, tokens)] if origin == 0 else group_ref.at[origin, c]
        return remote(
            count, source, group_ref.at[d, c], group_send.at[c, d], group_recv.at[c, d], masks[bit]
        )

    for c in range(chunks):
        load_rows(c).start()
    meet(count, tuple(range(1, count)) + (count,))
    for c in range(chunks):
        keep_grad(c).start()
        for d in range(1, pieces):
            if group_route(d)[0] == 0:
                grouped(c, d).start()

    @pl.loop(0, chunks)
    def _(c):
        load_rows(c).wait()

        @pl.when(c >= 2)
        def _():
            save_qkv(c - 2).wait()

        @pl.loop(0, pairs)
        def _(j):
            columns = pl.ds(pl.multiple_of(j * 3 * LANES, LANES), 3 * LANES)
            block = (dot(rows[c], weight_ref[:, columns]) + bias_ref[:, columns]).astype(BF16)
            projected[c % 2, :, columns] = block
            for part, target in enumerate((queries, keys, values)):
                to_places(
                    count,
                    span,
                    lambda p: order_ref[c, p],
                    lambda p: order_ref[c, count + p],
                    lambda r: block[r * tokens : (r + 1) * tokens, part * LANES : (part + 1) * LANES],
                    target,
                )

            def one_head(head):
                lane = lax.broadcasted_iota(jnp.int32, (TILE, LANES), 1)
                mine = (lane // HEAD) == head
                for first in range(0, length, TILE):
                    last = first + TILE
                    query = jnp.where(mine, queries[first:last, :] * BF16(HEAD**-0.5), BF16(0))
                    scores = dot(query, keys[0:last, :], NT)
                    row = lax.broadcasted_iota(jnp.int32, (TILE, TILE), 0)
                    column = lax.broadcasted_iota(jnp.int32, (TILE, TILE), 1)
                    corner = jnp.where(column <= row, scores[:, first:last], -1e30)
                    scores = corner if first == 0 else jnp.concatenate([scores[:, :first], corner], axis=1)
                    row_max = jnp.max(scores, 1, keepdims=True)
                    weights = jnp.exp(scores - row_max)
                    total = jnp.sum(weights, 1, keepdims=True)
                    part = dot(weights.astype(BF16), values[0:last, :]) / total
                    lse_ref[c, j, head, first:last] = (row_max + jnp.log(total))[:, 0]
                    if head == 0:
                        mixed[first:last, :] = jnp.where(mine, part, 0.0).astype(BF16)
                    else:
                        mixed[first:last, :] = jnp.where(mine, part.astype(BF16), mixed[first:last, :])

            one_head(0)
            if odd:
                pl.when(j < pairs - 1)(lambda: one_head(1))
            else:
                one_head(1)
            lanes = pl.ds(pl.multiple_of(j * LANES, LANES), LANES)

            def put(r, half, value):
                outgoing[c, r, half * span : (half + 1) * span, lanes] = value

            from_places(
                count, span, lambda r: place_ref[c, r], lambda r: place_ref[c, count + r], mixed, put
            )

        save_qkv(c).start()
        keep(c).start()
        for r in range(1, count):
            outward(c, r).start()

    for c in range(chunks):
        keep_grad(c).wait()
    for d in range(1, pieces):
        origin = group_route(d)[0]
        for c in range(chunks):
            if origin != 0:
                grouped(c, d).start()
        for c in range(chunks):
            grouped(c, d).wait()
    for c in range(chunks):
        keep(c).wait()
        for r in range(1, count):
            outward(c, r).wait()
    for c in range(max(chunks - 2, 0), chunks):
        save_qkv(c).wait()


def call_forward(order, place, rows, weight, bias, grad, count, heads, masks):
    chunks, length, width = rows.shape
    columns = weight.shape[1]
    pairs, tokens, pieces = columns // (3 * LANES), length // count, 1 << len(masks)
    return pl.pallas_call(
        functools.partial(forward_kernel, count, tokens // 2, heads % 2 == 1, masks),
        in_specs=[SMEM, SMEM, FAR, VMEM, VMEM, FAR],
        out_specs=[FAR, FAR, VMEM, FAR],
        out_shape=[
            jax.ShapeDtypeStruct((chunks, length, columns), BF16),
            jax.ShapeDtypeStruct((count, chunks * tokens, pairs * LANES), BF16),
            jax.ShapeDtypeStruct((chunks, pairs, 2, length), F32),
            jax.ShapeDtypeStruct((pieces, chunks, tokens, width), BF16),
        ],
        scratch_shapes=[
            pltpu.VMEM((chunks, length, width), BF16),
            pltpu.VMEM((2, length, columns), BF16),
            pltpu.VMEM((chunks, count, tokens, pairs * LANES), BF16),
        ]
        + [pltpu.VMEM((length, LANES), BF16)] * 4
        + [pltpu.SemaphoreType.DMA((chunks, count))] * 2
        + [pltpu.SemaphoreType.DMA((chunks, pieces))] * 2
        + [pltpu.SemaphoreType.DMA((4, chunks))],
        compiler_params=pltpu.CompilerParams(
            collective_id=2, has_side_effects=True, vmem_limit_bytes=52 * MIB
        ),
        cost_estimate=pl.CostEstimate(
            flops=chunks * (2 * length * width * columns + heads * length * length * 5 * 256),
            bytes_accessed=80 * MIB,
            transcendentals=chunks * heads * length * length,
        ),
        name="attend_forward",
    )(order, place, rows, weight, bias, grad)


def backward_kernel(
    count,
    span,
    odd,
    order_ref,
    place_ref,
    qkv_ref,
    grad_ref,
    lse_ref,
    weight_ref,
    out_ref,
    sum_ref,
    arrived,
    block,
    result,
    queries,
    keys,
    values,
    grads,
    query_grad,
    key_sum,
    value_sum,
    first_out,
    first_in,
    side,
    second_out,
    second_in,
    head_send,
    head_recv,
    first_send,
    first_recv,
    second_send,
    second_recv,
    local_sems,
):
    chunks, length = out_ref.shape[:2]
    pairs = weight_ref.shape[1] // (3 * LANES)
    tokens = 2 * span

    def load_qkv(c):
        return pltpu.make_async_copy(qkv_ref.at[c], block.at[c % 2], local_sems.at[0, c])

    def load_own(c):
        return pltpu.make_async_copy(
            grad_ref.at[0, pl.ds(c * tokens, tokens)], arrived.at[c, 0], local_sems.at[1, c]
        )

    def save(c):
        return pltpu.make_async_copy(result, out_ref.at[c], local_sems.at[2, c])

    def inward(c, r):
        return remote(
            count,
            grad_ref.at[r, pl.ds(c * tokens, tokens)],
            arrived.at[c, r],
            head_send.at[c, r],
            head_recv.at[c, r],
            r,
        )

    def first(c, half):
        return remote(
            count,
            first_out.at[c, half],
            first_in.at[c, half],
            first_send.at[c, half],
            first_recv.at[c, half],
            2 - half,
        )

    def second(c, r):
        return remote(
            count,
            second_out.at[c, r - 1],
            second_in.at[c, r - 1],
            second_send.at[c, r - 1],
            second_recv.at[c, r - 1],
            r,
        )

    direct_peers = (1, 2) if count == 4 else tuple(range(1, count))

    def send_sums(c):
        if count == 4:
            first(c, 0).wait_recv()
            first(c, 1).wait_recv()
            second_out[c, 0, 0:span] = (side[0, 0:span] + first_in[c, 0].astype(F32)).astype(BF16)
            second_out[c, 0, span:tokens] = side[0, span:tokens].astype(BF16)
            second_out[c, 1, 0:span] = side[1, 0:span].astype(BF16)
            second_out[c, 1, span:tokens] = (side[1, span:tokens] + first_in[c, 1].astype(F32)).astype(
                BF16
            )
        for r in direct_peers:
            second(c, r).start()

    load_qkv(0).start()
    meet(count, tuple(range(1, count)))
    for c in range(chunks):
        load_own(c).start()
        for r in range(1, count):
            inward(c, r).start()

    @pl.loop(0, chunks)
    def _(c):
        load_qkv(c).wait()

        @pl.when(c < chunks - 1)
        def _():
            load_qkv(c + 1).start()

        load_own(c).wait()
        for r in range(1, count):
            inward(c, r).wait_recv()

        @pl.when(c >= 1)
        def _():
            save(c - 1).wait()

        @pl.loop(0, pairs)
        def _(j):
            @pl.when((j == pairs - 1) & (c >= 1))
            def _():
                send_sums(c - 1)

            def place(source, target):
                to_places(
                    count,
                    span,
                    lambda p: order_ref[c, p],
                    lambda p: order_ref[c, count + p],
                    source,
                    target,
                )

            for part, target in enumerate((queries, keys, values)):
                lanes = pl.ds(pl.multiple_of(j * 3 * LANES + part * LANES, LANES), LANES)
                place(lambda r: block[c % 2, r * tokens : (r + 1) * tokens, lanes], target)
            lanes = pl.ds(pl.multiple_of(j * LANES, LANES), LANES)
            place(lambda r: arrived[c, r, :, lanes], grads)

            def one_head(head):
                lane = lax.broadcasted_iota(jnp.int32, (TILE, LANES), 1)
                mine = (lane // HEAD) == head
                for first_row in reversed(range(0, length, TILE)):
                    last = first_row + TILE
                    query = jnp.where(mine, queries[first_row:last, :] * BF16(HEAD**-0.5), BF16(0))
                    grad = jnp.where(mine, grads[first_row:last, :], BF16(0))
                    scores = dot(query, keys[0:last, :], NT)
                    row = lax.broadcasted_iota(jnp.int32, (TILE, TILE), 0)
                    column = lax.broadcasted_iota(jnp.int32, (TILE, TILE), 1)
                    corner = jnp.where(column <= row, scores[:, first_row:last], -1e30)
                    scores = (
                        corner if first_row == 0 else jnp.concatenate([scores[:, :first_row], corner], axis=1)
                    )
                    weights = jnp.exp(scores - lse_ref[c, j, head, first_row:last][:, None])
                    prob_grad = dot(grad, values[0:last, :], NT)
                    product = weights * prob_grad
                    inner = jnp.sum(product, 1, keepdims=True)
                    score_grad = (product - weights * inner).astype(BF16)
                    rounded = weights.astype(BF16)
                    part = (dot(score_grad, keys[0:last, :]) * HEAD**-0.5).astype(BF16)
                    key_part = dot(query, score_grad, TN)
                    value_part = dot(grad, rounded, TN)
                    if head == 0 and last == length:
                        key_sum[...] = key_part
                        value_sum[...] = value_part
                    else:
                        key_sum[:, 0:last] += key_part
                        value_sum[:, 0:last] += value_part
                    if head == 0:
                        query_grad[first_row:last, :] = jnp.where(mine, part, BF16(0))
                    else:
                        query_grad[first_row:last, :] = jnp.where(mine, part, query_grad[first_row:last, :])

            one_head(0)
            if odd:
                pl.when(j < pairs - 1)(lambda: one_head(1))
            else:
                one_head(1)
            keys[...] = key_sum[...].T.astype(BF16)
            values[...] = value_sum[...].T.astype(BF16)
            for part, source in enumerate((query_grad, keys, values)):
                lanes = pl.ds(pl.multiple_of(j * 3 * LANES + part * LANES, LANES), LANES)

                def put(r, half, value):
                    start = r * tokens + half * span
                    result[start : start + span, lanes] = value

                from_places(
                    count, span, lambda r: place_ref[c, r], lambda r: place_ref[c, count + r], source, put
                )

        save(c).start()

        def share(first_piece, last_piece):
            return dot(result[first_piece * tokens : last_piece * tokens, :], weight_ref[...], NT)

        if count == 4:
            far = share(2, 4)
            first_out[c, 0] = far[tokens : tokens + span].astype(BF16)
            first_out[c, 1] = far[tokens + span :].astype(BF16)
            first(c, 0).start()
            first(c, 1).start()
            side[1] = far[:tokens]
            near = share(0, 2)
            side[0] = near[tokens:]
        else:
            for r in direct_peers:
                second_out[c, r - 1] = share(r, r + 1).astype(BF16)
            near = share(0, 1)
        sum_ref[pl.ds(pl.multiple_of(c * tokens, tokens), tokens), :] = near[:tokens]

    send_sums(chunks - 1)

    for c in range(chunks):
        total = sum_ref[c * tokens : (c + 1) * tokens, :]
        for r in direct_peers:
            second(c, r).wait_recv()
            total = total + second_in[c, r - 1].astype(F32)
        sum_ref[c * tokens : (c + 1) * tokens, :] = total
        for r in direct_peers:
            second(c, r).wait_send()
        if count == 4:
            first(c, 0).wait_send()
            first(c, 1).wait_send()
        for r in range(1, count):
            inward(c, r).wait_send()
    save(chunks - 1).wait()


def call_backward(order, place, qkv, grads, lse, weight, count, heads):
    chunks, length, columns = qkv.shape
    width = weight.shape[0]
    pairs, tokens = columns // (3 * LANES), length // count
    sides = 2 if count == 4 else count - 1
    return pl.pallas_call(
        functools.partial(backward_kernel, count, tokens // 2, heads % 2 == 1),
        in_specs=[SMEM, SMEM, FAR, FAR, VMEM, VMEM],
        out_specs=[FAR, VMEM],
        out_shape=[
            jax.ShapeDtypeStruct((chunks, length, columns), BF16),
            jax.ShapeDtypeStruct((chunks * tokens, width), F32),
        ],
        scratch_shapes=[
            pltpu.VMEM((chunks, count, tokens, pairs * LANES), BF16),
            pltpu.VMEM((2, length, columns), BF16),
            pltpu.VMEM((length, columns), BF16),
        ]
        + [pltpu.VMEM((length, LANES), BF16)] * 5
        + [pltpu.VMEM((LANES, length), F32)] * 2
        + [
            pltpu.VMEM((chunks, 2, tokens // 2, width), BF16),
            pltpu.VMEM((chunks, 2, tokens // 2, width), BF16),
            pltpu.VMEM((2, tokens, width), F32),
            pltpu.VMEM((chunks, sides, tokens, width), BF16),
            pltpu.VMEM((chunks, sides, tokens, width), BF16),
        ]
        + [pltpu.SemaphoreType.DMA((chunks, count))] * 2
        + [pltpu.SemaphoreType.DMA((chunks, 2))] * 2
        + [pltpu.SemaphoreType.DMA((chunks, sides))] * 2
        + [pltpu.SemaphoreType.DMA((3, chunks))],
        compiler_params=pltpu.CompilerParams(
            collective_id=3, has_side_effects=True, vmem_limit_bytes=60 * MIB
        ),
        cost_estimate=pl.CostEstimate(
            flops=chunks * (2 * length * width * columns + heads * length * length * 8 * 256),
            bytes_accessed=80 * MIB,
            transcendentals=chunks * heads * length * length,
        ),
        name="attend_backward",
    )(order, place, qkv, grads, lse, weight)


def gelu_pair(u):
    scale = 0.7978845608028654
    square = u * u
    inner = jnp.tanh(u * (scale + scale * 0.044715 * square))
    half = 0.5 + 0.5 * inner
    slope = half + u * (half * (1.0 - inner)) * (scale + scale * 0.134145 * square)
    return u * half, slope


def hidden_kernel(
    count, masks, own_ref, weight_ref, bias_ref, rows_ref, value_ref, slope_ref, rows, staged,
    group_send, group_recv, local_sems, save_sems,
):
    chunks, pieces, tokens, width = rows.shape

    def keep(c):
        return pltpu.make_async_copy(own_ref.at[pl.ds(c * tokens, tokens)], rows.at[c, 0], local_sems.at[0, c])

    def save_rows(c):
        return pltpu.make_async_copy(rows.at[c], rows_ref.at[c], local_sems.at[1, c])

    def grouped(c, d):
        origin, bit = group_route(d)
        source = own_ref.at[pl.ds(c * tokens, tokens)] if origin == 0 else rows.at[c, origin]
        return remote(count, source, rows.at[c, d], group_send.at[c, d], group_recv.at[c, d], masks[bit])

    def save(n, part):
        c, i = n // pieces, n % pieces
        p = (i % 2) * 2 + i // 2
        target = value_ref.at[p, c] if part == 0 else slope_ref.at[c, p]
        return pltpu.make_async_copy(staged.at[n % 2, part], target, save_sems.at[n % 2, part])

    for c in range(chunks):
        keep(c).start()
    meet(count, masks)
    for c in range(chunks):
        grouped(c, 1).start()
    for c in range(chunks):
        grouped(c, 2).start()

    @pl.loop(0, chunks)
    def _(c):
        keep(c).wait()

        @pl.loop(0, pieces)
        def _(i):
            p = (i % 2) * 2 + i // 2
            step = c * pieces + i

            @pl.when(i == 1)
            def _():
                grouped(c, 2).wait_recv()

            @pl.when(i == 2)
            def _():
                grouped(c, 1).wait_recv()
                grouped(c, 3).start()

            @pl.when(i == 3)
            def _():
                grouped(c, 3).wait_recv()
                save_rows(c).start()

            value, slope = gelu_pair(dot(rows[c, p], weight_ref[...]) + bias_ref[...])

            @pl.when(step >= 2)
            def _():
                for part in range(2):
                    save(step - 2, part).wait()

            staged[step % 2, 0] = value.astype(BF16)
            staged[step % 2, 1] = slope.astype(BF16)
            for part in range(2):
                save(step, part).start()

    for c in range(chunks):
        save_rows(c).wait()
        for d in range(1, pieces):
            grouped(c, d).wait_send()
    for step in range(chunks * pieces - 2, chunks * pieces):
        for part in range(2):
            save(step, part).wait()


def call_hidden(own, weight, bias, chunks, count, masks):
    width, hidden = weight.shape
    tokens, pieces = own.shape[0] // chunks, 1 << len(masks)
    return pl.pallas_call(
        functools.partial(hidden_kernel, count, masks),
        in_specs=[FAR, VMEM, VMEM],
        out_specs=[FAR] * 3,
        out_shape=[
            jax.ShapeDtypeStruct((chunks, pieces, tokens, width), BF16),
            jax.ShapeDtypeStruct((pieces, chunks, tokens, hidden), BF16),
            jax.ShapeDtypeStruct((chunks, pieces, tokens, hidden), BF16),
        ],
        scratch_shapes=[
            pltpu.VMEM((chunks, pieces, tokens, width), BF16),
            pltpu.VMEM((2, 2, tokens, hidden), BF16),
            pltpu.SemaphoreType.DMA((chunks, pieces)),
            pltpu.SemaphoreType.DMA((chunks, pieces)),
            pltpu.SemaphoreType.DMA((2, chunks)),
            pltpu.SemaphoreType.DMA((2, 2)),
        ],
        compiler_params=pltpu.CompilerParams(
            collective_id=4, has_side_effects=True, vmem_limit_bytes=44 * MIB
        ),
        cost_estimate=pl.CostEstimate(
            flops=2 * chunks * pieces * tokens * width * hidden, bytes_accessed=100 * MIB, transcendentals=0
        ),
        name="hidden_forward",
    )(own, weight, bias)


def group_kernel(count, masks, backward, *refs):
    if backward:
        grad_ref, slope_ref, contract_ref, weight_ref, part_ref, other_ref, sum_ref, out_ref, staged = refs[:9]
        sources = (grad_ref, slope_ref)
    else:
        value_ref, weight_ref, residual_ref, bias_ref, part_ref, other_ref, sum_ref = refs[:7]
        sources = (value_ref,)
    scratch = refs[9:] if backward else refs[7:]
    loaded, partial, from_core, over, from_side = scratch[:5]
    core_send, core_recv, side_send, side_recv, cargo_sems, load_sems, save_sems = scratch[5:]
    chunks, tokens, _ = over.shape
    steps = 4 * chunks
    high = count // 2
    stays = lax.rem(lax.axis_index("seq"), 2) == lax.axis_index("tp") // high

    def place(step):
        return lax.rem(step, 2 * chunks) // 2, 3 - step // (2 * chunks) - 2 * lax.rem(step, 2)

    def load(step, part):
        c, p = place(step)
        slot = lax.rem(step, 2)
        source = sources[part].at[p, c] if part == 0 else sources[part].at[c, p]
        return pltpu.make_async_copy(source, loaded.at[slot, part], load_sems.at[slot, part])

    def save(step):
        c, p = place(step)
        slot = lax.rem(step, 2)
        return pltpu.make_async_copy(staged.at[slot], out_ref.at[c, p], save_sems.at[slot])

    def to_core(c, p):
        return remote(
            count, partial.at[c, p], from_core.at[c, p - 2], core_send.at[c, p - 2], core_recv.at[c, p - 2], masks[1]
        )

    def to_side(c):
        return remote(count, over.at[c], from_side.at[c], side_send.at[c], side_recv.at[c], masks[0])

    def cargo():
        return remote(count, part_ref, other_ref, cargo_sems.at[0], cargo_sems.at[1], high)

    for part in range(len(sources)):
        load(0, part).start()
    meet(count, masks + (high,))

    @pl.when(jnp.logical_not(stays))
    def _():
        cargo().start()

    @pl.loop(0, steps)
    def _(step):
        c, p = place(step)
        slot = lax.rem(step, 2)
        for part in range(len(sources)):
            load(step, part).wait()

        @pl.when(step < steps - 1)
        def _():
            for part in range(len(sources)):
                load(step + 1, part).start()

        @pl.when((slot == 0) & (step >= 2) & (step <= 2 * chunks))
        def _():
            before = step // 2 - 1
            to_core(before, 3).wait_recv()
            over[before] = (partial[before, 1].astype(F32) + from_core[before, 1].astype(F32)).astype(BF16)
            to_side(before).start()

        if backward:
            hidden = dot(loaded[slot, 0], contract_ref[...]) * loaded[slot, 1].astype(F32)
            hidden = hidden.astype(BF16)

            @pl.when(step >= 2)
            def _():
                save(step - 2).wait()

            staged[slot] = hidden
            save(step).start()
        else:
            hidden = loaded[slot, 0]
        partial[c, p] = dot(hidden, weight_ref[...], NT).astype(BF16)

        @pl.when(p >= 2)
        def _():
            to_core(c, p).start()

    for c in range(chunks):
        to_core(c, 2).wait_recv()
        to_side(c).wait_recv()
        total = partial[c, 0].astype(F32) + from_core[c, 0].astype(F32) + from_side[c].astype(F32)
        mine = slice(c * tokens, (c + 1) * tokens)
        if backward:
            sum_ref[mine, :] = total
        else:
            sum_ref[mine, :] = (residual_ref[mine, :] + total + bias_ref[...]).astype(BF16)
        to_core(c, 2).wait_send()
        to_core(c, 3).wait_send()
        to_side(c).wait_send()
    if backward:
        for step in range(steps - 2, steps):
            save(step).wait()

    @pl.when(stays)
    def _():
        cargo().wait_recv()

    @pl.when(jnp.logical_not(stays))
    def _():
        cargo().wait_send()


def call_group(count, masks, backward, tiles, weights, part):
    pieces, chunks, tokens, width = tiles[0].shape
    outs = [
        jax.ShapeDtypeStruct(part.shape, BF16),
        jax.ShapeDtypeStruct((chunks * tokens, width), F32 if backward else BF16),
    ]
    scratch = [
        pltpu.VMEM((2, len(tiles), tokens, width), BF16),
        pltpu.VMEM((chunks, pieces, tokens, width), BF16),
        pltpu.VMEM((chunks, 2, tokens, width), BF16),
        pltpu.VMEM((chunks, tokens, width), BF16),
        pltpu.VMEM((chunks, tokens, width), BF16),
        pltpu.SemaphoreType.DMA((chunks, 2)),
        pltpu.SemaphoreType.DMA((chunks, 2)),
        pltpu.SemaphoreType.DMA((chunks,)),
        pltpu.SemaphoreType.DMA((chunks,)),
        pltpu.SemaphoreType.DMA((2,)),
        pltpu.SemaphoreType.DMA((2, len(tiles))),
        pltpu.SemaphoreType.DMA((2,)),
    ]
    if backward:
        outs.append(jax.ShapeDtypeStruct((chunks, pieces, tokens, width), BF16))
        scratch = [pltpu.VMEM((2, tokens, width), BF16)] + scratch
    return pl.pallas_call(
        functools.partial(group_kernel, count, masks, backward),
        in_specs=[FAR] * len(tiles) + [VMEM] * len(weights) + [FAR],
        out_specs=[FAR, VMEM] + [FAR] * (len(outs) - 2),
        out_shape=outs,
        scratch_shapes=scratch,
        compiler_params=pltpu.CompilerParams(
            collective_id=5 if backward else 6, has_side_effects=True, vmem_limit_bytes=56 * MIB
        ),
        cost_estimate=pl.CostEstimate(
            flops=(4 if backward else 2) * chunks * pieces * tokens * width * width,
            bytes_accessed=160 * MIB,
            transcendentals=0,
        ),
        name="group_backward" if backward else "group_forward",
    )(*tiles, *weights, part)


def statistics(values):
    centred = values - jnp.mean(values, -1, keepdims=True)
    spread = jnp.mean(centred * centred, -1, keepdims=True)
    inverse = lax.rsqrt(spread + epsilon)
    return centred * inverse, inverse


def norm_forward(values, gain, shift):
    return (statistics(values)[0] * gain + shift).astype(BF16)


def norm_backward(values, gain, grad):
    normal, inverse = statistics(values)
    scaled = grad * gain
    spread = jnp.mean(scaled * normal, -1, keepdims=True)
    result = inverse * (scaled - jnp.mean(scaled, -1, keepdims=True) - normal * spread)
    return result, jnp.sum(grad * normal, 0), jnp.sum(grad, 0)


def body(
    seq_count,
    tp_count,
    tokens,
    positions,
    ln1_gain,
    ln1_bias,
    query_key_value_weight,
    qv_bias,
    attention_output_weight,
    attention_output_bias,
    ln2_gain,
    ln2_bias,
    expand_weight,
    expand_bias,
    contract_weight,
    contract_bias,
    cotangent,
):
    devices = seq_count * tp_count
    both = ("seq", "tp")
    t = lax.axis_index("tp")
    core = lax.axis_index("seq") % 2
    core_bit = tp_count
    tp_bits = [1 << k for k in range(tp_count.bit_length() - 1)]
    high = tp_bits[-1]
    ff_bits = tp_bits[:-1] + [core_bit]
    chunks, rows, width = tokens.shape
    span = rows // 2
    group_heads = -(-HEADS // tp_count)
    group = group_heads * HEAD
    pairs = -(-group_heads // 2)
    padded = pairs * LANES
    hidden = expand_weight.shape[1]
    peers = t ^ jnp.arange(tp_count)

    def swap(value, mask):
        return lax.ppermute(value, both, [(i, i ^ mask) for i in range(devices)])

    def after(value, *earlier):
        return lax.optimization_barrier((value, *earlier))[0]

    def choose(pieces, index):
        result = pieces[0]
        for n in range(1, len(pieces)):
            result = jnp.where(index == n, pieces[n], result)
        return result

    def gather_ff(value):
        pieces = [value]
        for bit in ff_bits:
            pieces += [swap(piece, bit) for piece in pieces]
        return pieces

    def sum_ff(pieces):
        while len(pieces) > 1:
            half = len(pieces) // 2
            bit = ff_bits[half.bit_length() - 1]
            pieces = [
                piece + swap(other, bit) for piece, other in zip(pieces[:half], pieces[half:], strict=True)
            ]
        return pieces[0]

    def sum_all(value):
        for k in range(devices.bit_length() - 1):
            value = value + swap(value, 1 << k)
        return value

    columns = query_key_value_weight.shape[1]
    feature = lax.broadcasted_iota(jnp.int32, (1, padded), 1)

    def shard_columns(owner, holder):
        found = []
        for part in range(3):
            column = part * width + holder * group + feature - columns * owner
            valid = (feature < group) & (holder * group + feature < width)
            found.append(jnp.where(valid & (column >= 0) & (column < columns), column, -1))
        return found

    def to_block(packed):
        parts = []
        for part in range(3):
            chosen = jnp.zeros_like(packed[0])
            for r in range(tp_count):
                chosen = jnp.where(shard_columns(t ^ r, t)[part] >= 0, packed[r], chosen)
            parts.append(chosen.reshape(-1, pairs, 1, LANES))
        return jnp.concatenate(parts, 2).reshape(-1, 3 * padded)

    def from_block(value):
        value = value.reshape(-1, pairs, 3, LANES)
        packed = []
        for r in range(tp_count):
            chosen = jnp.zeros((value.shape[0], padded), value.dtype)
            for part in range(3):
                here = shard_columns(t ^ r, t)[part] >= 0
                chosen = jnp.where(here, value[:, :, part].reshape(-1, padded), chosen)
            packed.append(chosen)
        return packed

    shard_index = lax.broadcasted_iota(jnp.int32, (columns, 1), 0)
    pick = []
    for r in range(tp_count):
        first, second, third = shard_columns(t, t ^ r)
        pick.append((shard_index == jnp.maximum(jnp.maximum(first, second), third)).astype(BF16))
    pick = jnp.concatenate(pick, 1)
    packed = dot(query_key_value_weight, pick).astype(BF16)
    packed = [packed[:, r * padded : (r + 1) * padded] for r in range(tp_count)]
    packed = [packed[0]] + [swap(packed[r], r) for r in range(1, tp_count)]

    flat = tokens.reshape(-1, width)
    gain_one, shift_one = ln1_gain.astype(F32), ln1_bias.astype(F32)
    gain_two, shift_two = ln2_gain.astype(F32), ln2_bias.astype(F32)
    normal_own = norm_forward(flat.astype(F32), gain_one, shift_one)
    qkv_rows = to_block(packed)
    qkv_weight = lax.all_gather(qkv_rows, "seq", axis=0, tiled=True)

    def head_columns(vector):
        whole = jnp.pad(vector, (0, tp_count * group - width))
        mine = lax.dynamic_slice_in_dim(whole, t * group, group)
        return jnp.pad(mine, (0, padded - group)).reshape(pairs, LANES)

    query_bias, value_bias = head_columns(qv_bias[0]), head_columns(qv_bias[1])
    qkv_bias = jnp.stack([query_bias, jnp.zeros_like(query_bias), value_bias], 1).reshape(-1)

    place = positions.reshape(chunks, tp_count, 2, span)[:, :, 0, 0] // span
    place = jnp.take(place, peers, axis=1)
    turned = (place >= tp_count).astype(jnp.int32)
    pair = jnp.minimum(place, 2 * tp_count - 1 - place)
    holds = pair[:, None, :] == jnp.arange(tp_count)[None, :, None]
    holder = jnp.sum(jnp.where(holds, jnp.arange(tp_count), 0), 2)
    orders = jnp.concatenate([holder, jnp.sum(jnp.where(holds, turned[:, None, :], 0), 2)], 1).astype(jnp.int32)
    places = jnp.concatenate([pair, turned], 1).astype(jnp.int32)
    masks = tuple(ff_bits)
    members = 1 << len(masks)

    stays = core == t // high
    block = t % high + core * high
    send = [
        (s * tp_count + i, s * tp_count + (i ^ high))
        for s in range(seq_count)
        for i in range(tp_count)
        if s % 2 == i // high
    ]

    def gather_seq(shard):
        return lax.all_gather(shard, "seq", axis=0, tiled=True)

    def take_block(whole):
        return jnp.where(stays, whole, lax.ppermute(whole, both, send))

    def give_block(partial):
        return lax.ppermute(partial, both, [(b, a) for a, b in send])

    def keep_block(partial, other):
        return jnp.where(stays, partial.astype(F32) + other, 0.0).astype(BF16)

    def sum_seq(partial):
        return after(lax.psum_scatter(partial, "seq", scatter_dimension=0, tiled=True))

    shards = [attention_output_weight] + [swap(attention_output_weight, r) for r in range(1, tp_count)]
    out_row = jnp.concatenate([choose(shards, t ^ a) for a in range(tp_count)], 1)
    normal_one = gather_rows(after(normal_own, out_row, qkv_rows), chunks, tp_count)
    expand = take_block(gather_seq(expand_weight))
    contract_whole = gather_seq(after(contract_weight.T, normal_one))
    hidden_bias = lax.dynamic_slice_in_dim(expand_bias, block * hidden, hidden).astype(F32)

    out_weight = gather_seq(after(out_row, normal_one))

    qkv, heads_out, lse, output_rows = call_forward(
        orders,
        places,
        normal_one,
        qkv_weight,
        qkv_bias.astype(F32).reshape(1, -1),
        cotangent.reshape(-1, width),
        tp_count,
        group_heads,
        masks,
    )
    contract = take_block(after(contract_whole, heads_out))
    pieces = [heads_out[r, :, :group] for r in range(tp_count)]
    mixed = jnp.concatenate([choose(pieces, t ^ a) for a in range(tp_count)], 1)[:, :width]
    residual = flat.astype(F32) + dot(mixed, out_weight) + attention_output_bias
    normal = norm_forward(residual, gain_two, shift_two)

    flat_rows = output_rows.reshape(-1, width)
    if tp_count == 4:
        normal_two, value, slope = call_hidden(
            normal, expand, hidden_bias.reshape(1, -1), chunks, tp_count, masks
        )
        value = value.reshape(-1, hidden)
        contract_grad = dot(flat_rows, value, TN).astype(BF16)
        other, norm_grad, hidden_grad = call_group(
            tp_count, masks, True, [output_rows, slope], [contract, expand], contract_grad
        )
        contract_grad = keep_block(contract_grad, other)
        proj_weight_grad = sum_seq(contract_grad)
        normal_two, hidden_grad = normal_two.reshape(-1, width), hidden_grad.reshape(-1, hidden)
        expand_grad = dot(normal_two, after(hidden_grad, contract_grad), TN).astype(BF16)
        expand_grad = after(expand_grad, proj_weight_grad)
        other, layer_out = call_group(
            tp_count,
            masks,
            False,
            [value.reshape(members, chunks, rows, hidden)],
            [contract, residual, contract_bias.astype(F32).reshape(1, -1)],
            expand_grad,
        )
        expand_grad = keep_block(expand_grad, other)
    else:
        normal_two = jnp.concatenate(gather_ff(normal), 0)
        value, slope = gelu_pair(dot(normal_two, expand) + hidden_bias)
        value = value.astype(BF16)
        contract_grad = dot(flat_rows, value, TN).astype(BF16)
        hidden_grad = (dot(flat_rows, contract) * slope).astype(BF16)
        partial = dot(hidden_grad, expand, NT).astype(BF16).reshape(members, -1, width)
        norm_grad = sum_ff([partial[d] for d in range(members)]).astype(F32)
        proj_weight_grad = sum_seq(keep_block(contract_grad, give_block(contract_grad)))
        expand_grad = dot(normal_two, hidden_grad, TN).astype(BF16)
        expand_grad = keep_block(expand_grad, give_block(expand_grad))
        members_value = value.reshape(members, -1, hidden)
        feed = [dot(members_value[d], contract, NT).astype(BF16) for d in range(members)]
        layer_out = (residual + sum_ff(feed) + contract_bias).astype(BF16)
    fc_weight_grad = sum_seq(expand_grad)
    hidden_bias_grad = jnp.sum(hidden_grad, 0, dtype=F32)

    from_norm, gain_two_grad, shift_two_grad = norm_backward(residual, gain_two, norm_grad)
    resid_grad = cotangent.reshape(-1, width).astype(F32) + from_norm
    branch = resid_grad.astype(BF16)
    head_grad = dot(branch, out_weight, NT).astype(BF16)
    head_grad = jnp.pad(head_grad, ((0, 0), (0, tp_count * group - width)))
    pieces = [head_grad[:, a * group : (a + 1) * group] for a in range(tp_count)]
    pieces = [jnp.pad(choose(pieces, t ^ r), ((0, 0), (0, padded - group))) for r in range(tp_count)]
    out_grad = sum_seq(dot(mixed, branch, TN).astype(BF16))

    qkv_grads, one_grad = call_backward(
        orders,
        places,
        after(qkv, expand_grad, out_grad),
        jnp.stack(pieces),
        lse,
        qkv_weight,
        tp_count,
        group_heads,
    )
    qkv_grads = after(qkv_grads, fc_weight_grad)
    out_grad = [out_grad[:, a * (width // tp_count) : (a + 1) * (width // tp_count)] for a in range(tp_count)]
    out_weight_grad = choose(out_grad, t).astype(F32)
    for r in range(1, tp_count):
        out_weight_grad = out_weight_grad + swap(choose(out_grad, t ^ r), r)

    qkv_grads = qkv_grads.reshape(-1, 3 * padded)
    qkv_grad = dot(normal_one.reshape(-1, width), qkv_grads, TN)
    qkv_bias_grad = jnp.sum(qkv_grads, 0, dtype=F32)
    from_norm, gain_one_grad, shift_one_grad = norm_backward(flat.astype(F32), gain_one, one_grad)
    input_grad = (resid_grad + from_norm).astype(BF16).reshape(tokens.shape)

    summed = lax.psum_scatter(qkv_grad.astype(BF16), "seq", scatter_dimension=0, tiled=True)
    packed = from_block(summed)
    packed = [packed[0]] + [swap(packed[r], r) for r in range(1, tp_count)]
    qkv_weight_grad = dot(jnp.concatenate(packed, 1), pick, NT)

    qkv_bias_grad = qkv_bias_grad.reshape(pairs, 3, LANES)

    def whole_bias(part):
        mine = qkv_bias_grad[:, part].reshape(-1)[:group]
        whole = jnp.zeros((tp_count * group,), F32)
        return lax.dynamic_update_slice_in_dim(whole, mine, t * group, 0)[:width]

    hidden_whole = lax.dynamic_update_slice_in_dim(
        jnp.zeros(expand_bias.shape, F32), hidden_bias_grad, block * hidden, 0
    )
    out_bias_part = jnp.sum(branch, 0, dtype=F32)
    proj_bias_part = jnp.sum(cotangent, axis=(0, 1), dtype=F32)
    early = sum_all(
        jnp.concatenate([gain_two_grad, shift_two_grad, out_bias_part, proj_bias_part, hidden_whole])
    )
    late = sum_all(jnp.concatenate([gain_one_grad, shift_one_grad, whole_bias(0), whole_bias(2)]))

    def part(vector, index):
        return vector[index * width : (index + 1) * width]

    return (
        layer_out.reshape(tokens.shape),
        input_grad,
        part(late, 0),
        part(late, 1),
        qkv_weight_grad,
        late[2 * width :].reshape(2, width),
        out_weight_grad,
        part(early, 2),
        part(early, 0),
        part(early, 1),
        fc_weight_grad.astype(F32),
        early[4 * width :],
        proj_weight_grad.astype(F32).T,
        part(early, 3),
    )


def solution(mesh):
    in_specs = (
        P("seq", "tp", None),
        P("seq", None),
        P(),
        P(),
        P("seq", "tp"),
        P(),
        P("seq", "tp"),
        P(),
        P(),
        P(),
        P("seq", "tp"),
        P(),
        P("tp", "seq"),
        P(),
        P("seq", "tp", None),
    )
    out_specs = (
        P("seq", "tp", None),
        P("seq", "tp", None),
        P(),
        P(),
        P("seq", "tp"),
        P(),
        P("seq", "tp"),
        P(),
        P(),
        P(),
        P("seq", "tp"),
        P(),
        P("tp", "seq"),
        P(),
    )
    placed = functools.partial(body, mesh.shape["seq"], mesh.shape["tp"])
    return jax.shard_map(placed, mesh=mesh, in_specs=in_specs, out_specs=out_specs, check_vma=False)
```

time: 1090 us -> 886 us (0.81)
  Pallas kernels: 103 us -> 528 us
  waiting for transfers between devices: 310 us -> 59 us
  matrix products: 336 us -> 108 us
  starting transfers between devices: 114 us -> 34.5 us
  other arithmetic: 115 us -> 82.2 us
  local copies, waits for them, and re-layouts: 82.1 us -> 49.3 us
    pallas_call x6, Pallas kernels: 103 us -> 528 us  [the longest x2 143 us: call_group(): pl.pallas_call(functools.partial(group_kernel, count, masks, backward), i...]
    ppermute x100 -> x22, waiting for transfers between devices: 309 us -> 43.9 us  [swap(): return lax.ppermute(value, both, [(i, i ^ mask) for i in range(devices)])]
    dot_general x45 -> x8, matrix products: 336 us -> 108 us  [dot(): return lax.dot_general(left, right, dims, preferred_element_type=F32)]
    ppermute x100 -> x22, starting transfers between devices: 101 us -> 21.1 us  [swap(): return lax.ppermute(value, both, [(i, i ^ mask) for i in range(devices)])]
    convert_element_type x16 -> x7, other arithmetic: 40.3 us -> 21.1 us  [the longest x2 13.2 us: keep_block(): return jnp.where(stays, partial.astype(F32) + other, 0.0).astype(BF16)]
    unnamed x11, waiting for transfers between devices: 0.8 us -> 15.1 us
    another operation x9 -> x1, other arithmetic: 14.9 us -> 1.92 us  [body(): jnp.stack(pieces)]
    slice x17 -> x3, local copies, waits for them, and re-layouts: 16.2 us -> 3.64 us  [the longest x1 3.58 us: from_block(): chosen = jnp.where(here, value[:, :, part].reshape(-1, padded), chosen)]
  transfers between devices with their start and end apart: 112 -> 32, of which waited for: 37 -> 13; matrix products, arithmetic and copies ran while one was open for 47% -> 21% of each run, Pallas kernels for 8% -> 52%
where the time goes in v2:
time: 886 us; the launch traced here: 876 us
  Pallas kernels  528 us (60%)
  matrix products  108 us (12%)
  other arithmetic  82.2 us (9%)
  waiting for transfers between devices  59 us (7%)
  local copies, waits for them, and re-layouts  49.3 us (6%)
  starting transfers between devices  34.5 us (4%)
  between operations  15.9 us (2%)
    pallas_call x2, Pallas kernels, call_group(): pl.pallas_call(functools.partial(group_kernel, count, masks, backward), i...  143 us
    pallas_call x1, Pallas kernels, call_backward(): pl.pallas_call(functools.partial(backward_kernel, count, tokens // 2, hea...  142 us
    dot_general x8, matrix products, dot(): return lax.dot_general(left, right, dims, preferred_element_type=F32)  108 us
    pallas_call x1, Pallas kernels, call_forward(): pl.pallas_call(functools.partial(forward_kernel, count, tokens // 2, head...  92.7 us
    pallas_call x1, Pallas kernels, gather_rows(): pl.pallas_call(functools.partial(gather_kernel, count, tokens), in_specs=...  84.4 us
    pallas_call x1, Pallas kernels, call_hidden(): pl.pallas_call(functools.partial(hidden_kernel, count, masks), in_specs=[...  65.2 us
    ppermute x22, waiting for transfers between devices, swap(): return lax.ppermute(value, both, [(i, i ^ mask) for i in range(devices)])  43.9 us
    unnamed x144, local copies, waits for them, and re-layouts  21.2 us
  transfers between devices with their start and end apart: 32, of which 13 were waited for; matrix products, arithmetic and copies ran while one was open for 21% of the time, Pallas kernels for 52%

profile of v2, /device:TPU:0, one launch (start us, length us, event | category | flops | bytes accessed | tf_op | source)
XLA Modules:
  0.0 876.1 jit_solution(15166315034951151504)
XLA Ops:
  12.5 3.9 collective-permute-start.3
  17.2 5.2 collective-permute-done.3
  22.3 3.6 collective-permute-done.4
  32.0 3.4 pad_maximum_fusion.1
  35.5 2.7 reshape.622
  41.8 3.6 copy.95
  46.7 5.0 add_convert_fusion.2.own_ref
  55.1 84.4 %gather_rows.1.rows_ref = bf16[3,1024,1600]{2,1,0:T(8,128)(2,1)} custom-call(bf16[768,1600]{1,0:T(8,128)(2,1)} %add_convert_fusion.2.own_ref), custom_call_target="tpu_custom_call" | custom-call | bytes 125829120 | tf_op jit(solution)/shard_map/gather_rows/pallas_call | solution.py:106
  141.5 3.0 copy.103
  145.7 6.5 collective-permute-start.6
  152.2 92.7 %attend_forward.1 = (bf16[3,1024,1536]{2,1,0:T(8,128)(2,1)}, bf16[4,768,512]{2,1,0:T(8,128)(2,1)}, f32[3,4,2,1024]{3,2,1,0:T(2,128)S(1)}, bf16[4,3,256,1600]{3,2,1,0:T(8,128)(2,1)}) custom-call(s32[3,8]{1,0:T(4,128)S(1)} %get-tuple-element.197.order_ref, s32[3,8]{1,0:T(4,128)S(1)} %get-tuple-element.198.place_ref, ...), custom_call_target="tpu_custom_call" | custom-call | flops 43285217280 | bytes 83886080 | tf_op jit(solution)/shard_map/attend_forward/pallas_call | solution.py:311
  248.9 5.1 concatenate.36
  253.9 6.6 collective-permute-start.7
  260.5 9.2 %fusion.147 = (f32[768]{0:T(1024)S(1)}, f32[768,1600]{1,0:T(8,128)S(1)}) fusion(f32[1600]{0:T(1024)S(1)} %convert_element_type.161, bf16[1600,1600]{1,0:T(8,128)(2,1)} %all-gather.7.cloned.1.call-done, bf16[768,1792]{1,0:T(8,128)(2,1)} %concatenate.36, f32[3,256,1600]{2,1,0:T(8,128)} %copy.95), kind=kOutput, calls=%fused_computation.277 | convolution fusion | flops 3935845632 | bytes 17917184 | tf_op jit(solution)/shard_map/dot_general | solution.py:26
  275.2 65.2 %hidden_forward.1 = (bf16[3,4,256,1600]{3,2,1,0:T(8,128)(2,1)}, bf16[4,3,256,1600]{3,2,1,0:T(8,128)(2,1)}, bf16[3,4,256,1600]{3,2,1,0:T(8,128)(2,1)}) custom-call(bf16[768,1600]{1,0:T(8,128)(2,1)S(1)} %add_convert_fusion.1.own_ref, bf16[1600,1600]{1,0:T(8,128)(2,1)S(1)} %broadcast_select_fusion.1.weight_ref.refs_3_, f32[1,1600]{1,0:T(1,128)S(1)} %reshape.637.bias_ref), custom_call_target="tpu_custom_call" | custom-call | flops 15728640000 | bytes 104857600 | tf_op jit(solution)/shard_map/hidden_forward/pallas_call | solution.py:702
  340.4 27.1 %bitcast_convert_fusion.refs_4_ = bf16[1600,1600]{1,0:T(8,128)(2,1)} fusion(bf16[4,3,256,1600]{3,2,1,0:T(8,128)(2,1)} %get-tuple-element.43.refs_0_, bf16[4,3,256,1600]{3,2,1,0:T(8,128)(2,1)} %get-tuple-element.39.refs_0_), kind=kOutput, calls=%fused_computation.3 | convolution fusion | flops 15731200000 | bytes 24780800 | tf_op jit(solution)/shard_map/dot_general | solution.py:26
  367.6 3.5 broadcast_select_fusion.refs_2_.refs_1_
  371.1 74.0 %group_backward.1 = (bf16[1600,1600]{1,0:T(8,128)(2,1)}, f32[768,1600]{1,0:T(8,128)}, bf16[3,4,256,1600]{3,2,1,0:T(8,128)(2,1)}) custom-call(bf16[4,3,256,1600]{3,2,1,0:T(8,128)(2,1)} %get-tuple-element.43.refs_0_, bf16[3,4,256,1600]{3,2,1,0:T(8,128)(2,1)} %get-tuple-element.44.refs_1_, bf16[1600,1600]{1,0:T(8,128)(2,1)} %broadcast_select_fusion.refs_2_.refs_1_, ...), custom_call_target="tpu_custom_call" | custom-call | flops 31457280000 | bytes 167772160 | tf_op jit(solution)/shard_map/group_backward/pallas_call | solution.py:862
  445.1 6.6 select_convert_fusion.1
  451.8 5.8 multiply_reduce_fusion
  458.7 3.9 convert_reduce_fusion.2
  462.7 2.2 copy-done.8
  464.9 7.0 convolution_convert_fusion
  473.2 27.5 %convolution_convert_fusion.1.refs_4_ = bf16[1600,1600]{1,0:T(8,128)(2,1)} fusion(bf16[3072,1600]{1,0:T(8,128)(2,1)} %bitcast.147, bf16[3072,1600]{1,0:T(8,128)(2,1)} %bitcast.131), kind=kOutput, calls=%fused_computation.9 | convolution fusion | flops 15731200000 | bytes 24780800 | tf_op jit(solution)/shard_map/dot_general | solution.py:26
  500.7 13.8 %reduce-scatter.13.cloned.1.call-done = bf16[200,1600]{1,0:T(8,128)(2,1)} async-done(((bf16[1600,1600]{1,0:T(8,128)(2,1)}), bf16[200,1600]{1,0:T(8,128)(2,1)}) %reduce-scatter.13.cloned.1.call-update) | async-done | bytes 640016
  514.4 69.3 %group_forward.1 = (bf16[1600,1600]{1,0:T(8,128)(2,1)}, bf16[768,1600]{1,0:T(8,128)(2,1)}) custom-call(bf16[4,3,256,1600]{3,2,1,0:T(8,128)(2,1)} %get-tuple-element.39.refs_0_, bf16[1600,1600]{1,0:T(8,128)(2,1)} %broadcast_select_fusion.refs_2_.refs_1_, f32[768,1600]{1,0:T(8,128)} %copy-done.6, f32[1,1600]{1,0:T(1,128)} %reshape.639.refs_3_, ...), custom_call_target="tpu_custom_call" | custom-call | flops 15728640000 | bytes 167772160 | tf_op jit(solution)/shard_map/group_forward/pallas_call | solution.py:862
  583.8 6.6 select_convert_fusion
  590.5 8.7 convolution_convert_fusion.2
  603.9 142.0 %attend_backward.1 = (bf16[3,1024,1536]{2,1,0:T(8,128)(2,1)}, f32[768,1600]{1,0:T(8,128)}) custom-call(s32[3,8]{1,0:T(4,128)} %copy-done.3, s32[3,8]{1,0:T(4,128)} %copy-done.4, bf16[3,1024,1536]{2,1,0:T(8,128)(2,1)} %get-tuple-element.53.qkv_ref, bf16[4,768,512]{2,1,0:T(8,128)(2,1)} %pad_maximum_fusion.grad_ref, f32[3,4,2,1024]{3,2,1,0:T(2,128)} %copy-done.5, ...), custom_call_target="tpu_custom_call" | custom-call | flops 60196651008 | bytes 83886080 | tf_op jit(solution)/shard_map/attend_backward/pallas_call | solution.py:577
  746.0 22.3 %bitcast_convert_fusion.1 = bf16[1600,1536]{1,0:T(8,128)(2,1)} fusion(bf16[3,1024,1600]{2,1,0:T(8,128)(2,1)} %gather_rows.1.rows_ref, bf16[3,1024,1536]{2,1,0:T(8,128)(2,1)} %get-tuple-element.57), kind=kOutput, calls=%fused_computation.6 | convolution fusion | flops 15101952000 | bytes 24182784 | tf_op jit(solution)/shard_map/dot_general | solution.py:26
  770.4 5.9 convert_reduce_fusion
  777.7 3.2 collective-permute-done.19
  781.9 3.2 collective-permute-done.20
  786.5 6.1 collective-permute-done.22
  792.7 7.7 collective-permute-done.23
  806.5 5.2 multiply_reduce_fusion.1
  811.7 5.1 convert_reduce_fusion.1
  818.2 2.8 collective-permute-done.8
  822.0 2.9 collective-permute-done.9
  825.0 6.6 add_convert_fusion
  832.8 2.7 copy.110
  835.7 4.5 copy.109
  841.7 2.6 convert_add_fusion
  846.2 2.3 reshape.633
  848.6 3.6 slice_reduce_fusion.2
  856.7 3.8 collective-permute-done.13
  860.5 3.9 collective-permute-done.14
  864.4 4.4 fusion.5
  (307 shorter events, 63.3 us)
Async XLA Ops:
  7.2 138.5 %all-gather.9.cloned.1.call-start = ((), (), s32[]{:S(2)}) async-start(), calls=%async_computation.6 | async-start | bytes 5990400 | tf_op jit(solution)/shard_map/all_gather | solution.py:1044
  7.9 144.2 %all-gather.5.cloned.1.call-start = ((), (), s32[]{:S(2)}) async-start(), calls=%async_computation.4 | async-start | bytes 5529600 | tf_op jit(solution)/shard_map/all_gather | solution.py:1013
  11.6 30.2 %copy-start.7 = (bf16[3,256,1600]{1,2,0:T(8,128)(2,1)S(1)}, bf16[3,256,1600]{1,2,0:T(8,128)(2,1)}, u32[]{:S(2)}) copy-start(bf16[3,256,1600]{1,2,0:T(8,128)(2,1)} %param.15) | copy-start | bytes 7372804
  12.5 9.8 %collective-permute-start.3 = (bf16[200,512]{1,0:T(8,128)(2,1)S(1)}, bf16[200,512]{1,0:T(8,128)(2,1)S(1)}, u32[]{:S(2)}, u32[]{:S(2)}) collective-permute-start(bf16[200,512]{1,0:T(8,128)(2,1)S(1)} %get-tuple-element.158), channel_id=1, source_target_pairs={{0,3},{1,2},{2,1},{3,0},{4,7},{5,6},{6,5},{7,4},{8,11},{9,10},{10,... | collective-permute-start | bytes 614408 | tf_op jit(solution)/shard_map/ppermute | solution.py:936
  16.4 9.6 %collective-permute-start.4 = (bf16[200,512]{1,0:T(8,128)(2,1)S(1)}, bf16[200,512]{1,0:T(8,128)(2,1)}, u32[]{:S(2)}, u32[]{:S(2)}) collective-permute-start(bf16[200,512]{1,0:T(8,128)(2,1)S(1)} %get-tuple-element.157), channel_id=1, source_target_pairs={{0,2},{1,3},{2,0},{3,1},{4,6},{5,7},{6,4},{7,5},{8,10},{9,11},{10,... | collective-permute-start | bytes 614408 | tf_op jit(solution)/shard_map/ppermute | solution.py:936
  16.9 9.4 %collective-permute-start.5 = (bf16[200,512]{1,0:T(8,128)(2,1)S(1)}, bf16[200,512]{1,0:T(8,128)(2,1)}, u32[]{:S(2)}, u32[]{:S(2)}) collective-permute-start(bf16[200,512]{1,0:T(8,128)(2,1)S(1)} %get-tuple-element.156), channel_id=1, source_target_pairs={{0,1},{1,0},{2,3},{3,2},{4,5},{5,4},{6,7},{7,6},{8,9},{9,8},{10,11... | collective-permute-start | bytes 614408 | tf_op jit(solution)/shard_map/ppermute | solution.py:936
  17.0 28.4 %copy-start.44 = (pred[512]{0:T(512)(128)(4,1)}, pred[512]{0:T(512)(128)(4,1)S(1)}, u32[]{:S(2)}) copy-start(pred[512]{0:T(512)(128)(4,1)S(1)} %get-tuple-element.183) | copy-start | bytes 1540
  38.2 215.7 %all-gather.11.cloned.1.call-start = ((), (), s32[]{:S(2)}) async-start(), calls=%async_computation.7 | async-start | bytes 5990400 | tf_op jit(solution)/shard_map/all_gather | solution.py:1044
  38.3 13.4 %collective-permute-start = (bf16[200,400]{1,0:T(8,128)(2,1)}, bf16[200,400]{1,0:T(8,128)(2,1)S(1)}, u32[]{:S(2)}, u32[]{:S(2)}) collective-permute-start(bf16[200,400]{1,0:T(8,128)(2,1)} %param.21), channel_id=1, source_target_pairs={{0,3},{1,2},{2,1},{3,0},{4,7},{5,6},{6,5},{7,4},{8,11},{9,10},{10,... | collective-permute-start | bytes 480008 | tf_op jit(solution)/shard_map/ppermute | solution.py:936
  39.8 11.9 %collective-permute-start.1 = (bf16[200,400]{1,0:T(8,128)(2,1)}, bf16[200,400]{1,0:T(8,128)(2,1)S(1)}, u32[]{:S(2)}, u32[]{:S(2)}) collective-permute-start(bf16[200,400]{1,0:T(8,128)(2,1)} %param.21), channel_id=1, source_target_pairs={{0,2},{1,3},{2,0},{3,1},{4,6},{5,7},{6,4},{7,5},{8,10},{9,11},{10,... | collective-permute-start | bytes 480008 | tf_op jit(solution)/shard_map/ppermute | solution.py:936
  41.3 11.1 %collective-permute-start.2 = (bf16[200,400]{1,0:T(8,128)(2,1)}, bf16[200,400]{1,0:T(8,128)(2,1)}, u32[]{:S(2)}, u32[]{:S(2)}) collective-permute-start(bf16[200,400]{1,0:T(8,128)(2,1)} %param.21), channel_id=1, source_target_pairs={{0,1},{1,0},{2,3},{3,2},{4,5},{5,4},{6,7},{7,6},{8,9},{9,8},{10,11... | collective-permute-start | bytes 480008 | tf_op jit(solution)/shard_map/ppermute | solution.py:936
  55.1 85.1 %copy-start.31 = (s32[3,1024]{1,0:T(4,128)S(1)}, s32[3,1024]{1,0:T(4,128)}, u32[]{:S(2)}) copy-start(s32[3,1024]{1,0:T(4,128)} %param.16) | copy-start | bytes 36868
  55.1 86.1 %copy-start.30 = (bf16[2,1600]{1,0:T(2,128)(2,1)S(1)}, bf16[2,1600]{1,0:T(2,128)(2,1)}, u32[]{:S(2)}) copy-start(bf16[2,1600]{1,0:T(2,128)(2,1)} %param.20) | copy-start | bytes 19204
  55.1 86.4 %copy-start.11 = (bf16[3,256,1600]{1,2,0:T(8,128)(2,1)S(1)}, bf16[3,256,1600]{1,2,0:T(8,128)(2,1)}, u32[]{:S(2)}) copy-start(bf16[3,256,1600]{1,2,0:T(8,128)(2,1)} %param.29) | copy-start | bytes 7372804
  139.6 121.0 %all-gather.7.cloned.1.call-start = ((), (), s32[]{:S(2)}) async-start(), calls=%async_computation.5 | async-start | bytes 5990400 | tf_op jit(solution)/shard_map/all_gather | solution.py:1044
  140.1 374.3 %reduce-scatter.13.cloned.1.call-start = ((), (), s32[]{:S(2)}) async-start(), calls=%async_computation.9 | async-start | bytes 5990400
  145.7 99.2 %copy-start.3 = (s32[3,8]{1,0:T(4,128)}, s32[3,8]{1,0:T(4,128)S(1)}, u32[]{:S(2)}) copy-start(s32[3,8]{1,0:T(4,128)S(1)} %get-tuple-element.197.order_ref) | copy-start | bytes 292
  145.7 99.2 %copy-start.4 = (s32[3,8]{1,0:T(4,128)}, s32[3,8]{1,0:T(4,128)S(1)}, u32[]{:S(2)}) copy-start(s32[3,8]{1,0:T(4,128)S(1)} %get-tuple-element.198.place_ref) | copy-start | bytes 292
  145.7 126.6 %collective-permute-start.6 = (bf16[1600,1600]{1,0:T(8,128)(2,1)}, bf16[1600,1600]{1,0:T(8,128)(2,1)}, u32[]{:S(2)}, u32[]{:S(2)}) collective-permute-start(bf16[1600,1600]{1,0:T(8,128)(2,1)} %all-gather.9.cloned.1.call-done), channel_id=1, source_target_pairs={{0,2},{1,3},{6,4},{7,5},{8,10},{9,11},{14,12},{15,13},{16,18},{17,... | collective-permute-start | bytes 15360008 | tf_op jit(solution)/shard_map/ppermute | solution.py:1047
  253.9 113.6 %collective-permute-start.7 = (bf16[1600,1600]{1,0:T(8,128)(2,1)}, bf16[1600,1600]{1,0:T(8,128)(2,1)}, u32[]{:S(2)}, u32[]{:S(2)}) collective-permute-start(bf16[1600,1600]{1,0:T(8,128)(2,1)} %all-gather.11.cloned.1.call-done), channel_id=1, source_target_pairs={{0,2},{1,3},{6,4},{7,5},{8,10},{9,11},{14,12},{15,13},{16,18},{17,... | collective-permute-start | bytes 15360008 | tf_op jit(solution)/shard_map/ppermute | solution.py:1047
  275.1 65.3 %copy-start.2 = (bf16[1600,1600]{1,0:T(8,128)(2,1)}, bf16[1600,1600]{1,0:T(8,128)(2,1)S(1)}, u32[]{:S(2)}) copy-start(bf16[1600,1600]{1,0:T(8,128)(2,1)S(1)} %broadcast_select_fusion.1.weight_ref.refs_3_) | copy-start | bytes 15360004
  275.1 92.4 %slice-start.4 = ((s8[5324800]{0:T(1024)(128)(4,1)}), s8[1130496]{0:T(1024)(128)(4,1)S(1)}, s32[]{:S(2)}) async-start(s8[5324800]{0:T(1024)(128)(4,1)} %bitcast.134), calls=%async_computation.16 | async-start | bytes 2260992
  367.5 77.6 %slice-start.6 = ((s8[5324800]{0:T(1024)(128)(4,1)}), s8[1130496]{0:T(1024)(128)(4,1)S(1)}, s32[]{:S(2)}) async-start(s8[5324800]{0:T(1024)(128)(4,1)} %bitcast.136), calls=%async_computation.18 | async-start | bytes 2260992
  371.1 74.0 %slice-start.7 = ((s8[5324800]{0:T(1024)(128)(4,1)}), s8[4194304]{0:T(1024)(128)(4,1)S(1)}, s32[]{:S(2)}) async-start(s8[5324800]{0:T(1024)(128)(4,1)} %bitcast.136), calls=%async_computation.19 | async-start | bytes 8388608
  451.7 152.2 %reduce-scatter.15.cloned.1.call-start = ((), (), s32[]{:S(2)}) async-start(), calls=%async_computation.10 | async-start | bytes 5990400
  471.9 274.0 %reduce-scatter.17.cloned.1.call-start = ((), (), s32[]{:S(2)}) async-start(), calls=%async_computation.11 | async-start | bytes 5990400
  514.4 69.3 %copy-start.14 = (bf16[1600,1600]{1,0:T(8,128)(2,1)S(1)}, bf16[1600,1600]{1,0:T(8,128)(2,1)}, u32[]{:S(2)}) copy-start(bf16[1600,1600]{1,0:T(8,128)(2,1)} %convolution_convert_fusion.1.refs_4_) | copy-start | bytes 15360004
  590.4 255.8 %reduce-scatter.11.cloned.1.call-start = ((), (), s32[]{:S(2)}) async-start(), calls=%async_computation.8 | async-start | bytes 5529600 | tf_op jit(solution)/shard_map/reduce_scatter | solution.py:1156
  770.3 31.4 %copy-start.13 = (bf16[200,1600]{1,0:T(8,128)(2,1)S(1)}, bf16[200,1600]{1,0:T(8,128)(2,1)}, u32[]{:S(2)}) copy-start(bf16[200,1600]{1,0:T(8,128)(2,1)} %reduce-scatter.15.cloned.1.call-done) | copy-start | bytes 1920004
  770.4 36.1 %copy-start.23 = (f32[1600]{0:T(1024)S(1)}, f32[1600]{0:T(1024)}, u32[]{:S(2)}) copy-start(f32[1600]{0:T(1024)} %copy-done.22) | copy-start | bytes 19204
  770.4 36.1 %copy-start.25 = (f32[768]{0:T(1024)S(1)}, f32[768]{0:T(1024)}, u32[]{:S(2)}) copy-start(f32[768]{0:T(1024)} %copy-done.24) | copy-start | bytes 9220
  770.4 36.1 %copy-start.27 = (f32[768]{0:T(1024)S(1)}, f32[768]{0:T(1024)}, u32[]{:S(2)}) copy-start(f32[768]{0:T(1024)} %copy-done.26) | copy-start | bytes 9220
  776.8 4.1 collective-permute-start.19
  780.9 4.2 collective-permute-start.20
  785.1 1.3 collective-permute-start.21
  786.4 6.2 collective-permute-start.22
  792.6 7.8 collective-permute-start.23
  802.0 39.7 %collective-permute-start.16 = (bf16[200,400]{1,0:T(8,128)(2,1)S(1)}, bf16[200,400]{1,0:T(8,128)(2,1)S(1)}, u32[]{:S(2)}, u32[]{:S(2)}) collective-permute-start(bf16[200,400]{1,0:T(8,128)(2,1)S(1)} %get-tuple-element.163), channel_id=1, source_target_pairs={{0,1},{1,0},{2,3},{3,2},{4,5},{5,4},{6,7},{7,6},{8,9},{9,8},{10,11... | collective-permute-start | bytes 480008 | tf_op jit(solution)/shard_map/ppermute | solution.py:936
  803.1 38.6 %collective-permute-start.17 = (bf16[200,400]{1,0:T(8,128)(2,1)S(1)}, bf16[200,400]{1,0:T(8,128)(2,1)S(1)}, u32[]{:S(2)}, u32[]{:S(2)}) collective-permute-start(bf16[200,400]{1,0:T(8,128)(2,1)S(1)} %get-tuple-element.164), channel_id=1, source_target_pairs={{0,2},{1,3},{2,0},{3,1},{4,6},{5,7},{6,4},{7,5},{8,10},{9,11},{10,... | collective-permute-start | bytes 480008 | tf_op jit(solution)/shard_map/ppermute | solution.py:936
  805.3 36.5 %collective-permute-start.18 = (bf16[200,400]{1,0:T(8,128)(2,1)}, bf16[200,400]{1,0:T(8,128)(2,1)}, u32[]{:S(2)}, u32[]{:S(2)}) collective-permute-start(bf16[200,400]{1,0:T(8,128)(2,1)} %select_select_fusion.4), channel_id=1, source_target_pairs={{0,3},{1,2},{2,1},{3,0},{4,7},{5,6},{6,5},{7,4},{8,11},{9,10},{10,... | collective-permute-start | bytes 480008 | tf_op jit(solution)/shard_map/ppermute | solution.py:936
  817.1 3.9 collective-permute-start.8
  821.0 3.9 collective-permute-start.9
  824.9 6.7 collective-permute-start.10
  831.6 8.5 collective-permute-start.11
  840.1 5.4 collective-permute-start.12
  852.5 8.0 collective-permute-start.13
  853.5 11.0 %collective-permute-start.14 = (bf16[200,512]{1,0:T(8,128)(2,1)S(1)}, bf16[200,512]{1,0:T(8,128)(2,1)S(1)}, u32[]{:S(2)}, u32[]{:S(2)}) collective-permute-start(bf16[200,512]{1,0:T(8,128)(2,1)S(1)} %get-tuple-element.167), channel_id=1, source_target_pairs={{0,2},{1,3},{2,0},{3,1},{4,6},{5,7},{6,4},{7,5},{8,10},{9,11},{10,... | collective-permute-start | bytes 614408 | tf_op jit(solution)/shard_map/ppermute | solution.py:936
  854.8 9.6 %collective-permute-start.15 = (bf16[200,512]{1,0:T(8,128)(2,1)S(1)}, bf16[200,512]{1,0:T(8,128)(2,1)S(1)}, u32[]{:S(2)}, u32[]{:S(2)}) collective-permute-start(bf16[200,512]{1,0:T(8,128)(2,1)S(1)} %get-tuple-element.166), channel_id=1, source_target_pairs={{0,3},{1,2},{2,1},{3,0},{4,7},{5,6},{6,5},{7,4},{8,11},{9,10},{10,... | collective-permute-start | bytes 614408 | tf_op jit(solution)/shard_map/ppermute | solution.py:936
  (54 other events, 683.5 us)
Sparse Core Ops, SparseCore 0:
  9.7 59.4 all-gather.8
  71.3 52.0 all-gather.4
  139.7 57.2 all-gather.10
  199.0 55.4 all-gather.6
  451.9 62.5 reduce-scatter.12
  516.6 60.0 reduce-scatter.14
  590.6 59.1 reduce-scatter.16
  768.4 56.9 reduce-scatter.10

commit v3 on v2

--- a/solution.py
+++ b/solution.py
@@ -48,6 +48,18 @@
         device_id=peer_id(count, mask),
         device_id_type=pl.DeviceIdType.MESH,
     )
+
+
+def block_stays(count):
+    return lax.rem(lax.axis_index("seq"), 2) == lax.axis_index("tp") // (count // 2)
+
+
+def pass_block(count, source, target, sems):
+    return remote(count, source, target, sems.at[0], sems.at[1], count // 2)
+
+
+def when(condition, action):
+    pl.when(condition)(action)
 
 
 def gather_kernel(count, tokens, own_ref, rows_ref, send_sems, recv_sems, local_sems):
@@ -160,10 +172,12 @@
     weight_ref,
     bias_ref,
     grad_ref,
+    block_ref,
     qkv_ref,
     mixed_ref,
     lse_ref,
     group_ref,
+    other_ref,
     rows,
     projected,
     outgoing,
@@ -176,7 +190,9 @@
     group_send,
     group_recv,
     local_sems,
+    block_sems,
 ):
+    stays = block_stays(count)
     chunks, length, _ = rows.shape
     pairs = weight_ref.shape[1] // (3 * LANES)
     tokens = 2 * span
@@ -218,6 +234,7 @@
     for c in range(chunks):
         load_rows(c).start()
     meet(count, tuple(range(1, count)) + (count,))
+    when(stays, lambda: pass_block(count, block_ref, other_ref, block_sems).start())
     for c in range(chunks):
         keep_grad(c).start()
         for d in range(1, pieces):
@@ -302,21 +319,24 @@
             outward(c, r).wait()
     for c in range(max(chunks - 2, 0), chunks):
         save_qkv(c).wait()
-
-
-def call_forward(order, place, rows, weight, bias, grad, count, heads, masks):
+    when(stays, lambda: pass_block(count, block_ref, other_ref, block_sems).wait_send())
+    when(jnp.logical_not(stays), lambda: pass_block(count, block_ref, other_ref, block_sems).wait_recv())
+
+
+def call_forward(order, place, rows, weight, bias, grad, block, count, heads, masks):
     chunks, length, width = rows.shape
     columns = weight.shape[1]
     pairs, tokens, pieces = columns // (3 * LANES), length // count, 1 << len(masks)
     return pl.pallas_call(
         functools.partial(forward_kernel, count, tokens // 2, heads % 2 == 1, masks),
-        in_specs=[SMEM, SMEM, FAR, VMEM, VMEM, FAR],
-        out_specs=[FAR, FAR, VMEM, FAR],
+        in_specs=[SMEM, SMEM, FAR, VMEM, VMEM, FAR, FAR],
+        out_specs=[FAR, FAR, VMEM, FAR, FAR],
         out_shape=[
             jax.ShapeDtypeStruct((chunks, length, columns), BF16),
             jax.ShapeDtypeStruct((count, chunks * tokens, pairs * LANES), BF16),
             jax.ShapeDtypeStruct((chunks, pairs, 2, length), F32),
             jax.ShapeDtypeStruct((pieces, chunks, tokens, width), BF16),
+            jax.ShapeDtypeStruct(block.shape, BF16),
         ],
         scratch_shapes=[
             pltpu.VMEM((chunks, length, width), BF16),
@@ -326,7 +346,7 @@
         + [pltpu.VMEM((length, LANES), BF16)] * 4
         + [pltpu.SemaphoreType.DMA((chunks, count))] * 2
         + [pltpu.SemaphoreType.DMA((chunks, pieces))] * 2
-        + [pltpu.SemaphoreType.DMA((4, chunks))],
+        + [pltpu.SemaphoreType.DMA((4, chunks)), pltpu.SemaphoreType.DMA((2,))],
         compiler_params=pltpu.CompilerParams(
             collective_id=2, has_side_effects=True, vmem_limit_bytes=52 * MIB
         ),
@@ -336,7 +356,7 @@
             transcendentals=chunks * heads * length * length,
         ),
         name="attend_forward",
-    )(order, place, rows, weight, bias, grad)
+    )(order, place, rows, weight, bias, grad, block)
 
 
 def backward_kernel(
@@ -621,10 +641,19 @@
     return u * half, slope
 
 
+def load_block(stays, whole_ref, other_ref, weight, sem, start):
+    if start:
+        when(stays, lambda: pltpu.make_async_copy(whole_ref, weight, sem).start())
+        when(jnp.logical_not(stays), lambda: pltpu.make_async_copy(other_ref, weight, sem).start())
+    else:
+        pltpu.make_async_copy(whole_ref, weight, sem).wait()
+
+
 def hidden_kernel(
-    count, masks, own_ref, weight_ref, bias_ref, rows_ref, value_ref, slope_ref, rows, staged,
-    group_send, group_recv, local_sems, save_sems,
+    count, masks, own_ref, whole_ref, other_ref, bias_ref, block_ref, rows_ref, value_ref, slope_ref, moved_ref,
+    rows, staged, weight, group_send, group_recv, local_sems, save_sems, weight_sem, block_sems,
 ):
+    stays = block_stays(count)
     chunks, pieces, tokens, width = rows.shape
 
     def keep(c):
@@ -644,13 +673,16 @@
         target = value_ref.at[p, c] if part == 0 else slope_ref.at[c, p]
         return pltpu.make_async_copy(staged.at[n % 2, part], target, save_sems.at[n % 2, part])
 
+    load_block(stays, whole_ref, other_ref, weight, weight_sem.at[0], True)
     for c in range(chunks):
         keep(c).start()
-    meet(count, masks)
+    meet(count, masks + (count // 2,))
     for c in range(chunks):
         grouped(c, 1).start()
     for c in range(chunks):
         grouped(c, 2).start()
+    when(stays, lambda: pass_block(count, block_ref, moved_ref, block_sems).start())
+    load_block(stays, whole_ref, other_ref, weight, weight_sem.at[0], False)
 
     @pl.loop(0, chunks)
     def _(c):
@@ -675,7 +707,7 @@
                 grouped(c, 3).wait_recv()
                 save_rows(c).start()
 
-            value, slope = gelu_pair(dot(rows[c, p], weight_ref[...]) + bias_ref[...])
+            value, slope = gelu_pair(dot(rows[c, p], weight[...]) + bias_ref[...])
 
             @pl.when(step >= 2)
             def _():
@@ -694,27 +726,33 @@
     for step in range(chunks * pieces - 2, chunks * pieces):
         for part in range(2):
             save(step, part).wait()
-
-
-def call_hidden(own, weight, bias, chunks, count, masks):
-    width, hidden = weight.shape
+    when(stays, lambda: pass_block(count, block_ref, moved_ref, block_sems).wait_send())
+    when(jnp.logical_not(stays), lambda: pass_block(count, block_ref, moved_ref, block_sems).wait_recv())
+
+
+def call_hidden(own, whole, other, bias, block, chunks, count, masks):
+    width, hidden = whole.shape
     tokens, pieces = own.shape[0] // chunks, 1 << len(masks)
     return pl.pallas_call(
         functools.partial(hidden_kernel, count, masks),
-        in_specs=[FAR, VMEM, VMEM],
-        out_specs=[FAR] * 3,
+        in_specs=[FAR, FAR, FAR, VMEM, FAR],
+        out_specs=[FAR] * 4,
         out_shape=[
             jax.ShapeDtypeStruct((chunks, pieces, tokens, width), BF16),
             jax.ShapeDtypeStruct((pieces, chunks, tokens, hidden), BF16),
             jax.ShapeDtypeStruct((chunks, pieces, tokens, hidden), BF16),
+            jax.ShapeDtypeStruct(block.shape, BF16),
         ],
         scratch_shapes=[
             pltpu.VMEM((chunks, pieces, tokens, width), BF16),
             pltpu.VMEM((2, 2, tokens, hidden), BF16),
+            pltpu.VMEM((width, hidden), BF16),
             pltpu.SemaphoreType.DMA((chunks, pieces)),
             pltpu.SemaphoreType.DMA((chunks, pieces)),
             pltpu.SemaphoreType.DMA((2, chunks)),
             pltpu.SemaphoreType.DMA((2, 2)),
+            pltpu.SemaphoreType.DMA((1,)),
+            pltpu.SemaphoreType.DMA((2,)),
         ],
         compiler_params=pltpu.CompilerParams(
             collective_id=4, has_side_effects=True, vmem_limit_bytes=44 * MIB
@@ -723,23 +761,26 @@
             flops=2 * chunks * pieces * tokens * width * hidden, bytes_accessed=100 * MIB, transcendentals=0
         ),
         name="hidden_forward",
-    )(own, weight, bias)
+    )(own, whole, other, bias, block)
 
 
 def group_kernel(count, masks, backward, *refs):
     if backward:
-        grad_ref, slope_ref, contract_ref, weight_ref, part_ref, other_ref, sum_ref, out_ref, staged = refs[:9]
+        grad_ref, slope_ref, *blocks, part_ref, other_ref, sum_ref, out_ref, staged, contract = refs[:12]
         sources = (grad_ref, slope_ref)
+        targets = (contract, refs[12])
+        scratch = refs[12:]
     else:
-        value_ref, weight_ref, residual_ref, bias_ref, part_ref, other_ref, sum_ref = refs[:7]
+        value_ref, *blocks, residual_ref, bias_ref, part_ref, other_ref, sum_ref = refs[:8]
         sources = (value_ref,)
-    scratch = refs[9:] if backward else refs[7:]
-    loaded, partial, from_core, over, from_side = scratch[:5]
-    core_send, core_recv, side_send, side_recv, cargo_sems, load_sems, save_sems = scratch[5:]
+        targets = (refs[8],)
+        scratch = refs[8:]
+    weight, loaded, partial, from_core, over, from_side = scratch[:6]
+    core_send, core_recv, side_send, side_recv, cargo_sems, load_sems, save_sems, weight_sems = scratch[6:]
     chunks, tokens, _ = over.shape
     steps = 4 * chunks
     high = count // 2
-    stays = lax.rem(lax.axis_index("seq"), 2) == lax.axis_index("tp") // high
+    stays = block_stays(count)
 
     def place(step):
         return lax.rem(step, 2 * chunks) // 2, 3 - step // (2 * chunks) - 2 * lax.rem(step, 2)
@@ -764,15 +805,18 @@
         return remote(count, over.at[c], from_side.at[c], side_send.at[c], side_recv.at[c], masks[0])
 
     def cargo():
-        return remote(count, part_ref, other_ref, cargo_sems.at[0], cargo_sems.at[1], high)
-
+        return pass_block(count, part_ref, other_ref, cargo_sems)
+
+    def load_blocks(start):
+        for n, target in enumerate(targets):
+            load_block(stays, blocks[2 * n], blocks[2 * n + 1], target, weight_sems.at[n], start)
+
+    load_blocks(True)
     for part in range(len(sources)):
         load(0, part).start()
     meet(count, masks + (high,))
-
-    @pl.when(jnp.logical_not(stays))
-    def _():
-        cargo().start()
+    when(jnp.logical_not(stays), lambda: cargo().start())
+    load_blocks(False)
 
     @pl.loop(0, steps)
     def _(step):
@@ -794,7 +838,7 @@
             to_side(before).start()
 
         if backward:
-            hidden = dot(loaded[slot, 0], contract_ref[...]) * loaded[slot, 1].astype(F32)
+            hidden = dot(loaded[slot, 0], contract[...]) * loaded[slot, 1].astype(F32)
             hidden = hidden.astype(BF16)
 
             @pl.when(step >= 2)
@@ -805,7 +849,7 @@
             save(step).start()
         else:
             hidden = loaded[slot, 0]
-        partial[c, p] = dot(hidden, weight_ref[...], NT).astype(BF16)
+        partial[c, p] = dot(hidden, weight[...], NT).astype(BF16)
 
         @pl.when(p >= 2)
         def _():
@@ -827,22 +871,18 @@
         for step in range(steps - 2, steps):
             save(step).wait()
 
-    @pl.when(stays)
-    def _():
-        cargo().wait_recv()
-
-    @pl.when(jnp.logical_not(stays))
-    def _():
-        cargo().wait_send()
-
-
-def call_group(count, masks, backward, tiles, weights, part):
+    when(stays, lambda: cargo().wait_recv())
+    when(jnp.logical_not(stays), lambda: cargo().wait_send())
+
+
+def call_group(count, masks, backward, tiles, blocks, rest, part):
     pieces, chunks, tokens, width = tiles[0].shape
     outs = [
         jax.ShapeDtypeStruct(part.shape, BF16),
         jax.ShapeDtypeStruct((chunks * tokens, width), F32 if backward else BF16),
     ]
     scratch = [
+        pltpu.VMEM((width, width), BF16),
         pltpu.VMEM((2, len(tiles), tokens, width), BF16),
         pltpu.VMEM((chunks, pieces, tokens, width), BF16),
         pltpu.VMEM((chunks, 2, tokens, width), BF16),
@@ -855,13 +895,14 @@
         pltpu.SemaphoreType.DMA((2,)),
         pltpu.SemaphoreType.DMA((2, len(tiles))),
         pltpu.SemaphoreType.DMA((2,)),
+        pltpu.SemaphoreType.DMA((2,)),
     ]
     if backward:
         outs.append(jax.ShapeDtypeStruct((chunks, pieces, tokens, width), BF16))
-        scratch = [pltpu.VMEM((2, tokens, width), BF16)] + scratch
+        scratch = [pltpu.VMEM((2, tokens, width), BF16), pltpu.VMEM((width, width), BF16)] + scratch
     return pl.pallas_call(
         functools.partial(group_kernel, count, masks, backward),
-        in_specs=[FAR] * len(tiles) + [VMEM] * len(weights) + [FAR],
+        in_specs=[FAR] * (len(tiles) + len(blocks)) + [VMEM] * len(rest) + [FAR],
         out_specs=[FAR, VMEM] + [FAR] * (len(outs) - 2),
         out_shape=outs,
         scratch_shapes=scratch,
@@ -874,7 +915,7 @@
             transcendentals=0,
         ),
         name="group_backward" if backward else "group_forward",
-    )(*tiles, *weights, part)
+    )(*tiles, *blocks, *rest, part)
 
 
 def statistics(values):
@@ -1009,6 +1050,7 @@
     gain_one, shift_one = ln1_gain.astype(F32), ln1_bias.astype(F32)
     gain_two, shift_two = ln2_gain.astype(F32), ln2_bias.astype(F32)
     normal_own = norm_forward(flat.astype(F32), gain_one, shift_one)
+    packed[-1] = after(packed[-1], normal_own)
     qkv_rows = to_block(packed)
     qkv_weight = lax.all_gather(qkv_rows, "seq", axis=0, tiled=True)
 
@@ -1044,7 +1086,7 @@
         return lax.all_gather(shard, "seq", axis=0, tiled=True)
 
     def take_block(whole):
-        return jnp.where(stays, whole, lax.ppermute(whole, both, send))
+        return lax.ppermute(whole, both, send)
 
     def give_block(partial):
         return lax.ppermute(partial, both, [(b, a) for a, b in send])
@@ -1058,61 +1100,90 @@
     shards = [attention_output_weight] + [swap(attention_output_weight, r) for r in range(1, tp_count)]
     out_row = jnp.concatenate([choose(shards, t ^ a) for a in range(tp_count)], 1)
     normal_one = gather_rows(after(normal_own, out_row, qkv_rows), chunks, tp_count)
-    expand = take_block(gather_seq(expand_weight))
+    expand_whole = gather_seq(expand_weight)
     contract_whole = gather_seq(after(contract_weight.T, normal_one))
     hidden_bias = lax.dynamic_slice_in_dim(expand_bias, block * hidden, hidden).astype(F32)
 
     out_weight = gather_seq(after(out_row, normal_one))
 
-    qkv, heads_out, lse, output_rows = call_forward(
+    qkv, heads_out, lse, output_rows, expand_other = call_forward(
         orders,
         places,
         normal_one,
         qkv_weight,
         qkv_bias.astype(F32).reshape(1, -1),
         cotangent.reshape(-1, width),
+        expand_whole,
         tp_count,
         group_heads,
         masks,
     )
-    contract = take_block(after(contract_whole, heads_out))
     pieces = [heads_out[r, :, :group] for r in range(tp_count)]
     mixed = jnp.concatenate([choose(pieces, t ^ a) for a in range(tp_count)], 1)[:, :width]
     residual = flat.astype(F32) + dot(mixed, out_weight) + attention_output_bias
     normal = norm_forward(residual, gain_two, shift_two)
 
+    def second_norm_back(norm_grad):
+        from_norm, gain_two_grad, shift_two_grad = norm_backward(residual, gain_two, norm_grad)
+        resid_grad = cotangent.reshape(-1, width).astype(F32) + from_norm
+        branch = resid_grad.astype(BF16)
+        head_grad = dot(branch, out_weight, NT).astype(BF16)
+        head_grad = jnp.pad(head_grad, ((0, 0), (0, tp_count * group - width)))
+        pieces = [head_grad[:, a * group : (a + 1) * group] for a in range(tp_count)]
+        pieces = [jnp.pad(choose(pieces, t ^ r), ((0, 0), (0, padded - group))) for r in range(tp_count)]
+        out_part = dot(mixed, branch, TN).astype(BF16)
+        out_grad = sum_seq(out_part)
+        return gain_two_grad, shift_two_grad, resid_grad, branch, jnp.stack(pieces), out_grad
+
     flat_rows = output_rows.reshape(-1, width)
     if tp_count == 4:
-        normal_two, value, slope = call_hidden(
-            normal, expand, hidden_bias.reshape(1, -1), chunks, tp_count, masks
+        normal_two, value, slope, contract_other = call_hidden(
+            normal,
+            expand_whole,
+            expand_other,
+            hidden_bias.reshape(1, -1),
+            contract_whole,
+            chunks,
+            tp_count,
+            masks,
         )
         value = value.reshape(-1, hidden)
         contract_grad = dot(flat_rows, value, TN).astype(BF16)
         other, norm_grad, hidden_grad = call_group(
-            tp_count, masks, True, [output_rows, slope], [contract, expand], contract_grad
+            tp_count,
+            masks,
+            True,
+            [output_rows, slope],
+            [contract_whole, contract_other, expand_whole, expand_other],
+            [],
+            contract_grad,
         )
         contract_grad = keep_block(contract_grad, other)
         proj_weight_grad = sum_seq(contract_grad)
         normal_two, hidden_grad = normal_two.reshape(-1, width), hidden_grad.reshape(-1, hidden)
         expand_grad = dot(normal_two, after(hidden_grad, contract_grad), TN).astype(BF16)
-        expand_grad = after(expand_grad, proj_weight_grad)
+        from_second = second_norm_back(norm_grad)
+        expand_grad = after(expand_grad, proj_weight_grad, from_second[4])
         other, layer_out = call_group(
             tp_count,
             masks,
             False,
             [value.reshape(members, chunks, rows, hidden)],
-            [contract, residual, contract_bias.astype(F32).reshape(1, -1)],
+            [contract_whole, contract_other],
+            [residual, contract_bias.astype(F32).reshape(1, -1)],
             expand_grad,
         )
         expand_grad = keep_block(expand_grad, other)
     else:
+        expand = jnp.where(stays, expand_whole, expand_other)
+        contract = jnp.where(stays, contract_whole, take_block(contract_whole))
         normal_two = jnp.concatenate(gather_ff(normal), 0)
         value, slope = gelu_pair(dot(normal_two, expand) + hidden_bias)
         value = value.astype(BF16)
         contract_grad = dot(flat_rows, value, TN).astype(BF16)
         hidden_grad = (dot(flat_rows, contract) * slope).astype(BF16)
         partial = dot(hidden_grad, expand, NT).astype(BF16).reshape(members, -1, width)
-        norm_grad = sum_ff([partial[d] for d in range(members)]).astype(F32)
+        from_second = second_norm_back(sum_ff([partial[d] for d in range(members)]).astype(F32))
         proj_weight_grad = sum_seq(keep_block(contract_grad, give_block(contract_grad)))
         expand_grad = dot(normal_two, hidden_grad, TN).astype(BF16)
         expand_grad = keep_block(expand_grad, give_block(expand_grad))
@@ -1122,20 +1193,12 @@
     fc_weight_grad = sum_seq(expand_grad)
     hidden_bias_grad = jnp.sum(hidden_grad, 0, dtype=F32)
 
-    from_norm, gain_two_grad, shift_two_grad = norm_backward(residual, gain_two, norm_grad)
-    resid_grad = cotangent.reshape(-1, width).astype(F32) + from_norm
-    branch = resid_grad.astype(BF16)
-    head_grad = dot(branch, out_weight, NT).astype(BF16)
-    head_grad = jnp.pad(head_grad, ((0, 0), (0, tp_count * group - width)))
-    pieces = [head_grad[:, a * group : (a + 1) * group] for a in range(tp_count)]
-    pieces = [jnp.pad(choose(pieces, t ^ r), ((0, 0), (0, padded - group))) for r in range(tp_count)]
-    out_grad = sum_seq(dot(mixed, branch, TN).astype(BF16))
-
+    gain_two_grad, shift_two_grad, resid_grad, branch, head_grads, out_grad = from_second
     qkv_grads, one_grad = call_backward(
         orders,
         places,
         after(qkv, expand_grad, out_grad),
-        jnp.stack(pieces),
+        head_grads,
         lse,
         qkv_weight,
         tp_count,
@@ -1154,10 +1217,6 @@
     input_grad = (resid_grad + from_norm).astype(BF16).reshape(tokens.shape)
 
     summed = lax.psum_scatter(qkv_grad.astype(BF16), "seq", scatter_dimension=0, tiled=True)
-    packed = from_block(summed)
-    packed = [packed[0]] + [swap(packed[r], r) for r in range(1, tp_count)]
-    qkv_weight_grad = dot(jnp.concatenate(packed, 1), pick, NT)
-
     qkv_bias_grad = qkv_bias_grad.reshape(pairs, 3, LANES)
 
     def whole_bias(part):
@@ -1170,10 +1229,24 @@
     )
     out_bias_part = jnp.sum(branch, 0, dtype=F32)
     proj_bias_part = jnp.sum(cotangent, axis=(0, 1), dtype=F32)
-    early = sum_all(
-        jnp.concatenate([gain_two_grad, shift_two_grad, out_bias_part, proj_bias_part, hidden_whole])
+    vector = sum_all(
+        jnp.concatenate(
+            [
+                gain_two_grad,
+                shift_two_grad,
+                out_bias_part,
+                proj_bias_part,
+                gain_one_grad,
+                shift_one_grad,
+                whole_bias(0),
+                whole_bias(2),
+                hidden_whole,
+            ]
+        )
     )
-    late = sum_all(jnp.concatenate([gain_one_grad, shift_one_grad, whole_bias(0), whole_bias(2)]))
+    packed = from_block(after(summed, vector, input_grad))
+    packed = [packed[0]] + [swap(packed[r], r) for r in range(1, tp_count)]
+    qkv_weight_grad = dot(jnp.concatenate(packed, 1), pick, NT)
 
     def part(vector, index):
         return vector[index * width : (index + 1) * width]
@@ -1181,18 +1254,18 @@
     return (
         layer_out.reshape(tokens.shape),
         input_grad,
-        part(late, 0),
-        part(late, 1),
+        part(vector, 4),
+        part(vector, 5),
         qkv_weight_grad,
-        late[2 * width :].reshape(2, width),
+        vector[6 * width : 8 * width].reshape(2, width),
         out_weight_grad,
-        part(early, 2),
-        part(early, 0),
-        part(early, 1),
+        part(vector, 2),
+        part(vector, 0),
+        part(vector, 1),
         fc_weight_grad.astype(F32),
-        early[4 * width :],
+        vector[8 * width :],
         proj_weight_grad.astype(F32).T,
-        part(early, 3),
+        part(vector, 3),
     )
 
 

time: 886 us -> 833 us (0.940)
  waiting for transfers between devices: 59 us -> 33.4 us
  starting transfers between devices: 34.5 us -> 20.5 us
    ppermute x22 -> x17, waiting for transfers between devices: 43.9 us -> 25.8 us  [swap(): return lax.ppermute(value, both, [(i, i ^ mask) for i in range(devices)])]
    unnamed x11, waiting for transfers between devices: 15.1 us -> 0.85 us
    ppermute x2 -> x0, starting transfers between devices: 13 us -> none  [take_block(): return jnp.where(stays, whole, lax.ppermute(whole, both, send))]
    ppermute x22 -> x17, starting transfers between devices: 21.1 us -> 19.8 us  [swap(): return lax.ppermute(value, both, [(i, i ^ mask) for i in range(devices)])]
    unnamed x144 -> x148, local copies, waits for them, and re-layouts: 21.2 us -> 22.2 us
  transfers between devices with their start and end apart: 32 -> 25, of which waited for: 13 -> 10; matrix products, arithmetic and copies ran while one was open for 21% -> 16% of each run, Pallas kernels for 52% -> 48%
where the time goes in v3:
time: 833 us; the launch traced here: 825 us
  Pallas kernels  531 us (64%)
  matrix products  104 us (12%)
  other arithmetic  74.7 us (9%)
  local copies, waits for them, and re-layouts  44.8 us (5%)
  waiting for transfers between devices  33.4 us (4%)
  starting transfers between devices  20.5 us (2%)
  between operations  15.9 us (2%)
    pallas_call x1, Pallas kernels, call_backward(): pl.pallas_call(functools.partial(backward_kernel, count, tokens // 2, hea...  142 us
    pallas_call x2, Pallas kernels, call_group(): pl.pallas_call(functools.partial(group_kernel, count, masks, backward), i...  141 us
    dot_general x8, matrix products, dot(): return lax.dot_general(left, right, dims, preferred_element_type=F32)  104 us
    pallas_call x1, Pallas kernels, call_forward(): pl.pallas_call(functools.partial(forward_kernel, count, tokens // 2, head...  97.4 us
    pallas_call x1, Pallas kernels, gather_rows(): pl.pallas_call(functools.partial(gather_kernel, count, tokens), in_specs=...  85.1 us
    pallas_call x1, Pallas kernels, call_hidden(): pl.pallas_call(functools.partial(hidden_kernel, count, masks), in_specs=[...  65.3 us
    ppermute x17, waiting for transfers between devices, swap(): return lax.ppermute(value, both, [(i, i ^ mask) for i in range(devices)])  25.8 us
    unnamed x148, local copies, waits for them, and re-layouts  22.2 us
  transfers between devices with their start and end apart: 25, of which 10 were waited for; matrix products, arithmetic and copies ran while one was open for 16% of the time, Pallas kernels for 48%

profile of v3, /device:TPU:0, one launch (start us, length us, event | category | flops | bytes accessed | tf_op | source)
XLA Modules:
  0.0 825.0 jit_solution(14782363280062003424)
XLA Ops:
  11.8 3.9 collective-permute-start.3
  16.3 3.6 copy.95
  21.2 4.8 add_convert_fusion.2.own_ref
  31.4 3.0 collective-permute-start
  35.0 5.3 collective-permute-done
  40.4 2.6 collective-permute-done.1
  43.4 1.6 concatenate.29
  45.1 85.1 %gather_rows.1.rows_ref = bf16[3,1024,1600]{2,1,0:T(8,128)(2,1)} custom-call(bf16[768,1600]{1,0:T(8,128)(2,1)} %add_convert_fusion.2.own_ref), custom_call_target="tpu_custom_call" | custom-call | bytes 125829120 | tf_op jit(solution)/shard_map/gather_rows/pallas_call | solution.py:118
  132.1 3.0 copy.103
  136.3 6.7 all-gather.7.cloned.1.call-done.block_ref.whole_ref.refs_4_
  143.0 97.4 %attend_forward.1 = (bf16[3,1024,1536]{2,1,0:T(8,128)(2,1)}, bf16[4,768,512]{2,1,0:T(8,128)(2,1)}, f32[3,4,2,1024]{3,2,1,0:T(2,128)S(1)}, bf16[4,3,256,1600]{3,2,1,0:T(8,128)(2,1)}, bf16[1600,1600]{1,0:T(8,128)(2,1)}) custom-call(s32[3,8]{1,0:T(4,128)S(1)} %get-tuple-element.203.order_ref, s32[3,8]{1,0:T(4,128)S(1)} %get-tuple-element.204.place_ref, ...), custom_call_target="tpu_custom_call" | custom-call | flops 43285217280 | bytes 83886080 | tf_op jit(solution)/shard_map/attend_forward/pallas_call | solution.py:330
  240.5 2.2 select_bitcast_fusion.1
  244.4 5.1 concatenate.33
  249.5 9.2 %fusion.146 = (f32[768]{0:T(1024)S(1)}, f32[768,1600]{1,0:T(8,128)S(1)}) fusion(f32[1600]{0:T(1024)S(1)} %convert_element_type.161, bf16[1600,1600]{1,0:T(8,128)(2,1)} %all-gather.9.cloned.1.call-done, bf16[768,1792]{1,0:T(8,128)(2,1)} %concatenate.33, f32[3,256,1600]{2,1,0:T(8,128)} %copy.95), kind=kOutput, calls=%fused_computation.274 | convolution fusion | flops 3935845632 | bytes 17917184 | tf_op jit(solution)/shard_map/dot_general | solution.py:26
  262.0 65.3 %hidden_forward.1 = (bf16[3,4,256,1600]{3,2,1,0:T(8,128)(2,1)}, bf16[4,3,256,1600]{3,2,1,0:T(8,128)(2,1)}, bf16[3,4,256,1600]{3,2,1,0:T(8,128)(2,1)}, bf16[1600,1600]{1,0:T(8,128)(2,1)S(1)}) custom-call(bf16[768,1600]{1,0:T(8,128)(2,1)S(1)} %add_convert_fusion.1.own_ref, bf16[1600,1600]{1,0:T(8,128)(2,1)} %all-gather.7.cloned.1.call-done.block_ref.whole_ref.refs_4_, ...), custom_call_target="tpu_custom_call" | custom-call | flops 15728640000 | bytes 104857600 | tf_op jit(solution)/shard_map/hidden_forward/pallas_call | solution.py:736
  327.3 28.9 %bitcast_convert_fusion.refs_6_ = bf16[1600,1600]{1,0:T(8,128)(2,1)} fusion(bf16[4,3,256,1600]{3,2,1,0:T(8,128)(2,1)} %get-tuple-element.48.refs_0_, bf16[4,3,256,1600]{3,2,1,0:T(8,128)(2,1)} %get-tuple-element.45.refs_0_), kind=kOutput, calls=%fused_computation.3 | convolution fusion | flops 15731200000 | bytes 24780800 | tf_op jit(solution)/shard_map/dot_general | solution.py:26
  356.2 72.0 %group_backward.1 = (bf16[1600,1600]{1,0:T(8,128)(2,1)}, f32[768,1600]{1,0:T(8,128)}, bf16[3,4,256,1600]{3,2,1,0:T(8,128)(2,1)}) custom-call(bf16[4,3,256,1600]{3,2,1,0:T(8,128)(2,1)} %get-tuple-element.48.refs_0_, bf16[3,4,256,1600]{3,2,1,0:T(8,128)(2,1)} %get-tuple-element.49.refs_1_, ...), custom_call_target="tpu_custom_call" | custom-call | flops 31457280000 | bytes 167772160 | tf_op jit(solution)/shard_map/group_backward/pallas_call | solution.py:903
  428.3 6.6 select_convert_fusion.1
  435.0 5.8 multiply_reduce_fusion.1
  440.8 1.6 copy-done.9
  442.4 4.4 convert_reduce_fusion.2
  446.8 2.2 copy-done.8
  449.0 7.1 convolution_convert_fusion
  457.4 9.3 %convolution_convert_fusion.2 = bf16[768,1600]{1,0:T(8,128)(2,1)S(1)} fusion(bf16[1600,1600]{1,0:T(8,128)(2,1)} %all-gather.9.cloned.1.call-done, f32[768,1600]{1,0:T(8,128)} %copy-done.8), kind=kOutput, calls=%fused_computation.29 | convolution fusion | flops 3934617600 | bytes 12492800 | tf_op jit(solution)/shard_map/dot_general | solution.py:26
  469.7 1.9 pad_maximum_fusion.grad_ref
  473.9 21.8 %convolution_convert_fusion.1.refs_5_ = bf16[1600,1600]{1,0:T(8,128)(2,1)} fusion(bf16[3072,1600]{1,0:T(8,128)(2,1)S(1)} %bitcast.145, bf16[3072,1600]{1,0:T(8,128)(2,1)S(1)} %bitcast.133), kind=kOutput, calls=%fused_computation.9 | convolution fusion | flops 15731200000 | bytes 24780800 | tf_op jit(solution)/shard_map/dot_general | solution.py:26
  495.7 69.3 %group_forward.1 = (bf16[1600,1600]{1,0:T(8,128)(2,1)}, bf16[768,1600]{1,0:T(8,128)(2,1)}) custom-call(bf16[4,3,256,1600]{3,2,1,0:T(8,128)(2,1)} %get-tuple-element.45.refs_0_, bf16[1600,1600]{1,0:T(8,128)(2,1)} %all-gather.11.cloned.1.call-done.block_ref.refs_2_.refs_1_, bf16[1600,1600]{1,0:T(8,128)(2,1)} %copy-done.4, f32[768,1600]{1,0:T(8,128)} %copy-done.6, ...), custom_call_target="tpu_custom_call" | custom-call | flops 15728640000 | bytes 167772160 | tf_op jit(solution)/shard_map/group_forward/pallas_call | solution.py:903
  565.0 6.6 select_convert_fusion
  571.7 142.1 %attend_backward.1 = (bf16[3,1024,1536]{2,1,0:T(8,128)(2,1)}, f32[768,1600]{1,0:T(8,128)}) custom-call(s32[3,8]{1,0:T(4,128)} %copy-done.2, s32[3,8]{1,0:T(4,128)} %copy-done.3, bf16[3,1024,1536]{2,1,0:T(8,128)(2,1)} %get-tuple-element.58.qkv_ref, bf16[4,768,512]{2,1,0:T(8,128)(2,1)} %pad_maximum_fusion.grad_ref, f32[3,4,2,1024]{3,2,1,0:T(2,128)} %copy-done.5, ...), custom_call_target="tpu_custom_call" | custom-call | flops 60196651008 | bytes 83886080 | tf_op jit(solution)/shard_map/attend_backward/pallas_call | solution.py:597
  713.9 22.3 %bitcast_convert_fusion.1 = bf16[1600,1536]{1,0:T(8,128)(2,1)} fusion(bf16[3,1024,1600]{2,1,0:T(8,128)(2,1)} %gather_rows.1.rows_ref, bf16[3,1024,1536]{2,1,0:T(8,128)(2,1)} %get-tuple-element.62), kind=kOutput, calls=%fused_computation.6 | convolution fusion | flops 15101952000 | bytes 24182784 | tf_op jit(solution)/shard_map/dot_general | solution.py:26
  736.2 1.7 copy-done.12
  738.3 5.9 convert_reduce_fusion
  748.4 1.5 collective-permute-start.16
  749.9 5.2 multiply_reduce_fusion
  755.1 5.1 convert_reduce_fusion.1
  761.9 3.2 collective-permute-done.6
  766.6 2.9 collective-permute-done.7
  769.6 6.7 add_convert_fusion
  777.7 2.7 copy.110
  780.5 4.5 copy.109
  785.0 1.7 collective-permute-start.10
  786.7 2.2 convert_add_fusion
  790.1 3.7 collective-permute-done.10
  795.1 2.3 reshape.633
  797.5 3.6 slice_reduce_fusion.2
  805.6 3.8 collective-permute-done.11
  810.5 2.9 collective-permute-done.13
  813.4 4.4 fusion.5
  (287 shorter events, 44.0 us)
Async XLA Ops:
  7.2 129.1 %all-gather.5.cloned.1.call-start = ((), (), s32[]{:S(2)}) async-start(), calls=%async_computation.4 | async-start | bytes 5529600 | tf_op jit(solution)/shard_map/all_gather | solution.py:1055
  11.8 14.3 %collective-permute-start.3 = (bf16[200,512]{1,0:T(8,128)(2,1)S(1)}, bf16[200,512]{1,0:T(8,128)(2,1)S(1)}, u32[]{:S(2)}, u32[]{:S(2)}) collective-permute-start(bf16[200,512]{1,0:T(8,128)(2,1)S(1)} %get-tuple-element.164), channel_id=1, source_target_pairs={{0,3},{1,2},{2,1},{3,0},{4,7},{5,6},{6,5},{7,4},{8,11},{9,10},{10,... | collective-permute-start | bytes 614408 | tf_op jit(solution)/shard_map/ppermute | solution.py:977
  15.7 10.4 %collective-permute-start.4 = (bf16[200,512]{1,0:T(8,128)(2,1)S(1)}, bf16[200,512]{1,0:T(8,128)(2,1)}, u32[]{:S(2)}, u32[]{:S(2)}) collective-permute-start(bf16[200,512]{1,0:T(8,128)(2,1)S(1)} %get-tuple-element.163), channel_id=1, source_target_pairs={{0,2},{1,3},{2,0},{3,1},{4,6},{5,7},{6,4},{7,5},{8,10},{9,11},{10,... | collective-permute-start | bytes 614408 | tf_op jit(solution)/shard_map/ppermute | solution.py:977
  16.2 9.9 %collective-permute-start.5 = (bf16[200,512]{1,0:T(8,128)(2,1)S(1)}, bf16[200,512]{1,0:T(8,128)(2,1)}, u32[]{:S(2)}, u32[]{:S(2)}) collective-permute-start(bf16[200,512]{1,0:T(8,128)(2,1)S(1)} %get-tuple-element.162), channel_id=1, source_target_pairs={{0,1},{1,0},{2,3},{3,2},{4,5},{5,4},{6,7},{7,6},{8,9},{9,8},{10,11... | collective-permute-start | bytes 614408 | tf_op jit(solution)/shard_map/ppermute | solution.py:977
  26.0 19.0 %copy-start.38 = (pred[512]{0:T(512)(128)(4,1)}, pred[512]{0:T(512)(128)(4,1)S(1)}, u32[]{:S(2)}) copy-start(pred[512]{0:T(512)(128)(4,1)S(1)} %get-tuple-element.197) | copy-start | bytes 1540
  26.0 19.0 %copy-start.40 = (pred[512]{0:T(512)(128)(4,1)}, pred[512]{0:T(512)(128)(4,1)S(1)}, u32[]{:S(2)}) copy-start(pred[512]{0:T(512)(128)(4,1)S(1)} %get-tuple-element.198) | copy-start | bytes 1540
  26.0 19.0 %copy-start.42 = (pred[512]{0:T(512)(128)(4,1)}, pred[512]{0:T(512)(128)(4,1)S(1)}, u32[]{:S(2)}) copy-start(pred[512]{0:T(512)(128)(4,1)S(1)} %get-tuple-element.199) | copy-start | bytes 1540
  30.6 112.4 %all-gather.7.cloned.1.call-start = ((), (), s32[]{:S(2)}) async-start(), calls=%async_computation.5 | async-start | bytes 5990400 | tf_op jit(solution)/shard_map/all_gather | solution.py:1086
  31.4 218.2 %all-gather.9.cloned.1.call-start = ((), (), s32[]{:S(2)}) async-start(), calls=%async_computation.6 | async-start | bytes 5990400 | tf_op jit(solution)/shard_map/all_gather | solution.py:1086
  31.4 9.0 %collective-permute-start = (bf16[200,400]{1,0:T(8,128)(2,1)S(1)}, bf16[200,400]{1,0:T(8,128)(2,1)S(1)}, u32[]{:S(2)}, u32[]{:S(2)}) collective-permute-start(bf16[200,400]{1,0:T(8,128)(2,1)S(1)} %copy-done.22), channel_id=1, source_target_pairs={{0,3},{1,2},{2,1},{3,0},{4,7},{5,6},{6,5},{7,4},{8,11},{9,10},{10,... | collective-permute-start | bytes 480008 | tf_op jit(solution)/shard_map/ppermute | solution.py:977
  34.4 8.6 %collective-permute-start.1 = (bf16[200,400]{1,0:T(8,128)(2,1)S(1)}, bf16[200,400]{1,0:T(8,128)(2,1)S(1)}, u32[]{:S(2)}, u32[]{:S(2)}) collective-permute-start(bf16[200,400]{1,0:T(8,128)(2,1)S(1)} %copy-done.22), channel_id=1, source_target_pairs={{0,2},{1,3},{2,0},{3,1},{4,6},{5,7},{6,4},{7,5},{8,10},{9,11},{10,... | collective-permute-start | bytes 480008 | tf_op jit(solution)/shard_map/ppermute | solution.py:977
  34.9 8.4 %collective-permute-start.2 = (bf16[200,400]{1,0:T(8,128)(2,1)S(1)}, bf16[200,400]{1,0:T(8,128)(2,1)S(1)}, u32[]{:S(2)}, u32[]{:S(2)}) collective-permute-start(bf16[200,400]{1,0:T(8,128)(2,1)S(1)} %copy-done.22), channel_id=1, source_target_pairs={{0,1},{1,0},{2,3},{3,2},{4,5},{5,4},{6,7},{7,6},{8,9},{9,8},{10,11... | collective-permute-start | bytes 480008 | tf_op jit(solution)/shard_map/ppermute | solution.py:977
  45.0 85.3 %copy-start.33 = (s32[3,1024]{1,0:T(4,128)S(1)}, s32[3,1024]{1,0:T(4,128)}, u32[]{:S(2)}) copy-start(s32[3,1024]{1,0:T(4,128)} %param.16) | copy-start | bytes 36868
  45.1 86.8 %copy-start.32 = (bf16[2,1600]{1,0:T(2,128)(2,1)S(1)}, bf16[2,1600]{1,0:T(2,128)(2,1)}, u32[]{:S(2)}) copy-start(bf16[2,1600]{1,0:T(2,128)(2,1)} %param.20) | copy-start | bytes 19204
  45.1 87.1 %copy-start.11 = (bf16[3,256,1600]{1,2,0:T(8,128)(2,1)S(1)}, bf16[3,256,1600]{1,2,0:T(8,128)(2,1)}, u32[]{:S(2)}) copy-start(bf16[3,256,1600]{1,2,0:T(8,128)(2,1)} %param.29) | copy-start | bytes 7372804
  130.2 131.7 %all-gather.11.cloned.1.call-start = ((), (), s32[]{:S(2)}) async-start(), calls=%async_computation.7 | async-start | bytes 5990400 | tf_op jit(solution)/shard_map/all_gather | solution.py:1086
  131.3 364.3 %reduce-scatter.13.cloned.1.call-start = ((), (), s32[]{:S(2)}) async-start(), calls=%async_computation.9 | async-start | bytes 5990400
  136.3 104.2 %copy-start.2 = (s32[3,8]{1,0:T(4,128)}, s32[3,8]{1,0:T(4,128)S(1)}, u32[]{:S(2)}) copy-start(s32[3,8]{1,0:T(4,128)S(1)} %get-tuple-element.203.order_ref) | copy-start | bytes 292
  136.3 104.2 %copy-start.3 = (s32[3,8]{1,0:T(4,128)}, s32[3,8]{1,0:T(4,128)S(1)}, u32[]{:S(2)}) copy-start(s32[3,8]{1,0:T(4,128)S(1)} %get-tuple-element.204.place_ref) | copy-start | bytes 292
  327.3 28.9 %copy-start.4 = (bf16[1600,1600]{1,0:T(8,128)(2,1)}, bf16[1600,1600]{1,0:T(8,128)(2,1)S(1)}, u32[]{:S(2)}) copy-start(bf16[1600,1600]{1,0:T(8,128)(2,1)S(1)} %get-tuple-element.46.refs_3_.refs_2_) | copy-start | bytes 15360004
  356.2 72.0 %copy-start.16 = (bf16[1600,1600]{1,0:T(8,128)(2,1)S(1)}, bf16[1600,1600]{1,0:T(8,128)(2,1)}, u32[]{:S(2)}) copy-start(bf16[1600,1600]{1,0:T(8,128)(2,1)} %bitcast_convert_fusion.refs_6_) | copy-start | bytes 15360004
  434.9 136.8 %reduce-scatter.15.cloned.1.call-start = ((), (), s32[]{:S(2)}) async-start(), calls=%async_computation.10 | async-start | bytes 5990400
  456.2 257.7 %reduce-scatter.17.cloned.1.call-start = ((), (), s32[]{:S(2)}) async-start(), calls=%async_computation.11 | async-start | bytes 5990400
  495.7 69.3 %copy-start.15 = (bf16[1600,1600]{1,0:T(8,128)(2,1)S(1)}, bf16[1600,1600]{1,0:T(8,128)(2,1)}, u32[]{:S(2)}) copy-start(bf16[1600,1600]{1,0:T(8,128)(2,1)} %convolution_convert_fusion.1.refs_5_) | copy-start | bytes 15360004
  571.7 223.5 %reduce-scatter.11.cloned.1.call-start = ((), (), s32[]{:S(2)}) async-start(), calls=%async_computation.8 | async-start | bytes 5529600 | tf_op jit(solution)/shard_map/reduce_scatter | solution.py:1219
  745.5 41.2 %collective-permute-start.14 = (bf16[200,400]{1,0:T(8,128)(2,1)}, bf16[200,400]{1,0:T(8,128)(2,1)S(1)}, u32[]{:S(2)}, u32[]{:S(2)}) collective-permute-start(bf16[200,400]{1,0:T(8,128)(2,1)} %get-tuple-element.169), channel_id=1, source_target_pairs={{0,1},{1,0},{2,3},{3,2},{4,5},{5,4},{6,7},{7,6},{8,9},{9,8},{10,11... | collective-permute-start | bytes 480008 | tf_op jit(solution)/shard_map/ppermute | solution.py:977
  746.7 40.0 %collective-permute-start.15 = (bf16[200,400]{1,0:T(8,128)(2,1)S(1)}, bf16[200,400]{1,0:T(8,128)(2,1)S(1)}, u32[]{:S(2)}, u32[]{:S(2)}) collective-permute-start(bf16[200,400]{1,0:T(8,128)(2,1)S(1)} %get-tuple-element.170), channel_id=1, source_target_pairs={{0,2},{1,3},{2,0},{3,1},{4,6},{5,7},{6,4},{7,5},{8,10},{9,11},{10,... | collective-permute-start | bytes 480008 | tf_op jit(solution)/shard_map/ppermute | solution.py:977
  748.4 38.3 %collective-permute-start.16 = (bf16[200,400]{1,0:T(8,128)(2,1)}, bf16[200,400]{1,0:T(8,128)(2,1)}, u32[]{:S(2)}, u32[]{:S(2)}) collective-permute-start(bf16[200,400]{1,0:T(8,128)(2,1)} %select_select_fusion.4), channel_id=1, source_target_pairs={{0,3},{1,2},{2,1},{3,0},{4,7},{5,6},{6,5},{7,4},{8,11},{9,10},{10,... | collective-permute-start | bytes 480008 | tf_op jit(solution)/shard_map/ppermute | solution.py:977
  760.6 4.5 collective-permute-start.6
  765.1 4.5 collective-permute-start.7
  769.6 6.8 collective-permute-start.8
  776.4 8.6 %collective-permute-start.9 = (f32[19200]{0:T(1024)S(1)}, f32[19200]{0:T(1024)S(1)}, u32[]{:S(2)}, u32[]{:S(2)}) collective-permute-start(f32[19200]{0:T(1024)S(1)} %add.551), channel_id=1, source_target_pairs={{0,8},{1,9},{2,10},{3,11},{4,12},{5,13},{6,14},{7,15},{8,0},{9,1},... | collective-permute-start | bytes 230408 | tf_op jit(solution)/shard_map/ppermute | solution.py:977
  780.4 20.7 %copy-start.35 = (pred[512]{0:T(512)(128)(4,1)S(1)}, pred[512]{0:T(512)(128)(4,1)}, u32[]{:S(2)}) copy-start(pred[512]{0:T(512)(128)(4,1)} %copy-done.34) | copy-start | bytes 1540
  780.4 20.7 %copy-start.37 = (pred[512]{0:T(512)(128)(4,1)S(1)}, pred[512]{0:T(512)(128)(4,1)}, u32[]{:S(2)}) copy-start(pred[512]{0:T(512)(128)(4,1)} %copy-done.36) | copy-start | bytes 1540
  780.4 20.7 %copy-start.39 = (pred[512]{0:T(512)(128)(4,1)S(1)}, pred[512]{0:T(512)(128)(4,1)}, u32[]{:S(2)}) copy-start(pred[512]{0:T(512)(128)(4,1)} %copy-done.38) | copy-start | bytes 1540
  780.4 20.7 %copy-start.41 = (pred[512]{0:T(512)(128)(4,1)S(1)}, pred[512]{0:T(512)(128)(4,1)}, u32[]{:S(2)}) copy-start(pred[512]{0:T(512)(128)(4,1)} %copy-done.40) | copy-start | bytes 1540
  780.4 20.7 %copy-start.43 = (pred[512]{0:T(512)(128)(4,1)S(1)}, pred[512]{0:T(512)(128)(4,1)}, u32[]{:S(2)}) copy-start(pred[512]{0:T(512)(128)(4,1)} %copy-done.42) | copy-start | bytes 1540
  780.4 20.7 %copy-start.45 = (pred[512]{0:T(512)(128)(4,1)S(1)}, pred[512]{0:T(512)(128)(4,1)}, u32[]{:S(2)}) copy-start(pred[512]{0:T(512)(128)(4,1)} %copy-done.44) | copy-start | bytes 1540
  780.4 20.7 %copy-start.47 = (pred[512]{0:T(512)(128)(4,1)S(1)}, pred[512]{0:T(512)(128)(4,1)}, u32[]{:S(2)}) copy-start(pred[512]{0:T(512)(128)(4,1)} %copy-done.46) | copy-start | bytes 1540
  780.5 20.7 %copy-start.49 = (pred[512]{0:T(512)(128)(4,1)S(1)}, pred[512]{0:T(512)(128)(4,1)}, u32[]{:S(2)}) copy-start(pred[512]{0:T(512)(128)(4,1)} %copy-done.48) | copy-start | bytes 1540
  780.5 20.7 %copy-start.51 = (pred[512]{0:T(512)(128)(4,1)S(1)}, pred[512]{0:T(512)(128)(4,1)}, u32[]{:S(2)}) copy-start(pred[512]{0:T(512)(128)(4,1)} %copy-done.50) | copy-start | bytes 1540
  780.5 20.7 %copy-start.53 = (pred[512]{0:T(512)(128)(4,1)S(1)}, pred[512]{0:T(512)(128)(4,1)}, u32[]{:S(2)}) copy-start(pred[512]{0:T(512)(128)(4,1)} %copy-done.52) | copy-start | bytes 1540
  780.5 20.7 %copy-start.55 = (pred[512]{0:T(512)(128)(4,1)S(1)}, pred[512]{0:T(512)(128)(4,1)}, u32[]{:S(2)}) copy-start(pred[512]{0:T(512)(128)(4,1)} %copy-done.54) | copy-start | bytes 1540
  780.5 20.7 %copy-start.57 = (pred[512]{0:T(512)(128)(4,1)S(1)}, pred[512]{0:T(512)(128)(4,1)}, u32[]{:S(2)}) copy-start(pred[512]{0:T(512)(128)(4,1)} %copy-done.56) | copy-start | bytes 1540
  785.0 8.8 %collective-permute-start.10 = (f32[19200]{0:T(1024)S(1)}, f32[19200]{0:T(1024)S(1)}, u32[]{:S(2)}, u32[]{:S(2)}) collective-permute-start(f32[19200]{0:T(1024)S(1)} %add.552), channel_id=1, source_target_pairs={{0,16},{1,17},{2,18},{3,19},{4,20},{5,21},{6,22},{7,23},{8,24},{9,... | collective-permute-start | bytes 230408 | tf_op jit(solution)/shard_map/ppermute | solution.py:977
  801.4 8.1 collective-permute-start.11
  802.7 7.7 collective-permute-start.12
  803.9 9.4 %collective-permute-start.13 = (bf16[200,512]{1,0:T(8,128)(2,1)S(1)}, bf16[200,512]{1,0:T(8,128)(2,1)S(1)}, u32[]{:S(2)}, u32[]{:S(2)}) collective-permute-start(bf16[200,512]{1,0:T(8,128)(2,1)S(1)} %get-tuple-element.172), channel_id=1, source_target_pairs={{0,3},{1,2},{2,1},{3,0},{4,7},{5,6},{6,5},{7,4},{8,11},{9,10},{10,... | collective-permute-start | bytes 614408 | tf_op jit(solution)/shard_map/ppermute | solution.py:977
  (49 other events, 306.0 us)
Sparse Core Ops, SparseCore 0:
  30.7 55.0 all-gather.4
  87.5 55.5 all-gather.6
  145.2 55.4 all-gather.8
  202.3 55.4 all-gather.10
  435.0 59.9 reduce-scatter.12
  497.1 60.0 reduce-scatter.14
  571.8 60.0 reduce-scatter.16
  736.3 57.9 reduce-scatter.10

commit v4 on v3

--- a/solution.py
+++ b/solution.py
@@ -369,8 +369,11 @@
     grad_ref,
     lse_ref,
     weight_ref,
+    rows_ref,
     out_ref,
     sum_ref,
+    product_ref,
+    bias_ref,
     arrived,
     block,
     result,
@@ -393,6 +396,12 @@
     second_send,
     second_recv,
     local_sems,
+    left,
+    right,
+    product,
+    rounded_product,
+    tile_sems,
+    product_sem,
 ):
     chunks, length = out_ref.shape[:2]
     pairs = weight_ref.shape[1] // (3 * LANES)
@@ -571,7 +580,64 @@
             near = share(0, 1)
         sum_ref[pl.ds(pl.multiple_of(c * tokens, tokens), tokens), :] = near[:tokens]
 
-    send_sums(chunks - 1)
+    save(chunks - 1).wait()
+    depth, third = left.shape[1], product.shape[1]
+    tiles = length // depth
+    rounds = chunks * tiles
+
+    def load(n, side_index):
+        c, k = lax.rem(n, rounds) // tiles, lax.rem(n, tiles)
+        span_rows = pl.ds(pl.multiple_of(k * depth, depth), depth)
+        slot = lax.rem(n, 2)
+        if side_index == 0:
+            source, target = rows_ref.at[c, span_rows], left.at[slot]
+        else:
+            lanes = pl.ds(pl.multiple_of(n // rounds * third, third), third)
+            source, target = out_ref.at[c, span_rows, lanes], right.at[slot]
+        return pltpu.make_async_copy(source, target, tile_sems.at[slot, side_index])
+
+    def save_product(part):
+        lanes = pl.ds(pl.multiple_of(part * third, third), third)
+        return pltpu.make_async_copy(rounded_product, product_ref.at[:, lanes], product_sem.at[0])
+
+    for side_index in range(2):
+        load(0, side_index).start()
+
+    @pl.loop(0, 3 * rounds)
+    def _(n):
+        slot = lax.rem(n, 2)
+        part = n // rounds
+        lanes = pl.ds(pl.multiple_of(part * third, third), third)
+        for side_index in range(2):
+            load(n, side_index).wait()
+
+        @pl.when(n < 3 * rounds - 1)
+        def _():
+            for side_index in range(2):
+                load(n + 1, side_index).start()
+
+        @pl.when(n == rounds)
+        def _():
+            send_sums(chunks - 1)
+
+        term = dot(left[slot], right[slot], TN)
+        column_sum = jnp.sum(right[slot].astype(F32), 0, keepdims=True)
+
+        @pl.when(lax.rem(n, rounds) == 0)
+        def _():
+            product[...] = term
+            bias_ref[:, lanes] = column_sum
+
+        @pl.when(lax.rem(n, rounds) != 0)
+        def _():
+            product[...] += term
+            bias_ref[:, lanes] += column_sum
+
+        @pl.when(lax.rem(n, rounds) == rounds - 1)
+        def _():
+            when(part >= 1, lambda: save_product(part - 1).wait())
+            rounded_product[...] = product[...].astype(BF16)
+            save_product(part).start()
 
     for c in range(chunks):
         total = sum_ref[c * tokens : (c + 1) * tokens, :]
@@ -586,21 +652,23 @@
             first(c, 1).wait_send()
         for r in range(1, count):
             inward(c, r).wait_send()
-    save(chunks - 1).wait()
-
-
-def call_backward(order, place, qkv, grads, lse, weight, count, heads):
+    save_product(2).wait()
+
+
+def call_backward(order, place, qkv, grads, lse, weight, rows, count, heads):
     chunks, length, columns = qkv.shape
     width = weight.shape[0]
     pairs, tokens = columns // (3 * LANES), length // count
     sides = 2 if count == 4 else count - 1
     return pl.pallas_call(
         functools.partial(backward_kernel, count, tokens // 2, heads % 2 == 1),
-        in_specs=[SMEM, SMEM, FAR, FAR, VMEM, VMEM],
-        out_specs=[FAR, VMEM],
+        in_specs=[SMEM, SMEM, FAR, FAR, VMEM, VMEM, FAR],
+        out_specs=[FAR, VMEM, FAR, VMEM],
         out_shape=[
             jax.ShapeDtypeStruct((chunks, length, columns), BF16),
             jax.ShapeDtypeStruct((chunks * tokens, width), F32),
+            jax.ShapeDtypeStruct((width, columns), BF16),
+            jax.ShapeDtypeStruct((1, columns), F32),
         ],
         scratch_shapes=[
             pltpu.VMEM((chunks, count, tokens, pairs * LANES), BF16),
@@ -619,7 +687,15 @@
         + [pltpu.SemaphoreType.DMA((chunks, count))] * 2
         + [pltpu.SemaphoreType.DMA((chunks, 2))] * 2
         + [pltpu.SemaphoreType.DMA((chunks, sides))] * 2
-        + [pltpu.SemaphoreType.DMA((3, chunks))],
+        + [
+            pltpu.SemaphoreType.DMA((3, chunks)),
+            pltpu.VMEM((2, 2 * tokens, width), BF16),
+            pltpu.VMEM((2, 2 * tokens, columns // 3), BF16),
+            pltpu.VMEM((width, columns // 3), F32),
+            pltpu.VMEM((width, columns // 3), BF16),
+            pltpu.SemaphoreType.DMA((2, 2)),
+            pltpu.SemaphoreType.DMA((1,)),
+        ],
         compiler_params=pltpu.CompilerParams(
             collective_id=3, has_side_effects=True, vmem_limit_bytes=60 * MIB
         ),
@@ -629,7 +705,7 @@
             transcendentals=chunks * heads * length * length,
         ),
         name="attend_backward",
-    )(order, place, qkv, grads, lse, weight)
+    )(order, place, qkv, grads, lse, weight, rows)
 
 
 def gelu_pair(u):
@@ -766,10 +842,10 @@
 
 def group_kernel(count, masks, backward, *refs):
     if backward:
-        grad_ref, slope_ref, *blocks, part_ref, other_ref, sum_ref, out_ref, staged, contract = refs[:12]
+        grad_ref, slope_ref, *blocks, part_ref, other_ref, sum_ref, out_ref, bias_ref, staged, contract = refs[:13]
         sources = (grad_ref, slope_ref)
-        targets = (contract, refs[12])
-        scratch = refs[12:]
+        targets = (contract, refs[13])
+        scratch = refs[13:]
     else:
         value_ref, *blocks, residual_ref, bias_ref, part_ref, other_ref, sum_ref = refs[:8]
         sources = (value_ref,)
@@ -804,6 +880,9 @@
     def to_side(c):
         return remote(count, over.at[c], from_side.at[c], side_send.at[c], side_recv.at[c], masks[0])
 
+    def put_sum(value):
+        bias_ref[...] = value
+
     def cargo():
         return pass_block(count, part_ref, other_ref, cargo_sems)
 
@@ -847,6 +926,9 @@
 
             staged[slot] = hidden
             save(step).start()
+            column_sum = jnp.sum(hidden.astype(F32), 0, keepdims=True)
+            when(step == 0, lambda: put_sum(column_sum))
+            when(step > 0, lambda: put_sum(bias_ref[...] + column_sum))
         else:
             hidden = loaded[slot, 0]
         partial[c, p] = dot(hidden, weight[...], NT).astype(BF16)
@@ -899,11 +981,12 @@
     ]
     if backward:
         outs.append(jax.ShapeDtypeStruct((chunks, pieces, tokens, width), BF16))
+        outs.append(jax.ShapeDtypeStruct((1, width), F32))
         scratch = [pltpu.VMEM((2, tokens, width), BF16), pltpu.VMEM((width, width), BF16)] + scratch
     return pl.pallas_call(
         functools.partial(group_kernel, count, masks, backward),
         in_specs=[FAR] * (len(tiles) + len(blocks)) + [VMEM] * len(rest) + [FAR],
-        out_specs=[FAR, VMEM] + [FAR] * (len(outs) - 2),
+        out_specs=[FAR, VMEM] + ([FAR, VMEM] if backward else []),
         out_shape=outs,
         scratch_shapes=scratch,
         compiler_params=pltpu.CompilerParams(
@@ -1149,7 +1232,7 @@
         )
         value = value.reshape(-1, hidden)
         contract_grad = dot(flat_rows, value, TN).astype(BF16)
-        other, norm_grad, hidden_grad = call_group(
+        other, norm_grad, hidden_grad, hidden_bias_grad = call_group(
             tp_count,
             masks,
             True,
@@ -1163,17 +1246,18 @@
         normal_two, hidden_grad = normal_two.reshape(-1, width), hidden_grad.reshape(-1, hidden)
         expand_grad = dot(normal_two, after(hidden_grad, contract_grad), TN).astype(BF16)
         from_second = second_norm_back(norm_grad)
-        expand_grad = after(expand_grad, proj_weight_grad, from_second[4])
-        other, layer_out = call_group(
-            tp_count,
-            masks,
-            False,
-            [value.reshape(members, chunks, rows, hidden)],
-            [contract_whole, contract_other],
-            [residual, contract_bias.astype(F32).reshape(1, -1)],
-            expand_grad,
-        )
-        expand_grad = keep_block(expand_grad, other)
+
+        def group_forward(expand_grad):
+            return call_group(
+                tp_count,
+                masks,
+                False,
+                [value.reshape(members, chunks, rows, hidden)],
+                [contract_whole, contract_other],
+                [residual, contract_bias.astype(F32).reshape(1, -1)],
+                expand_grad,
+            )
+
     else:
         expand = jnp.where(stays, expand_whole, expand_other)
         contract = jnp.where(stays, contract_whole, take_block(contract_whole))
@@ -1183,40 +1267,47 @@
         contract_grad = dot(flat_rows, value, TN).astype(BF16)
         hidden_grad = (dot(flat_rows, contract) * slope).astype(BF16)
         partial = dot(hidden_grad, expand, NT).astype(BF16).reshape(members, -1, width)
+        hidden_bias_grad = jnp.sum(hidden_grad, 0, dtype=F32)
         from_second = second_norm_back(sum_ff([partial[d] for d in range(members)]).astype(F32))
         proj_weight_grad = sum_seq(keep_block(contract_grad, give_block(contract_grad)))
         expand_grad = dot(normal_two, hidden_grad, TN).astype(BF16)
-        expand_grad = keep_block(expand_grad, give_block(expand_grad))
-        members_value = value.reshape(members, -1, hidden)
-        feed = [dot(members_value[d], contract, NT).astype(BF16) for d in range(members)]
-        layer_out = (residual + sum_ff(feed) + contract_bias).astype(BF16)
-    fc_weight_grad = sum_seq(expand_grad)
-    hidden_bias_grad = jnp.sum(hidden_grad, 0, dtype=F32)
+
+        def group_forward(expand_grad):
+            members_value = value.reshape(members, -1, hidden)
+            feed = [dot(members_value[d], contract, NT).astype(BF16) for d in range(members)]
+            return give_block(expand_grad), (residual + sum_ff(feed) + contract_bias).astype(BF16)
+
 
     gain_two_grad, shift_two_grad, resid_grad, branch, head_grads, out_grad = from_second
-    qkv_grads, one_grad = call_backward(
+    _, one_grad, qkv_grad, qkv_bias_grad = call_backward(
         orders,
         places,
-        after(qkv, expand_grad, out_grad),
+        after(qkv, expand_grad),
         head_grads,
         lse,
         qkv_weight,
+        normal_one,
         tp_count,
         group_heads,
     )
-    qkv_grads = after(qkv_grads, fc_weight_grad)
+    qkv_grad = after(qkv_grad, proj_weight_grad, out_grad)
     out_grad = [out_grad[:, a * (width // tp_count) : (a + 1) * (width // tp_count)] for a in range(tp_count)]
     out_weight_grad = choose(out_grad, t).astype(F32)
     for r in range(1, tp_count):
         out_weight_grad = out_weight_grad + swap(choose(out_grad, t ^ r), r)
 
-    qkv_grads = qkv_grads.reshape(-1, 3 * padded)
-    qkv_grad = dot(normal_one.reshape(-1, width), qkv_grads, TN)
-    qkv_bias_grad = jnp.sum(qkv_grads, 0, dtype=F32)
+
+    summed = lax.psum_scatter(qkv_grad, "seq", scatter_dimension=0, tiled=True)
+    other, layer_out = group_forward(after(expand_grad, qkv_grad))
+    expand_grad = keep_block(expand_grad, after(other, summed))
+    fc_weight_grad = sum_seq(expand_grad)
+
+    packed = from_block(after(summed, expand_grad))
+    one_grad = after(one_grad, packed[-1])
+    packed = [packed[0]] + [swap(packed[r], r) for r in range(1, tp_count)]
+    qkv_weight_grad = dot(jnp.concatenate(packed, 1), pick, NT)
     from_norm, gain_one_grad, shift_one_grad = norm_backward(flat.astype(F32), gain_one, one_grad)
     input_grad = (resid_grad + from_norm).astype(BF16).reshape(tokens.shape)
-
-    summed = lax.psum_scatter(qkv_grad.astype(BF16), "seq", scatter_dimension=0, tiled=True)
     qkv_bias_grad = qkv_bias_grad.reshape(pairs, 3, LANES)
 
     def whole_bias(part):
@@ -1225,7 +1316,7 @@
         return lax.dynamic_update_slice_in_dim(whole, mine, t * group, 0)[:width]
 
     hidden_whole = lax.dynamic_update_slice_in_dim(
-        jnp.zeros(expand_bias.shape, F32), hidden_bias_grad, block * hidden, 0
+        jnp.zeros(expand_bias.shape, F32), hidden_bias_grad.reshape(-1), block * hidden, 0
     )
     out_bias_part = jnp.sum(branch, 0, dtype=F32)
     proj_bias_part = jnp.sum(cotangent, axis=(0, 1), dtype=F32)
@@ -1244,10 +1335,6 @@
             ]
         )
     )
-    packed = from_block(after(summed, vector, input_grad))
-    packed = [packed[0]] + [swap(packed[r], r) for r in range(1, tp_count)]
-    qkv_weight_grad = dot(jnp.concatenate(packed, 1), pick, NT)
-
     def part(vector, index):
         return vector[index * width : (index + 1) * width]
 

time: 833 us -> 799 us (0.959)
  matrix products: 104 us -> 86.7 us
  other arithmetic: 74.7 us -> 66 us
    dot_general x8 -> x7, matrix products: 104 us -> 86.7 us  [dot(): return lax.dot_general(left, right, dims, preferred_element_type=F32)]
    reduce_sum x2 -> x0, other arithmetic: 11 us -> none  [the longest x1 5.93 us: body(): hidden_bias_grad = jnp.sum(hidden_grad, 0, dtype=F32)]
    unnamed x148 -> x134, local copies, waits for them, and re-layouts: 22.2 us -> 17.8 us
  transfers between devices with their start and end apart: 25 -> 25, of which waited for: 10 -> 7; matrix products, arithmetic and copies ran while one was open for 16% -> 16% of each run, Pallas kernels for 48% -> 50%
where the time goes in v4:
time: 799 us; the launch traced here: 790 us
  Pallas kernels  534 us (67%)
  matrix products  86.7 us (11%)
  other arithmetic  66 us (8%)
  local copies, waits for them, and re-layouts  38.6 us (5%)
  waiting for transfers between devices  29.2 us (4%)
  starting transfers between devices  20.1 us (3%)
  between operations  15.7 us (2%)
    pallas_call x1, Pallas kernels, call_backward(): pl.pallas_call(functools.partial(backward_kernel, count, tokens // 2, hea...  146 us
    pallas_call x2, Pallas kernels, call_group(): pl.pallas_call(functools.partial(group_kernel, count, masks, backward), i...  139 us
    pallas_call x1, Pallas kernels, call_forward(): pl.pallas_call(functools.partial(forward_kernel, count, tokens // 2, head...  97.4 us
    dot_general x7, matrix products, dot(): return lax.dot_general(left, right, dims, preferred_element_type=F32)  86.7 us
    pallas_call x1, Pallas kernels, gather_rows(): pl.pallas_call(functools.partial(gather_kernel, count, tokens), in_specs=...  85.1 us
    pallas_call x1, Pallas kernels, call_hidden(): pl.pallas_call(functools.partial(hidden_kernel, count, masks), in_specs=[...  65.3 us
    ppermute x17, waiting for transfers between devices, swap(): return lax.ppermute(value, both, [(i, i ^ mask) for i in range(devices)])  21.3 us
    ppermute x17, starting transfers between devices, swap(): return lax.ppermute(value, both, [(i, i ^ mask) for i in range(devices)])  19.5 us
  transfers between devices with their start and end apart: 25, of which 7 were waited for; matrix products, arithmetic and copies ran while one was open for 16% of the time, Pallas kernels for 50%

profile of v4, /device:TPU:0, one launch (start us, length us, event | category | flops | bytes accessed | tf_op | source)
XLA Modules:
  0.0 789.9 jit_solution(5558072451457455580)
XLA Ops:
  9.5 1.4 fusion.2
  11.8 3.9 collective-permute-start.3
  16.2 3.6 copy.73
  21.2 4.9 add_convert_fusion.2.own_ref
  27.9 1.4 pad_maximum_fusion.1
  31.5 3.0 collective-permute-start
  35.1 5.3 collective-permute-done
  40.5 2.6 collective-permute-done.1
  43.5 1.6 concatenate.29
  45.2 85.1 %gather_rows.1.rows_ref = bf16[3,1024,1600]{2,1,0:T(8,128)(2,1)} custom-call(bf16[768,1600]{1,0:T(8,128)(2,1)} %add_convert_fusion.2.own_ref), custom_call_target="tpu_custom_call" | custom-call | bytes 125829120 | tf_op jit(solution)/shard_map/gather_rows/pallas_call | solution.py:118
  132.0 3.0 copy.81
  136.1 7.0 all-gather.7.cloned.1.call-done.block_ref.whole_ref.refs_4_
  143.1 97.4 %attend_forward.1 = (bf16[3,1024,1536]{2,1,0:T(8,128)(2,1)}, bf16[4,768,512]{2,1,0:T(8,128)(2,1)}, f32[3,4,2,1024]{3,2,1,0:T(2,128)S(1)}, bf16[4,3,256,1600]{3,2,1,0:T(8,128)(2,1)}, bf16[1600,1600]{1,0:T(8,128)(2,1)}) custom-call(s32[3,8]{1,0:T(4,128)S(1)} %get-tuple-element.197.order_ref, s32[3,8]{1,0:T(4,128)S(1)} %get-tuple-element.198.place_ref, ...), custom_call_target="tpu_custom_call" | custom-call | flops 43285217280 | bytes 83886080 | tf_op jit(solution)/shard_map/attend_forward/pallas_call | solution.py:330
  240.6 2.2 select_bitcast_fusion.1
  244.5 5.2 concatenate.33
  249.7 9.2 %fusion.146 = (f32[768]{0:T(1024)S(1)}, f32[768,1600]{1,0:T(8,128)S(1)}) fusion(f32[1600]{0:T(1024)S(1)} %convert_element_type.150, bf16[1600,1600]{1,0:T(8,128)(2,1)} %all-gather.9.cloned.1.call-done, bf16[768,1792]{1,0:T(8,128)(2,1)} %concatenate.33, f32[3,256,1600]{2,1,0:T(8,128)} %copy.73), kind=kOutput, calls=%fused_computation.271 | convolution fusion | flops 3935845632 | bytes 17917184 | tf_op jit(solution)/shard_map/dot_general | solution.py:26
  259.6 1.5 copy-done.6
  262.1 65.3 %hidden_forward.1 = (bf16[3,4,256,1600]{3,2,1,0:T(8,128)(2,1)}, bf16[4,3,256,1600]{3,2,1,0:T(8,128)(2,1)}, bf16[3,4,256,1600]{3,2,1,0:T(8,128)(2,1)}, bf16[1600,1600]{1,0:T(8,128)(2,1)S(1)}) custom-call(bf16[768,1600]{1,0:T(8,128)(2,1)S(1)} %add_convert_fusion.1.own_ref, bf16[1600,1600]{1,0:T(8,128)(2,1)} %all-gather.7.cloned.1.call-done.block_ref.whole_ref.refs_4_, ...), custom_call_target="tpu_custom_call" | custom-call | flops 15728640000 | bytes 104857600 | tf_op jit(solution)/shard_map/hidden_forward/pallas_call | solution.py:812
  327.5 28.9 %bitcast_convert_fusion.refs_6_ = bf16[1600,1600]{1,0:T(8,128)(2,1)} fusion(bf16[4,3,256,1600]{3,2,1,0:T(8,128)(2,1)} %get-tuple-element.52.refs_0_, bf16[4,3,256,1600]{3,2,1,0:T(8,128)(2,1)} %get-tuple-element.49.refs_0_), kind=kOutput, calls=%fused_computation.1 | convolution fusion | flops 15731200000 | bytes 24780800 | tf_op jit(solution)/shard_map/dot_general | solution.py:26
  356.4 72.4 %group_backward.1 = (bf16[1600,1600]{1,0:T(8,128)(2,1)}, f32[768,1600]{1,0:T(8,128)}, bf16[3,4,256,1600]{3,2,1,0:T(8,128)(2,1)}, f32[1,1600]{1,0:T(1,128)}) custom-call(bf16[4,3,256,1600]{3,2,1,0:T(8,128)(2,1)} %get-tuple-element.52.refs_0_, bf16[3,4,256,1600]{3,2,1,0:T(8,128)(2,1)} %get-tuple-element.53.refs_1_, ...), custom_call_target="tpu_custom_call" | custom-call | flops 31457280000 | bytes 167772160 | tf_op jit(solution)/shard_map/group_backward/pallas_call | solution.py:986
  428.9 4.7 multiply_reduce_fusion.1
  433.7 2.2 convert_reduce_fusion
  435.9 2.2 copy-done.8
  438.2 7.1 convolution_convert_fusion
  445.3 8.1 %select_convert_fusion.1 = bf16[1600,1600]{1,0:T(8,128)(2,1)} fusion(bf16[1600,1600]{1,0:T(8,128)(2,1)} %get-tuple-element.55, bf16[1600,1600]{1,0:T(8,128)(2,1)} %bitcast_convert_fusion.refs_6_, pred[]{:T(512)S(6)} %eq.170), kind=kLoop, calls=%fused_computation.3 | loop fusion | flops 12800000 | bytes 15360001 | tf_op jit(solution)/shard_map/convert_element_type | solution.py:1178
  453.5 27.1 %convolution_convert_fusion.1.refs_5_ = bf16[1600,1600]{1,0:T(8,128)(2,1)} fusion(bf16[3072,1600]{1,0:T(8,128)(2,1)} %bitcast.138, bf16[3072,1600]{1,0:T(8,128)(2,1)} %bitcast.139), kind=kOutput, calls=%fused_computation.6 | convolution fusion | flops 15731200000 | bytes 24780800 | tf_op jit(solution)/shard_map/dot_general | solution.py:26
  480.7 8.2 %convolution_convert_fusion.2 = bf16[768,1600]{1,0:T(8,128)(2,1)S(1)} fusion(bf16[1600,1600]{1,0:T(8,128)(2,1)} %all-gather.9.cloned.1.call-done, f32[768,1600]{1,0:T(8,128)S(1)} %bitcast.126), kind=kOutput, calls=%fused_computation.26 | convolution fusion | flops 3934617600 | bytes 12492800 | tf_op jit(solution)/shard_map/dot_general | solution.py:26
  491.7 1.9 pad_maximum_fusion.grad_ref
  493.6 146.4 %attend_backward.1 = (bf16[3,1024,1536]{2,1,0:T(8,128)(2,1)}, f32[768,1600]{1,0:T(8,128)}, bf16[1600,1536]{1,0:T(8,128)(2,1)}, f32[1,1536]{1,0:T(1,128)}) custom-call(s32[3,8]{1,0:T(4,128)} %copy-done.2, s32[3,8]{1,0:T(4,128)} %copy-done.3, bf16[3,1024,1536]{2,1,0:T(8,128)(2,1)} %get-tuple-element.58.qkv_ref, bf16[4,768,512]{2,1,0:T(8,128)(2,1)} %pad_maximum_fusion.grad_ref, ...), custom_call_target="tpu_custom_call" | custom-call | flops 60196651008 | bytes 83886080 | tf_op jit(solution)/shard_map/attend_backward/pallas_call | solution.py:663
  640.8 66.9 %group_forward.1 = (bf16[1600,1600]{1,0:T(8,128)(2,1)}, bf16[768,1600]{1,0:T(8,128)(2,1)}) custom-call(bf16[4,3,256,1600]{3,2,1,0:T(8,128)(2,1)} %get-tuple-element.49.refs_0_, bf16[1600,1600]{1,0:T(8,128)(2,1)} %all-gather.11.cloned.1.call-done.block_ref.refs_2_.refs_1_, bf16[1600,1600]{1,0:T(8,128)(2,1)} %copy-done.4, f32[768,1600]{1,0:T(8,128)} %copy-done.6, ...), custom_call_target="tpu_custom_call" | custom-call | flops 15728640000 | bytes 167772160 | tf_op jit(solution)/shard_map/group_forward/pallas_call | solution.py:986
  707.8 8.1 %select_convert_fusion = bf16[1600,1600]{1,0:T(8,128)(2,1)} fusion(bf16[1600,1600]{1,0:T(8,128)(2,1)} %get-tuple-element.67, bf16[1600,1600]{1,0:T(8,128)(2,1)} %convolution_convert_fusion.1.refs_5_, pred[]{:T(512)S(6)} %eq.170), kind=kLoop, calls=%fused_computation.2 | loop fusion | flops 12800000 | bytes 15360001 | tf_op jit(solution)/shard_map/convert_element_type | solution.py:1178
  715.9 1.7 copy-done.13
  718.6 1.5 select_select_fusion.6
  720.2 3.0 collective-permute-start.14
  723.3 2.2 select_select_fusion.4
  725.5 1.4 collective-permute-start.16
  727.1 4.6 copy.86
  733.3 3.6 slice_reduce_fusion.2
  737.9 5.2 multiply_reduce_fusion
  743.3 2.0 collective-permute-start.6
  746.6 1.5 collective-permute-start.13
  748.2 1.9 collective-permute-start.12
  750.3 9.3 %collective-permute-done.7 = f32[19200]{0:T(1024)S(1)} collective-permute-done((f32[19200]{0:T(1024)S(1)}, f32[19200]{0:T(1024)S(1)}, u32[]{:S(2)}, u32[]{:S(2)}) %collective-permute-start.7) | collective-permute-done | bytes 76832 | tf_op jit(solution)/shard_map/ppermute | solution.py:1060
  761.0 6.5 add_convert_fusion
  767.5 2.7 copy.87
  771.3 4.7 fusion.5
  776.0 2.5 collective-permute-done.10
  780.6 2.2 convert_element_type.173
  (271 shorter events, 29.5 us)
Async XLA Ops:
  7.2 128.9 %all-gather.5.cloned.1.call-start = ((), (), s32[]{:S(2)}) async-start(), calls=%async_computation.4 | async-start | bytes 5529600 | tf_op jit(solution)/shard_map/all_gather | solution.py:1138
  11.8 14.4 %collective-permute-start.3 = (bf16[200,512]{1,0:T(8,128)(2,1)S(1)}, bf16[200,512]{1,0:T(8,128)(2,1)S(1)}, u32[]{:S(2)}, u32[]{:S(2)}) collective-permute-start(bf16[200,512]{1,0:T(8,128)(2,1)S(1)} %get-tuple-element.158), channel_id=1, source_target_pairs={{0,3},{1,2},{2,1},{3,0},{4,7},{5,6},{6,5},{7,4},{8,11},{9,10},{10,... | collective-permute-start | bytes 614408 | tf_op jit(solution)/shard_map/ppermute | solution.py:1060
  15.7 10.5 %collective-permute-start.4 = (bf16[200,512]{1,0:T(8,128)(2,1)S(1)}, bf16[200,512]{1,0:T(8,128)(2,1)}, u32[]{:S(2)}, u32[]{:S(2)}) collective-permute-start(bf16[200,512]{1,0:T(8,128)(2,1)S(1)} %get-tuple-element.157), channel_id=1, source_target_pairs={{0,2},{1,3},{2,0},{3,1},{4,6},{5,7},{6,4},{7,5},{8,10},{9,11},{10,... | collective-permute-start | bytes 614408 | tf_op jit(solution)/shard_map/ppermute | solution.py:1060
  16.2 10.0 %collective-permute-start.5 = (bf16[200,512]{1,0:T(8,128)(2,1)S(1)}, bf16[200,512]{1,0:T(8,128)(2,1)}, u32[]{:S(2)}, u32[]{:S(2)}) collective-permute-start(bf16[200,512]{1,0:T(8,128)(2,1)S(1)} %get-tuple-element.156), channel_id=1, source_target_pairs={{0,1},{1,0},{2,3},{3,2},{4,5},{5,4},{6,7},{7,6},{8,9},{9,8},{10,11... | collective-permute-start | bytes 614408 | tf_op jit(solution)/shard_map/ppermute | solution.py:1060
  26.1 19.0 %copy-start.35 = (pred[512]{0:T(512)(128)(4,1)}, pred[512]{0:T(512)(128)(4,1)S(1)}, u32[]{:S(2)}) copy-start(pred[512]{0:T(512)(128)(4,1)S(1)} %get-tuple-element.191) | copy-start | bytes 1540
  26.1 19.0 %copy-start.37 = (pred[512]{0:T(512)(128)(4,1)}, pred[512]{0:T(512)(128)(4,1)S(1)}, u32[]{:S(2)}) copy-start(pred[512]{0:T(512)(128)(4,1)S(1)} %get-tuple-element.192) | copy-start | bytes 1540
  26.1 19.0 %copy-start.39 = (pred[512]{0:T(512)(128)(4,1)}, pred[512]{0:T(512)(128)(4,1)S(1)}, u32[]{:S(2)}) copy-start(pred[512]{0:T(512)(128)(4,1)S(1)} %get-tuple-element.193) | copy-start | bytes 1540
  26.1 19.0 %copy-start.41 = (pred[512]{0:T(512)(128)(4,1)}, pred[512]{0:T(512)(128)(4,1)S(1)}, u32[]{:S(2)}) copy-start(pred[512]{0:T(512)(128)(4,1)S(1)} %get-tuple-element.194) | copy-start | bytes 1540
  30.7 112.4 %all-gather.7.cloned.1.call-start = ((), (), s32[]{:S(2)}) async-start(), calls=%async_computation.5 | async-start | bytes 5990400 | tf_op jit(solution)/shard_map/all_gather | solution.py:1169
  31.5 218.2 %all-gather.9.cloned.1.call-start = ((), (), s32[]{:S(2)}) async-start(), calls=%async_computation.6 | async-start | bytes 5990400 | tf_op jit(solution)/shard_map/all_gather | solution.py:1169
  31.5 9.0 %collective-permute-start = (bf16[200,400]{1,0:T(8,128)(2,1)S(1)}, bf16[200,400]{1,0:T(8,128)(2,1)S(1)}, u32[]{:S(2)}, u32[]{:S(2)}) collective-permute-start(bf16[200,400]{1,0:T(8,128)(2,1)S(1)} %copy-done.20), channel_id=1, source_target_pairs={{0,3},{1,2},{2,1},{3,0},{4,7},{5,6},{6,5},{7,4},{8,11},{9,10},{10,... | collective-permute-start | bytes 480008 | tf_op jit(solution)/shard_map/ppermute | solution.py:1060
  34.5 8.6 %collective-permute-start.1 = (bf16[200,400]{1,0:T(8,128)(2,1)S(1)}, bf16[200,400]{1,0:T(8,128)(2,1)S(1)}, u32[]{:S(2)}, u32[]{:S(2)}) collective-permute-start(bf16[200,400]{1,0:T(8,128)(2,1)S(1)} %copy-done.20), channel_id=1, source_target_pairs={{0,2},{1,3},{2,0},{3,1},{4,6},{5,7},{6,4},{7,5},{8,10},{9,11},{10,... | collective-permute-start | bytes 480008 | tf_op jit(solution)/shard_map/ppermute | solution.py:1060
  35.0 8.4 %collective-permute-start.2 = (bf16[200,400]{1,0:T(8,128)(2,1)S(1)}, bf16[200,400]{1,0:T(8,128)(2,1)S(1)}, u32[]{:S(2)}, u32[]{:S(2)}) collective-permute-start(bf16[200,400]{1,0:T(8,128)(2,1)S(1)} %copy-done.20), channel_id=1, source_target_pairs={{0,1},{1,0},{2,3},{3,2},{4,5},{5,4},{6,7},{7,6},{8,9},{9,8},{10,11... | collective-permute-start | bytes 480008 | tf_op jit(solution)/shard_map/ppermute | solution.py:1060
  45.1 85.3 %copy-start.28 = (s32[3,1024]{1,0:T(4,128)S(1)}, s32[3,1024]{1,0:T(4,128)}, u32[]{:S(2)}) copy-start(s32[3,1024]{1,0:T(4,128)} %param.16) | copy-start | bytes 36868
  45.2 86.6 %copy-start.27 = (bf16[2,1600]{1,0:T(2,128)(2,1)S(1)}, bf16[2,1600]{1,0:T(2,128)(2,1)}, u32[]{:S(2)}) copy-start(bf16[2,1600]{1,0:T(2,128)(2,1)} %param.20) | copy-start | bytes 19204
  45.2 86.8 %copy-start.12 = (bf16[3,256,1600]{1,2,0:T(8,128)(2,1)S(1)}, bf16[3,256,1600]{1,2,0:T(8,128)(2,1)}, u32[]{:S(2)}) copy-start(bf16[3,256,1600]{1,2,0:T(8,128)(2,1)} %param.29) | copy-start | bytes 7372804
  130.3 131.8 %all-gather.11.cloned.1.call-start = ((), (), s32[]{:S(2)}) async-start(), calls=%async_computation.7 | async-start | bytes 5990400 | tf_op jit(solution)/shard_map/all_gather | solution.py:1169
  131.4 508.6 %reduce-scatter.15.cloned.1.call-start = ((), (), s32[]{:S(2)}) async-start(), calls=%async_computation.10 | async-start | bytes 5990400
  136.1 104.4 %copy-start.2 = (s32[3,8]{1,0:T(4,128)}, s32[3,8]{1,0:T(4,128)S(1)}, u32[]{:S(2)}) copy-start(s32[3,8]{1,0:T(4,128)S(1)} %get-tuple-element.197.order_ref) | copy-start | bytes 292
  136.1 104.5 %copy-start.3 = (s32[3,8]{1,0:T(4,128)}, s32[3,8]{1,0:T(4,128)S(1)}, u32[]{:S(2)}) copy-start(s32[3,8]{1,0:T(4,128)S(1)} %get-tuple-element.198.place_ref) | copy-start | bytes 292
  327.4 29.0 %copy-start.4 = (bf16[1600,1600]{1,0:T(8,128)(2,1)}, bf16[1600,1600]{1,0:T(8,128)(2,1)S(1)}, u32[]{:S(2)}) copy-start(bf16[1600,1600]{1,0:T(8,128)(2,1)S(1)} %get-tuple-element.50.refs_3_.refs_2_) | copy-start | bytes 15360004
  327.5 101.4 %slice-start = ((s8[5111808]{0:T(1024)(128)(4,1)}), s8[4194304]{0:T(1024)(128)(4,1)S(1)}, s32[]{:S(2)}) async-start(s8[5111808]{0:T(1024)(128)(4,1)} %bitcast.123), calls=%async_computation.12 | async-start | bytes 8388608
  356.4 72.5 %slice-start.1 = ((s8[5111808]{0:T(1024)(128)(4,1)}), s8[917504]{0:T(1024)(128)(4,1)S(1)}, s32[]{:S(2)}) async-start(s8[5111808]{0:T(1024)(128)(4,1)} %bitcast.123), calls=%async_computation.13 | async-start | bytes 1835008
  445.3 194.8 %reduce-scatter.13.cloned.1.call-start = ((), (), s32[]{:S(2)}) async-start(), calls=%async_computation.9 | async-start | bytes 5990400
  453.4 27.2 %slice-start.2 = ((s8[5111808]{0:T(1024)(128)(4,1)}), s8[917504]{0:T(1024)(128)(4,1)S(1)}, s32[]{:S(2)}) async-start(s8[5111808]{0:T(1024)(128)(4,1)} %bitcast.125), calls=%async_computation.14 | async-start | bytes 1835008
  453.4 254.3 %reduce-scatter.11.cloned.1.call-start = ((), (), s32[]{:S(2)}) async-start(), calls=%async_computation.8 | async-start | bytes 5529600 | tf_op jit(solution)/shard_map/reduce_scatter | solution.py:1300
  453.5 27.2 %slice-start.3 = ((s8[5111808]{0:T(1024)(128)(4,1)}), s8[4194304]{0:T(1024)(128)(4,1)S(1)}, s32[]{:S(2)}) async-start(s8[5111808]{0:T(1024)(128)(4,1)} %bitcast.125), calls=%async_computation.15 | async-start | bytes 8388608
  493.6 146.6 %copy-start.60 = (bf16[1600]{0:T(1024)(128)(2,1)S(1)}, bf16[1600]{0:T(1024)(128)(2,1)}, u32[]{:S(2)}) copy-start(bf16[1600]{0:T(1024)(128)(2,1)} %param.28) | copy-start | bytes 9604
  640.1 140.5 %reduce-scatter.17.cloned.1.call-start = ((), (), s32[]{:S(2)}) async-start(), calls=%async_computation.11 | async-start | bytes 5990400
  718.0 13.7 %copy-start.18 = (bf16[200,1600]{1,0:T(8,128)(2,1)S(1)}, bf16[200,1600]{1,0:T(8,128)(2,1)}, u32[]{:S(2)}) copy-start(bf16[200,1600]{1,0:T(8,128)(2,1)} %reduce-scatter.13.cloned.1.call-done) | copy-start | bytes 1920004
  718.0 14.9 %copy-start.19 = (bf16[200,1536]{1,0:T(8,128)(2,1)S(1)}, bf16[200,1536]{1,0:T(8,128)(2,1)}, u32[]{:S(2)}) copy-start(bf16[200,1536]{1,0:T(8,128)(2,1)} %reduce-scatter.11.cloned.1.call-done) | copy-start | bytes 1843204
  720.2 25.1 %collective-permute-start.14 = (bf16[200,400]{1,0:T(8,128)(2,1)S(1)}, bf16[200,400]{1,0:T(8,128)(2,1)S(1)}, u32[]{:S(2)}, u32[]{:S(2)}) collective-permute-start(bf16[200,400]{1,0:T(8,128)(2,1)S(1)} %get-tuple-element.163), channel_id=1, source_target_pairs={{0,1},{1,0},{2,3},{3,2},{4,5},{5,4},{6,7},{7,6},{8,9},{9,8},{10,11... | collective-permute-start | bytes 480008 | tf_op jit(solution)/shard_map/ppermute | solution.py:1060
  723.2 22.1 %collective-permute-start.15 = (bf16[200,400]{1,0:T(8,128)(2,1)S(1)}, bf16[200,400]{1,0:T(8,128)(2,1)S(1)}, u32[]{:S(2)}, u32[]{:S(2)}) collective-permute-start(bf16[200,400]{1,0:T(8,128)(2,1)S(1)} %get-tuple-element.164), channel_id=1, source_target_pairs={{0,2},{1,3},{2,0},{3,1},{4,6},{5,7},{6,4},{7,5},{8,10},{9,11},{10,... | collective-permute-start | bytes 480008 | tf_op jit(solution)/shard_map/ppermute | solution.py:1060
  725.5 19.7 %collective-permute-start.16 = (bf16[200,400]{1,0:T(8,128)(2,1)}, bf16[200,400]{1,0:T(8,128)(2,1)S(1)}, u32[]{:S(2)}, u32[]{:S(2)}) collective-permute-start(bf16[200,400]{1,0:T(8,128)(2,1)} %select_select_fusion.4), channel_id=1, source_target_pairs={{0,3},{1,2},{2,1},{3,0},{4,7},{5,6},{6,5},{7,4},{8,11},{9,10},{10,... | collective-permute-start | bytes 480008 | tf_op jit(solution)/shard_map/ppermute | solution.py:1060
  727.0 9.9 %copy-start.40 = (pred[512]{0:T(512)(128)(4,1)S(1)}, pred[512]{0:T(512)(128)(4,1)}, u32[]{:S(2)}) copy-start(pred[512]{0:T(512)(128)(4,1)} %copy-done.39) | copy-start | bytes 1540
  727.0 9.9 %copy-start.42 = (pred[512]{0:T(512)(128)(4,1)S(1)}, pred[512]{0:T(512)(128)(4,1)}, u32[]{:S(2)}) copy-start(pred[512]{0:T(512)(128)(4,1)} %copy-done.41) | copy-start | bytes 1540
  727.0 10.9 %copy-start.22 = (f32[1600]{0:T(1024)S(1)}, f32[1600]{0:T(1024)}, u32[]{:S(2)}) copy-start(f32[1600]{0:T(1024)} %copy-done.21) | copy-start | bytes 19204
  727.1 10.9 %copy-start.24 = (f32[768]{0:T(1024)S(1)}, f32[768]{0:T(1024)}, u32[]{:S(2)}) copy-start(f32[768]{0:T(1024)} %copy-done.23) | copy-start | bytes 9220
  727.1 10.9 %copy-start.26 = (f32[768]{0:T(1024)S(1)}, f32[768]{0:T(1024)}, u32[]{:S(2)}) copy-start(f32[768]{0:T(1024)} %copy-done.25) | copy-start | bytes 9220
  743.3 6.8 collective-permute-start.6
  746.6 24.7 %collective-permute-start.13 = (bf16[200,512]{1,0:T(8,128)(2,1)S(1)}, bf16[200,512]{1,0:T(8,128)(2,1)}, u32[]{:S(2)}, u32[]{:S(2)}) collective-permute-start(bf16[200,512]{1,0:T(8,128)(2,1)S(1)} %get-tuple-element.168), channel_id=1, source_target_pairs={{0,3},{1,2},{2,1},{3,0},{4,7},{5,6},{6,5},{7,4},{8,11},{9,10},{10,... | collective-permute-start | bytes 614408 | tf_op jit(solution)/shard_map/ppermute | solution.py:1060
  748.1 23.2 %collective-permute-start.11 = (bf16[200,512]{1,0:T(8,128)(2,1)}, bf16[200,512]{1,0:T(8,128)(2,1)}, u32[]{:S(2)}, u32[]{:S(2)}) collective-permute-start(bf16[200,512]{1,0:T(8,128)(2,1)} %get-tuple-element.167), channel_id=1, source_target_pairs={{0,1},{1,0},{2,3},{3,2},{4,5},{5,4},{6,7},{7,6},{8,9},{9,8},{10,11... | collective-permute-start | bytes 614408 | tf_op jit(solution)/shard_map/ppermute | solution.py:1060
  748.2 23.1 %collective-permute-start.12 = (bf16[200,512]{1,0:T(8,128)(2,1)}, bf16[200,512]{1,0:T(8,128)(2,1)}, u32[]{:S(2)}, u32[]{:S(2)}) collective-permute-start(bf16[200,512]{1,0:T(8,128)(2,1)} %get-tuple-element.166), channel_id=1, source_target_pairs={{0,2},{1,3},{2,0},{3,1},{4,6},{5,7},{6,4},{7,5},{8,10},{9,11},{10,... | collective-permute-start | bytes 614408 | tf_op jit(solution)/shard_map/ppermute | solution.py:1060
  750.1 9.5 %collective-permute-start.7 = (f32[19200]{0:T(1024)S(1)}, f32[19200]{0:T(1024)S(1)}, u32[]{:S(2)}, u32[]{:S(2)}) collective-permute-start(f32[19200]{0:T(1024)S(1)} %add.549), channel_id=1, source_target_pairs={{0,2},{1,3},{2,0},{3,1},{4,6},{5,7},{6,4},{7,5},{8,10},{9,11},{10,... | collective-permute-start | bytes 230408 | tf_op jit(solution)/shard_map/ppermute | solution.py:1060
  759.6 1.3 collective-permute-start.8
  760.9 9.3 %collective-permute-start.9 = (f32[19200]{0:T(1024)S(1)}, f32[19200]{0:T(1024)S(1)}, u32[]{:S(2)}, u32[]{:S(2)}) collective-permute-start(f32[19200]{0:T(1024)S(1)} %add.551), channel_id=1, source_target_pairs={{0,8},{1,9},{2,10},{3,11},{4,12},{5,13},{6,14},{7,15},{8,0},{9,1},... | collective-permute-start | bytes 230408 | tf_op jit(solution)/shard_map/ppermute | solution.py:1060
  770.3 8.3 %collective-permute-start.10 = (f32[19200]{0:T(1024)S(1)}, f32[19200]{0:T(1024)S(1)}, u32[]{:S(2)}, u32[]{:S(2)}) collective-permute-start(f32[19200]{0:T(1024)S(1)} %add.552), channel_id=1, source_target_pairs={{0,16},{1,17},{2,18},{3,19},{4,20},{5,21},{6,22},{7,23},{8,24},{9,... | collective-permute-start | bytes 230408 | tf_op jit(solution)/shard_map/ppermute | solution.py:1060
  771.3 11.5 %copy-start.1 = (bf16[200,1200]{1,0:T(8,128)(2,1)S(1)}, bf16[200,1200]{1,0:T(8,128)(2,1)}, u32[]{:S(2)}) copy-start(bf16[200,1200]{1,0:T(8,128)(2,1)} %param.19) | copy-start | bytes 1440004
  (42 other events, 257.5 us)
Sparse Core Ops, SparseCore 0:
  30.8 55.0 all-gather.4
  87.6 55.5 all-gather.6
  145.3 55.4 all-gather.8
  202.4 55.4 all-gather.10
  445.4 59.8 reduce-scatter.14
  507.4 60.1 reduce-scatter.12
  640.2 54.6 reduce-scatter.10
  716.0 62.9 reduce-scatter.16

commit v5 on v4

--- a/solution.py
+++ b/solution.py
@@ -29,7 +29,9 @@
 def peer_id(count, mask):
     if mask < count:
         return {"tp": lax.axis_index("tp") ^ mask}
-    return {"seq": lax.axis_index("seq") ^ 1}
+    if mask == count:
+        return {"seq": lax.axis_index("seq") ^ 1}
+    return {"seq": lax.axis_index("seq") ^ 1, "tp": lax.axis_index("tp") ^ (mask - count)}
 
 
 def meet(count, masks):
@@ -852,7 +854,7 @@
         targets = (refs[8],)
         scratch = refs[8:]
     weight, loaded, partial, from_core, over, from_side = scratch[:6]
-    core_send, core_recv, side_send, side_recv, cargo_sems, load_sems, save_sems, weight_sems = scratch[6:]
+    core_send, core_recv, side_send, side_recv, cargo_sems, load_sems, save_sems, weight_sems, held = scratch[6:]
     chunks, tokens, _ = over.shape
     steps = 4 * chunks
     high = count // 2
@@ -884,7 +886,13 @@
         bias_ref[...] = value
 
     def cargo():
-        return pass_block(count, part_ref, other_ref, cargo_sems)
+        return remote(count, part_ref, other_ref, cargo_sems.at[0], cargo_sems.at[1], count + high)
+
+    def take_part():
+        return pltpu.make_async_copy(part_ref, held, cargo_sems.at[0])
+
+    def keep_part():
+        return pltpu.make_async_copy(held, other_ref, cargo_sems.at[1])
 
     def load_blocks(start):
         for n, target in enumerate(targets):
@@ -893,9 +901,12 @@
     load_blocks(True)
     for part in range(len(sources)):
         load(0, part).start()
-    meet(count, masks + (high,))
+    meet(count, masks + (count + high,))
+    when(stays, lambda: take_part().start())
     when(jnp.logical_not(stays), lambda: cargo().start())
     load_blocks(False)
+    when(stays, lambda: take_part().wait())
+    when(stays, lambda: keep_part().start())
 
     @pl.loop(0, steps)
     def _(step):
@@ -953,8 +964,8 @@
         for step in range(steps - 2, steps):
             save(step).wait()
 
-    when(stays, lambda: cargo().wait_recv())
-    when(jnp.logical_not(stays), lambda: cargo().wait_send())
+    when(stays, lambda: keep_part().wait())
+    when(jnp.logical_not(stays), lambda: cargo().wait())
 
 
 def call_group(count, masks, backward, tiles, blocks, rest, part):
@@ -978,6 +989,7 @@
         pltpu.SemaphoreType.DMA((2, len(tiles))),
         pltpu.SemaphoreType.DMA((2,)),
         pltpu.SemaphoreType.DMA((2,)),
+        pltpu.VMEM(part.shape, BF16),
     ]
     if backward:
         outs.append(jax.ShapeDtypeStruct((chunks, pieces, tokens, width), BF16))
@@ -1232,7 +1244,7 @@
         )
         value = value.reshape(-1, hidden)
         contract_grad = dot(flat_rows, value, TN).astype(BF16)
-        other, norm_grad, hidden_grad, hidden_bias_grad = call_group(
+        contract_grad, norm_grad, hidden_grad, hidden_bias_grad = call_group(
             tp_count,
             masks,
             True,
@@ -1241,7 +1253,6 @@
             [],
             contract_grad,
         )
-        contract_grad = keep_block(contract_grad, other)
         proj_weight_grad = sum_seq(contract_grad)
         normal_two, hidden_grad = normal_two.reshape(-1, width), hidden_grad.reshape(-1, hidden)
         expand_grad = dot(normal_two, after(hidden_grad, contract_grad), TN).astype(BF16)
@@ -1275,7 +1286,8 @@
         def group_forward(expand_grad):
             members_value = value.reshape(members, -1, hidden)
             feed = [dot(members_value[d], contract, NT).astype(BF16) for d in range(members)]
-            return give_block(expand_grad), (residual + sum_ff(feed) + contract_bias).astype(BF16)
+            kept = keep_block(expand_grad, give_block(expand_grad))
+            return kept, (residual + sum_ff(feed) + contract_bias).astype(BF16)
 
 
     gain_two_grad, shift_two_grad, resid_grad, branch, head_grads, out_grad = from_second
@@ -1298,8 +1310,8 @@
 
 
     summed = lax.psum_scatter(qkv_grad, "seq", scatter_dimension=0, tiled=True)
-    other, layer_out = group_forward(after(expand_grad, qkv_grad))
-    expand_grad = keep_block(expand_grad, after(other, summed))
+    expand_grad, layer_out = group_forward(after(expand_grad, qkv_grad))
+    expand_grad = after(expand_grad, summed)
     fc_weight_grad = sum_seq(expand_grad)
 
     packed = from_block(after(summed, expand_grad))

time: 799 us -> 786 us (0.984)
  other arithmetic: 66 us -> 49.9 us
    convert_element_type x2 -> x0, other arithmetic: 16.2 us -> none  [keep_block(): return jnp.where(stays, partial.astype(F32) + other, 0.0).astype(BF16)]
  transfers between devices with their start and end apart: 25 -> 25, of which waited for: 7 -> 7; matrix products, arithmetic and copies ran while one was open for 16% -> 15% of each run, Pallas kernels for 50% -> 52%
where the time goes in v5:
time: 786 us; the launch traced here: 777 us
  Pallas kernels  538 us (68%)
  matrix products  87.1 us (11%)
  other arithmetic  49.9 us (6%)
  local copies, waits for them, and re-layouts  38.5 us (5%)
  waiting for transfers between devices  29.2 us (4%)
  starting transfers between devices  18 us (2%)
  between operations  15.7 us (2%)
    pallas_call x1, Pallas kernels, call_backward(): pl.pallas_call(functools.partial(backward_kernel, count, tokens // 2, hea...  147 us
    pallas_call x2, Pallas kernels, call_group(): pl.pallas_call(functools.partial(group_kernel, count, masks, backward), i...  143 us
    pallas_call x1, Pallas kernels, call_forward(): pl.pallas_call(functools.partial(forward_kernel, count, tokens // 2, head...  97.4 us
    dot_general x7, matrix products, dot(): return lax.dot_general(left, right, dims, preferred_element_type=F32)  87.1 us
    pallas_call x1, Pallas kernels, gather_rows(): pl.pallas_call(functools.partial(gather_kernel, count, tokens), in_specs=...  85.1 us
    pallas_call x1, Pallas kernels, call_hidden(): pl.pallas_call(functools.partial(hidden_kernel, count, masks), in_specs=[...  65.3 us
    ppermute x17, waiting for transfers between devices, swap(): return lax.ppermute(value, both, [(i, i ^ mask) for i in range(devices)])  20.8 us
    unnamed x134, local copies, waits for them, and re-layouts  17.8 us
  transfers between devices with their start and end apart: 25, of which 7 were waited for; matrix products, arithmetic and copies ran while one was open for 15% of the time, Pallas kernels for 52%

profile of v5, /device:TPU:0, one launch (start us, length us, event | category | flops | bytes accessed | tf_op | source)
XLA Modules:
  0.0 776.7 jit_solution(15475199639099772824)
XLA Ops:
  9.5 1.4 fusion.2
  11.8 3.9 collective-permute-start.3
  16.2 3.6 copy.73
  21.2 4.9 add_convert_fusion.2.own_ref
  26.2 1.3 select_select_fusion.9
  27.9 1.4 pad_maximum_fusion.1
  29.3 1.3 reshape.623
  31.5 3.0 collective-permute-start
  35.1 5.3 collective-permute-done
  40.5 2.6 collective-permute-done.1
  43.5 1.6 concatenate.29
  45.2 85.1 %gather_rows.1.rows_ref = bf16[3,1024,1600]{2,1,0:T(8,128)(2,1)} custom-call(bf16[768,1600]{1,0:T(8,128)(2,1)} %add_convert_fusion.2.own_ref), custom_call_target="tpu_custom_call" | custom-call | bytes 125829120 | tf_op jit(solution)/shard_map/gather_rows/pallas_call | solution.py:120
  132.0 3.0 copy.81
  136.1 7.0 all-gather.7.cloned.1.call-done.block_ref.whole_ref.refs_4_
  143.1 97.4 %attend_forward.1 = (bf16[3,1024,1536]{2,1,0:T(8,128)(2,1)}, bf16[4,768,512]{2,1,0:T(8,128)(2,1)}, f32[3,4,2,1024]{3,2,1,0:T(2,128)S(1)}, bf16[4,3,256,1600]{3,2,1,0:T(8,128)(2,1)}, bf16[1600,1600]{1,0:T(8,128)(2,1)}) custom-call(s32[3,8]{1,0:T(4,128)S(1)} %get-tuple-element.197.order_ref, s32[3,8]{1,0:T(4,128)S(1)} %get-tuple-element.198.place_ref, ...), custom_call_target="tpu_custom_call" | custom-call | flops 43285217280 | bytes 83886080 | tf_op jit(solution)/shard_map/attend_forward/pallas_call | solution.py:332
  240.6 2.2 select_bitcast_fusion.1
  244.5 5.2 concatenate.33
  249.7 9.2 %fusion.146 = (f32[768]{0:T(1024)S(1)}, f32[768,1600]{1,0:T(8,128)S(1)}) fusion(f32[1600]{0:T(1024)S(1)} %convert_element_type.132, bf16[1600,1600]{1,0:T(8,128)(2,1)} %all-gather.9.cloned.1.call-done, bf16[768,1792]{1,0:T(8,128)(2,1)} %concatenate.33, f32[3,256,1600]{2,1,0:T(8,128)} %copy.73), kind=kOutput, calls=%fused_computation.269 | convolution fusion | flops 3935845632 | bytes 17917184 | tf_op jit(solution)/shard_map/dot_general | solution.py:26
  259.6 1.5 copy-done.6
  262.1 65.3 %hidden_forward.1 = (bf16[3,4,256,1600]{3,2,1,0:T(8,128)(2,1)}, bf16[4,3,256,1600]{3,2,1,0:T(8,128)(2,1)}, bf16[3,4,256,1600]{3,2,1,0:T(8,128)(2,1)}, bf16[1600,1600]{1,0:T(8,128)(2,1)S(1)}) custom-call(bf16[768,1600]{1,0:T(8,128)(2,1)S(1)} %add_convert_fusion.1.own_ref, bf16[1600,1600]{1,0:T(8,128)(2,1)} %all-gather.7.cloned.1.call-done.block_ref.whole_ref.refs_4_, ...), custom_call_target="tpu_custom_call" | custom-call | flops 15728640000 | bytes 104857600 | tf_op jit(solution)/shard_map/hidden_forward/pallas_call | solution.py:814
  327.5 29.0 %bitcast_convert_fusion.refs_6_ = bf16[1600,1600]{1,0:T(8,128)(2,1)} fusion(bf16[4,3,256,1600]{3,2,1,0:T(8,128)(2,1)} %get-tuple-element.52.refs_0_, bf16[4,3,256,1600]{3,2,1,0:T(8,128)(2,1)} %get-tuple-element.49.refs_0_), kind=kOutput, calls=%fused_computation.1 | convolution fusion | flops 15731200000 | bytes 24780800 | tf_op jit(solution)/shard_map/dot_general | solution.py:26
  356.4 72.3 %group_backward.1 = (bf16[1600,1600]{1,0:T(8,128)(2,1)}, f32[768,1600]{1,0:T(8,128)}, bf16[3,4,256,1600]{3,2,1,0:T(8,128)(2,1)}, f32[1,1600]{1,0:T(1,128)}) custom-call(bf16[4,3,256,1600]{3,2,1,0:T(8,128)(2,1)} %get-tuple-element.52.refs_0_, bf16[3,4,256,1600]{3,2,1,0:T(8,128)(2,1)} %get-tuple-element.53.refs_1_, ...), custom_call_target="tpu_custom_call" | custom-call | flops 31457280000 | bytes 167772160 | tf_op jit(solution)/shard_map/group_backward/pallas_call | solution.py:998
  428.8 4.7 multiply_reduce_fusion.1
  433.6 2.2 convert_reduce_fusion
  435.8 2.2 copy-done.8
  438.1 7.1 convolution_convert_fusion
  445.8 27.5 %convolution_convert_fusion.1.refs_5_ = bf16[1600,1600]{1,0:T(8,128)(2,1)} fusion(bf16[3072,1600]{1,0:T(8,128)(2,1)} %bitcast.138, bf16[3072,1600]{1,0:T(8,128)(2,1)} %bitcast.139), kind=kOutput, calls=%fused_computation.4 | convolution fusion | flops 15731200000 | bytes 24780800 | tf_op jit(solution)/shard_map/dot_general | solution.py:26
  473.4 8.2 %convolution_convert_fusion.2 = bf16[768,1600]{1,0:T(8,128)(2,1)S(1)} fusion(bf16[1600,1600]{1,0:T(8,128)(2,1)} %all-gather.9.cloned.1.call-done, f32[768,1600]{1,0:T(8,128)S(1)} %bitcast.126), kind=kOutput, calls=%fused_computation.24 | convolution fusion | flops 3934617600 | bytes 12492800 | tf_op jit(solution)/shard_map/dot_general | solution.py:26
  484.4 1.9 pad_maximum_fusion.grad_ref
  486.3 147.2 %attend_backward.1 = (bf16[3,1024,1536]{2,1,0:T(8,128)(2,1)}, f32[768,1600]{1,0:T(8,128)}, bf16[1600,1536]{1,0:T(8,128)(2,1)}, f32[1,1536]{1,0:T(1,128)}) custom-call(s32[3,8]{1,0:T(4,128)} %copy-done.2, s32[3,8]{1,0:T(4,128)} %copy-done.3, bf16[3,1024,1536]{2,1,0:T(8,128)(2,1)} %get-tuple-element.58.qkv_ref, bf16[4,768,512]{2,1,0:T(8,128)(2,1)} %pad_maximum_fusion.grad_ref, ...), custom_call_target="tpu_custom_call" | custom-call | flops 60196651008 | bytes 83886080 | tf_op jit(solution)/shard_map/attend_backward/pallas_call | solution.py:665
  634.2 70.9 %group_forward.1 = (bf16[1600,1600]{1,0:T(8,128)(2,1)}, bf16[768,1600]{1,0:T(8,128)(2,1)}) custom-call(bf16[4,3,256,1600]{3,2,1,0:T(8,128)(2,1)} %get-tuple-element.49.refs_0_, bf16[1600,1600]{1,0:T(8,128)(2,1)} %all-gather.11.cloned.1.call-done.block_ref.refs_2_.refs_1_, bf16[1600,1600]{1,0:T(8,128)(2,1)} %copy-done.4, f32[768,1600]{1,0:T(8,128)} %copy-done.6, ...), custom_call_target="tpu_custom_call" | custom-call | flops 15728640000 | bytes 167772160 | tf_op jit(solution)/shard_map/group_forward/pallas_call | solution.py:998
  705.3 1.6 copy-done.13
  708.0 1.6 select_select_fusion.6
  710.1 2.2 select_select_fusion.4
  712.3 3.1 collective-permute-start.16
  715.5 4.6 copy.86
  721.7 3.6 slice_reduce_fusion.2
  726.4 5.2 multiply_reduce_fusion
  732.2 1.3 convert_add_fusion
  735.2 1.9 collective-permute-start.12
  737.3 9.1 %collective-permute-done.7 = f32[19200]{0:T(1024)S(1)} collective-permute-done((f32[19200]{0:T(1024)S(1)}, f32[19200]{0:T(1024)S(1)}, u32[]{:S(2)}, u32[]{:S(2)}) %collective-permute-start.7) | collective-permute-done | bytes 76832 | tf_op jit(solution)/shard_map/ppermute | solution.py:1072
  746.5 1.2 collective-permute-done.8
  747.8 6.5 add_convert_fusion
  754.3 2.7 copy.87
  757.1 1.5 collective-permute-start.10
  758.5 4.7 fusion.5
  763.2 2.2 collective-permute-done.10
  767.5 2.2 convert_element_type.149
  (269 shorter events, 26.1 us)
Async XLA Ops:
  7.2 128.9 %all-gather.5.cloned.1.call-start = ((), (), s32[]{:S(2)}) async-start(), calls=%async_computation.4 | async-start | bytes 5529600 | tf_op jit(solution)/shard_map/all_gather | solution.py:1150
  11.8 14.4 %collective-permute-start.3 = (bf16[200,512]{1,0:T(8,128)(2,1)S(1)}, bf16[200,512]{1,0:T(8,128)(2,1)S(1)}, u32[]{:S(2)}, u32[]{:S(2)}) collective-permute-start(bf16[200,512]{1,0:T(8,128)(2,1)S(1)} %get-tuple-element.158), channel_id=1, source_target_pairs={{0,3},{1,2},{2,1},{3,0},{4,7},{5,6},{6,5},{7,4},{8,11},{9,10},{10,... | collective-permute-start | bytes 614408 | tf_op jit(solution)/shard_map/ppermute | solution.py:1072
  15.7 10.5 %collective-permute-start.4 = (bf16[200,512]{1,0:T(8,128)(2,1)S(1)}, bf16[200,512]{1,0:T(8,128)(2,1)}, u32[]{:S(2)}, u32[]{:S(2)}) collective-permute-start(bf16[200,512]{1,0:T(8,128)(2,1)S(1)} %get-tuple-element.157), channel_id=1, source_target_pairs={{0,2},{1,3},{2,0},{3,1},{4,6},{5,7},{6,4},{7,5},{8,10},{9,11},{10,... | collective-permute-start | bytes 614408 | tf_op jit(solution)/shard_map/ppermute | solution.py:1072
  16.2 10.0 %collective-permute-start.5 = (bf16[200,512]{1,0:T(8,128)(2,1)S(1)}, bf16[200,512]{1,0:T(8,128)(2,1)}, u32[]{:S(2)}, u32[]{:S(2)}) collective-permute-start(bf16[200,512]{1,0:T(8,128)(2,1)S(1)} %get-tuple-element.156), channel_id=1, source_target_pairs={{0,1},{1,0},{2,3},{3,2},{4,5},{5,4},{6,7},{7,6},{8,9},{9,8},{10,11... | collective-permute-start | bytes 614408 | tf_op jit(solution)/shard_map/ppermute | solution.py:1072
  26.1 19.0 %copy-start.35 = (pred[512]{0:T(512)(128)(4,1)}, pred[512]{0:T(512)(128)(4,1)S(1)}, u32[]{:S(2)}) copy-start(pred[512]{0:T(512)(128)(4,1)S(1)} %get-tuple-element.191) | copy-start | bytes 1540
  26.1 19.0 %copy-start.37 = (pred[512]{0:T(512)(128)(4,1)}, pred[512]{0:T(512)(128)(4,1)S(1)}, u32[]{:S(2)}) copy-start(pred[512]{0:T(512)(128)(4,1)S(1)} %get-tuple-element.192) | copy-start | bytes 1540
  26.1 19.0 %copy-start.39 = (pred[512]{0:T(512)(128)(4,1)}, pred[512]{0:T(512)(128)(4,1)S(1)}, u32[]{:S(2)}) copy-start(pred[512]{0:T(512)(128)(4,1)S(1)} %get-tuple-element.193) | copy-start | bytes 1540
  26.1 19.0 %copy-start.41 = (pred[512]{0:T(512)(128)(4,1)}, pred[512]{0:T(512)(128)(4,1)S(1)}, u32[]{:S(2)}) copy-start(pred[512]{0:T(512)(128)(4,1)S(1)} %get-tuple-element.194) | copy-start | bytes 1540
  30.7 112.4 %all-gather.7.cloned.1.call-start = ((), (), s32[]{:S(2)}) async-start(), calls=%async_computation.5 | async-start | bytes 5990400 | tf_op jit(solution)/shard_map/all_gather | solution.py:1181
  31.5 218.2 %all-gather.9.cloned.1.call-start = ((), (), s32[]{:S(2)}) async-start(), calls=%async_computation.6 | async-start | bytes 5990400 | tf_op jit(solution)/shard_map/all_gather | solution.py:1181
  31.5 9.0 %collective-permute-start = (bf16[200,400]{1,0:T(8,128)(2,1)S(1)}, bf16[200,400]{1,0:T(8,128)(2,1)S(1)}, u32[]{:S(2)}, u32[]{:S(2)}) collective-permute-start(bf16[200,400]{1,0:T(8,128)(2,1)S(1)} %copy-done.20), channel_id=1, source_target_pairs={{0,3},{1,2},{2,1},{3,0},{4,7},{5,6},{6,5},{7,4},{8,11},{9,10},{10,... | collective-permute-start | bytes 480008 | tf_op jit(solution)/shard_map/ppermute | solution.py:1072
  34.5 8.6 %collective-permute-start.1 = (bf16[200,400]{1,0:T(8,128)(2,1)S(1)}, bf16[200,400]{1,0:T(8,128)(2,1)S(1)}, u32[]{:S(2)}, u32[]{:S(2)}) collective-permute-start(bf16[200,400]{1,0:T(8,128)(2,1)S(1)} %copy-done.20), channel_id=1, source_target_pairs={{0,2},{1,3},{2,0},{3,1},{4,6},{5,7},{6,4},{7,5},{8,10},{9,11},{10,... | collective-permute-start | bytes 480008 | tf_op jit(solution)/shard_map/ppermute | solution.py:1072
  35.0 8.4 %collective-permute-start.2 = (bf16[200,400]{1,0:T(8,128)(2,1)S(1)}, bf16[200,400]{1,0:T(8,128)(2,1)S(1)}, u32[]{:S(2)}, u32[]{:S(2)}) collective-permute-start(bf16[200,400]{1,0:T(8,128)(2,1)S(1)} %copy-done.20), channel_id=1, source_target_pairs={{0,1},{1,0},{2,3},{3,2},{4,5},{5,4},{6,7},{7,6},{8,9},{9,8},{10,11... | collective-permute-start | bytes 480008 | tf_op jit(solution)/shard_map/ppermute | solution.py:1072
  45.1 85.3 %copy-start.28 = (s32[3,1024]{1,0:T(4,128)S(1)}, s32[3,1024]{1,0:T(4,128)}, u32[]{:S(2)}) copy-start(s32[3,1024]{1,0:T(4,128)} %param.16) | copy-start | bytes 36868
  45.2 86.5 %copy-start.27 = (bf16[2,1600]{1,0:T(2,128)(2,1)S(1)}, bf16[2,1600]{1,0:T(2,128)(2,1)}, u32[]{:S(2)}) copy-start(bf16[2,1600]{1,0:T(2,128)(2,1)} %param.20) | copy-start | bytes 19204
  45.2 86.8 %copy-start.12 = (bf16[3,256,1600]{1,2,0:T(8,128)(2,1)S(1)}, bf16[3,256,1600]{1,2,0:T(8,128)(2,1)}, u32[]{:S(2)}) copy-start(bf16[3,256,1600]{1,2,0:T(8,128)(2,1)} %param.29) | copy-start | bytes 7372804
  130.3 131.8 %all-gather.11.cloned.1.call-start = ((), (), s32[]{:S(2)}) async-start(), calls=%async_computation.7 | async-start | bytes 5990400 | tf_op jit(solution)/shard_map/all_gather | solution.py:1181
  131.4 502.1 %reduce-scatter.15.cloned.1.call-start = ((), (), s32[]{:S(2)}) async-start(), calls=%async_computation.10 | async-start | bytes 5990400
  136.1 104.5 %copy-start.2 = (s32[3,8]{1,0:T(4,128)}, s32[3,8]{1,0:T(4,128)S(1)}, u32[]{:S(2)}) copy-start(s32[3,8]{1,0:T(4,128)S(1)} %get-tuple-element.197.order_ref) | copy-start | bytes 292
  136.1 104.5 %copy-start.3 = (s32[3,8]{1,0:T(4,128)}, s32[3,8]{1,0:T(4,128)S(1)}, u32[]{:S(2)}) copy-start(s32[3,8]{1,0:T(4,128)S(1)} %get-tuple-element.198.place_ref) | copy-start | bytes 292
  327.4 29.0 %copy-start.4 = (bf16[1600,1600]{1,0:T(8,128)(2,1)}, bf16[1600,1600]{1,0:T(8,128)(2,1)S(1)}, u32[]{:S(2)}) copy-start(bf16[1600,1600]{1,0:T(8,128)(2,1)S(1)} %get-tuple-element.50.refs_3_.refs_2_) | copy-start | bytes 15360004
  327.5 101.3 %slice-start = ((s8[5111808]{0:T(1024)(128)(4,1)}), s8[4194304]{0:T(1024)(128)(4,1)S(1)}, s32[]{:S(2)}) async-start(s8[5111808]{0:T(1024)(128)(4,1)} %bitcast.123), calls=%async_computation.12 | async-start | bytes 8388608
  356.4 72.3 %slice-start.1 = ((s8[5111808]{0:T(1024)(128)(4,1)}), s8[917504]{0:T(1024)(128)(4,1)S(1)}, s32[]{:S(2)}) async-start(s8[5111808]{0:T(1024)(128)(4,1)} %bitcast.123), calls=%async_computation.13 | async-start | bytes 1835008
  445.2 188.4 %reduce-scatter.13.cloned.1.call-start = ((), (), s32[]{:S(2)}) async-start(), calls=%async_computation.9 | async-start | bytes 5990400
  445.2 28.1 %slice-start.2 = ((s8[5111808]{0:T(1024)(128)(4,1)}), s8[917504]{0:T(1024)(128)(4,1)S(1)}, s32[]{:S(2)}) async-start(s8[5111808]{0:T(1024)(128)(4,1)} %bitcast.125), calls=%async_computation.14 | async-start | bytes 1835008
  445.7 259.5 %reduce-scatter.11.cloned.1.call-start = ((), (), s32[]{:S(2)}) async-start(), calls=%async_computation.8 | async-start | bytes 5529600 | tf_op jit(solution)/shard_map/reduce_scatter | solution.py:1312
  445.8 27.6 %slice-start.3 = ((s8[5111808]{0:T(1024)(128)(4,1)}), s8[4194304]{0:T(1024)(128)(4,1)S(1)}, s32[]{:S(2)}) async-start(s8[5111808]{0:T(1024)(128)(4,1)} %bitcast.125), calls=%async_computation.15 | async-start | bytes 8388608
  486.3 147.3 %copy-start.60 = (bf16[1600]{0:T(1024)(128)(2,1)S(1)}, bf16[1600]{0:T(1024)(128)(2,1)}, u32[]{:S(2)}) copy-start(bf16[1600]{0:T(1024)(128)(2,1)} %param.28) | copy-start | bytes 9604
  633.6 133.9 %reduce-scatter.17.cloned.1.call-start = ((), (), s32[]{:S(2)}) async-start(), calls=%async_computation.11 | async-start | bytes 5990400
  707.3 12.8 %copy-start.18 = (bf16[200,1600]{1,0:T(8,128)(2,1)S(1)}, bf16[200,1600]{1,0:T(8,128)(2,1)}, u32[]{:S(2)}) copy-start(bf16[200,1600]{1,0:T(8,128)(2,1)} %reduce-scatter.13.cloned.1.call-done) | copy-start | bytes 1920004
  707.3 14.0 %copy-start.19 = (bf16[200,1536]{1,0:T(8,128)(2,1)S(1)}, bf16[200,1536]{1,0:T(8,128)(2,1)}, u32[]{:S(2)}) copy-start(bf16[200,1536]{1,0:T(8,128)(2,1)} %reduce-scatter.11.cloned.1.call-done) | copy-start | bytes 1843204
  709.6 22.6 %collective-permute-start.14 = (bf16[200,400]{1,0:T(8,128)(2,1)S(1)}, bf16[200,400]{1,0:T(8,128)(2,1)S(1)}, u32[]{:S(2)}, u32[]{:S(2)}) collective-permute-start(bf16[200,400]{1,0:T(8,128)(2,1)S(1)} %get-tuple-element.163), channel_id=1, source_target_pairs={{0,1},{1,0},{2,3},{3,2},{4,5},{5,4},{6,7},{7,6},{8,9},{9,8},{10,11... | collective-permute-start | bytes 480008 | tf_op jit(solution)/shard_map/ppermute | solution.py:1072
  710.1 22.1 %collective-permute-start.15 = (bf16[200,400]{1,0:T(8,128)(2,1)S(1)}, bf16[200,400]{1,0:T(8,128)(2,1)S(1)}, u32[]{:S(2)}, u32[]{:S(2)}) collective-permute-start(bf16[200,400]{1,0:T(8,128)(2,1)S(1)} %get-tuple-element.164), channel_id=1, source_target_pairs={{0,2},{1,3},{2,0},{3,1},{4,6},{5,7},{6,4},{7,5},{8,10},{9,11},{10,... | collective-permute-start | bytes 480008 | tf_op jit(solution)/shard_map/ppermute | solution.py:1072
  712.3 19.9 %collective-permute-start.16 = (bf16[200,400]{1,0:T(8,128)(2,1)}, bf16[200,400]{1,0:T(8,128)(2,1)S(1)}, u32[]{:S(2)}, u32[]{:S(2)}) collective-permute-start(bf16[200,400]{1,0:T(8,128)(2,1)} %select_select_fusion.4), channel_id=1, source_target_pairs={{0,3},{1,2},{2,1},{3,0},{4,7},{5,6},{6,5},{7,4},{8,11},{9,10},{10,... | collective-permute-start | bytes 480008 | tf_op jit(solution)/shard_map/ppermute | solution.py:1072
  715.4 9.9 %copy-start.40 = (pred[512]{0:T(512)(128)(4,1)S(1)}, pred[512]{0:T(512)(128)(4,1)}, u32[]{:S(2)}) copy-start(pred[512]{0:T(512)(128)(4,1)} %copy-done.39) | copy-start | bytes 1540
  715.4 9.9 %copy-start.42 = (pred[512]{0:T(512)(128)(4,1)S(1)}, pred[512]{0:T(512)(128)(4,1)}, u32[]{:S(2)}) copy-start(pred[512]{0:T(512)(128)(4,1)} %copy-done.41) | copy-start | bytes 1540
  715.5 10.9 %copy-start.22 = (f32[1600]{0:T(1024)S(1)}, f32[1600]{0:T(1024)}, u32[]{:S(2)}) copy-start(f32[1600]{0:T(1024)} %copy-done.21) | copy-start | bytes 19204
  715.5 10.8 %copy-start.24 = (f32[768]{0:T(1024)S(1)}, f32[768]{0:T(1024)}, u32[]{:S(2)}) copy-start(f32[768]{0:T(1024)} %copy-done.23) | copy-start | bytes 9220
  715.5 10.8 %copy-start.26 = (f32[768]{0:T(1024)S(1)}, f32[768]{0:T(1024)}, u32[]{:S(2)}) copy-start(f32[768]{0:T(1024)} %copy-done.25) | copy-start | bytes 9220
  731.7 5.3 collective-permute-start.6
  733.6 25.0 %collective-permute-start.13 = (bf16[200,512]{1,0:T(8,128)(2,1)S(1)}, bf16[200,512]{1,0:T(8,128)(2,1)}, u32[]{:S(2)}, u32[]{:S(2)}) collective-permute-start(bf16[200,512]{1,0:T(8,128)(2,1)S(1)} %get-tuple-element.168), channel_id=1, source_target_pairs={{0,3},{1,2},{2,1},{3,0},{4,7},{5,6},{6,5},{7,4},{8,11},{9,10},{10,... | collective-permute-start | bytes 614408 | tf_op jit(solution)/shard_map/ppermute | solution.py:1072
  734.6 24.0 %collective-permute-start.11 = (bf16[200,512]{1,0:T(8,128)(2,1)}, bf16[200,512]{1,0:T(8,128)(2,1)}, u32[]{:S(2)}, u32[]{:S(2)}) collective-permute-start(bf16[200,512]{1,0:T(8,128)(2,1)} %get-tuple-element.167), channel_id=1, source_target_pairs={{0,1},{1,0},{2,3},{3,2},{4,5},{5,4},{6,7},{7,6},{8,9},{9,8},{10,11... | collective-permute-start | bytes 614408 | tf_op jit(solution)/shard_map/ppermute | solution.py:1072
  735.2 23.3 %collective-permute-start.12 = (bf16[200,512]{1,0:T(8,128)(2,1)}, bf16[200,512]{1,0:T(8,128)(2,1)}, u32[]{:S(2)}, u32[]{:S(2)}) collective-permute-start(bf16[200,512]{1,0:T(8,128)(2,1)} %get-tuple-element.166), channel_id=1, source_target_pairs={{0,2},{1,3},{2,0},{3,1},{4,6},{5,7},{6,4},{7,5},{8,10},{9,11},{10,... | collective-permute-start | bytes 614408 | tf_op jit(solution)/shard_map/ppermute | solution.py:1072
  737.1 9.3 %collective-permute-start.7 = (f32[19200]{0:T(1024)S(1)}, f32[19200]{0:T(1024)S(1)}, u32[]{:S(2)}, u32[]{:S(2)}) collective-permute-start(f32[19200]{0:T(1024)S(1)} %add.540), channel_id=1, source_target_pairs={{0,2},{1,3},{2,0},{3,1},{4,6},{5,7},{6,4},{7,5},{8,10},{9,11},{10,... | collective-permute-start | bytes 230408 | tf_op jit(solution)/shard_map/ppermute | solution.py:1072
  746.4 1.3 collective-permute-start.8
  747.7 9.3 %collective-permute-start.9 = (f32[19200]{0:T(1024)S(1)}, f32[19200]{0:T(1024)S(1)}, u32[]{:S(2)}, u32[]{:S(2)}) collective-permute-start(f32[19200]{0:T(1024)S(1)} %add.542), channel_id=1, source_target_pairs={{0,8},{1,9},{2,10},{3,11},{4,12},{5,13},{6,14},{7,15},{8,0},{9,1},... | collective-permute-start | bytes 230408 | tf_op jit(solution)/shard_map/ppermute | solution.py:1072
  757.1 8.4 %collective-permute-start.10 = (f32[19200]{0:T(1024)S(1)}, f32[19200]{0:T(1024)S(1)}, u32[]{:S(2)}, u32[]{:S(2)}) collective-permute-start(f32[19200]{0:T(1024)S(1)} %add.543), channel_id=1, source_target_pairs={{0,16},{1,17},{2,18},{3,19},{4,20},{5,21},{6,22},{7,23},{8,24},{9,... | collective-permute-start | bytes 230408 | tf_op jit(solution)/shard_map/ppermute | solution.py:1072
  758.5 11.2 %copy-start.1 = (bf16[200,1200]{1,0:T(8,128)(2,1)S(1)}, bf16[200,1200]{1,0:T(8,128)(2,1)}, u32[]{:S(2)}) copy-start(bf16[200,1200]{1,0:T(8,128)(2,1)} %param.19) | copy-start | bytes 1440004
  (42 other events, 255.8 us)
Sparse Core Ops, SparseCore 0:
  30.8 55.0 all-gather.4
  87.6 55.5 all-gather.6
  145.3 55.4 all-gather.8
  202.4 55.4 all-gather.10
  445.3 60.0 reduce-scatter.14
  507.5 60.1 reduce-scatter.12
  633.7 54.3 reduce-scatter.10
  705.4 61.1 reduce-scatter.16

commit v6 on v5

--- a/solution.py
+++ b/solution.py
@@ -1255,8 +1255,9 @@
         )
         proj_weight_grad = sum_seq(contract_grad)
         normal_two, hidden_grad = normal_two.reshape(-1, width), hidden_grad.reshape(-1, hidden)
-        expand_grad = dot(normal_two, after(hidden_grad, contract_grad), TN).astype(BF16)
         from_second = second_norm_back(norm_grad)
+        late_grad = after(hidden_grad, contract_grad, from_second[4])
+        expand_grad = dot(normal_two, late_grad, TN).astype(BF16)
 
         def group_forward(expand_grad):
             return call_group(

time: 786 us -> 782 us (level)
    unnamed x134 -> x142, local copies, waits for them, and re-layouts: 17.8 us -> 20.1 us
  transfers between devices with their start and end apart: 25 -> 25, of which waited for: 7 -> 7; matrix products, arithmetic and copies ran while one was open for 15% -> 14% of each run, Pallas kernels for 52% -> 52%
where the time goes in v6:
time: 782 us; the launch traced here: 774 us
  Pallas kernels  538 us (69%)
  matrix products  81.8 us (10%)
  other arithmetic  50.2 us (6%)
  local copies, waits for them, and re-layouts  40.7 us (5%)
  waiting for transfers between devices  29.2 us (4%)
  starting transfers between devices  18.2 us (2%)
  between operations  16.1 us (2%)
    pallas_call x1, Pallas kernels, call_backward(): pl.pallas_call(functools.partial(backward_kernel, count, tokens // 2, hea...  147 us
    pallas_call x2, Pallas kernels, call_group(): pl.pallas_call(functools.partial(group_kernel, count, masks, backward), i...  143 us
    pallas_call x1, Pallas kernels, call_forward(): pl.pallas_call(functools.partial(forward_kernel, count, tokens // 2, head...  97.4 us
    pallas_call x1, Pallas kernels, gather_rows(): pl.pallas_call(functools.partial(gather_kernel, count, tokens), in_specs=...  85.1 us
    dot_general x7, matrix products, dot(): return lax.dot_general(left, right, dims, preferred_element_type=F32)  81.8 us
    pallas_call x1, Pallas kernels, call_hidden(): pl.pallas_call(functools.partial(hidden_kernel, count, masks), in_specs=[...  65.3 us
    ppermute x17, waiting for transfers between devices, swap(): return lax.ppermute(value, both, [(i, i ^ mask) for i in range(devices)])  20.9 us
    unnamed x142, local copies, waits for them, and re-layouts  20.1 us
  transfers between devices with their start and end apart: 25, of which 7 were waited for; matrix products, arithmetic and copies ran while one was open for 14% of the time, Pallas kernels for 52%

profile of v6, /device:TPU:0, one launch (start us, length us, event | category | flops | bytes accessed | tf_op | source)
XLA Modules:
  0.0 774.2 jit_solution(13001528394593931111)
XLA Ops:
  9.5 1.4 fusion.2
  11.8 3.9 collective-permute-start.3
  16.2 3.6 copy.73
  21.1 4.8 add_convert_fusion.2.own_ref
  26.1 1.3 select_select_fusion.9
  27.8 1.4 pad_maximum_fusion.1
  29.2 1.3 reshape.623
  31.4 3.0 collective-permute-start
  35.0 5.3 collective-permute-done
  40.4 2.6 collective-permute-done.1
  43.4 1.6 concatenate.29
  45.1 85.1 %gather_rows.1.rows_ref = bf16[3,1024,1600]{2,1,0:T(8,128)(2,1)} custom-call(bf16[768,1600]{1,0:T(8,128)(2,1)} %add_convert_fusion.2.own_ref), custom_call_target="tpu_custom_call" | custom-call | bytes 125829120 | tf_op jit(solution)/shard_map/gather_rows/pallas_call | solution.py:120
  131.8 3.0 copy.81
  136.0 7.0 all-gather.7.cloned.1.call-done.block_ref.whole_ref.refs_4_
  143.0 97.4 %attend_forward.1 = (bf16[3,1024,1536]{2,1,0:T(8,128)(2,1)}, bf16[4,768,512]{2,1,0:T(8,128)(2,1)}, f32[3,4,2,1024]{3,2,1,0:T(2,128)S(1)}, bf16[4,3,256,1600]{3,2,1,0:T(8,128)(2,1)}, bf16[1600,1600]{1,0:T(8,128)(2,1)}) custom-call(s32[3,8]{1,0:T(4,128)S(1)} %get-tuple-element.197.order_ref, s32[3,8]{1,0:T(4,128)S(1)} %get-tuple-element.198.place_ref, ...), custom_call_target="tpu_custom_call" | custom-call | flops 43285217280 | bytes 83886080 | tf_op jit(solution)/shard_map/attend_forward/pallas_call | solution.py:332
  240.5 2.2 select_bitcast_fusion.1
  244.4 5.1 concatenate.33
  249.5 9.3 %fusion.146 = (f32[768]{0:T(1024)S(1)}, f32[768,1600]{1,0:T(8,128)S(1)}) fusion(f32[1600]{0:T(1024)S(1)} %convert_element_type.132, bf16[1600,1600]{1,0:T(8,128)(2,1)} %all-gather.9.cloned.1.call-done, bf16[768,1792]{1,0:T(8,128)(2,1)} %concatenate.33, f32[3,256,1600]{2,1,0:T(8,128)} %copy.73), kind=kOutput, calls=%fused_computation.269 | convolution fusion | flops 3935845632 | bytes 17917184 | tf_op jit(solution)/shard_map/dot_general | solution.py:26
  259.4 1.5 copy-done.6
  262.0 65.3 %hidden_forward.1 = (bf16[3,4,256,1600]{3,2,1,0:T(8,128)(2,1)}, bf16[4,3,256,1600]{3,2,1,0:T(8,128)(2,1)}, bf16[3,4,256,1600]{3,2,1,0:T(8,128)(2,1)}, bf16[1600,1600]{1,0:T(8,128)(2,1)S(1)}) custom-call(bf16[768,1600]{1,0:T(8,128)(2,1)S(1)} %add_convert_fusion.1.own_ref, bf16[1600,1600]{1,0:T(8,128)(2,1)} %all-gather.7.cloned.1.call-done.block_ref.whole_ref.refs_4_, ...), custom_call_target="tpu_custom_call" | custom-call | flops 15728640000 | bytes 104857600 | tf_op jit(solution)/shard_map/hidden_forward/pallas_call | solution.py:814
  327.3 28.9 %bitcast_convert_fusion.refs_6_ = bf16[1600,1600]{1,0:T(8,128)(2,1)} fusion(bf16[4,3,256,1600]{3,2,1,0:T(8,128)(2,1)} %get-tuple-element.52.refs_0_, bf16[4,3,256,1600]{3,2,1,0:T(8,128)(2,1)} %get-tuple-element.49.refs_0_), kind=kOutput, calls=%fused_computation.1 | convolution fusion | flops 15731200000 | bytes 24780800 | tf_op jit(solution)/shard_map/dot_general | solution.py:26
  356.2 72.3 %group_backward.1 = (bf16[1600,1600]{1,0:T(8,128)(2,1)}, f32[768,1600]{1,0:T(8,128)}, bf16[3,4,256,1600]{3,2,1,0:T(8,128)(2,1)}, f32[1,1600]{1,0:T(1,128)}) custom-call(bf16[4,3,256,1600]{3,2,1,0:T(8,128)(2,1)} %get-tuple-element.52.refs_0_, bf16[3,4,256,1600]{3,2,1,0:T(8,128)(2,1)} %get-tuple-element.53.refs_1_, ...), custom_call_target="tpu_custom_call" | custom-call | flops 31457280000 | bytes 167772160 | tf_op jit(solution)/shard_map/group_backward/pallas_call | solution.py:998
  428.6 4.9 multiply_reduce_fusion.1
  433.6 2.3 convert_reduce_fusion
  435.9 2.2 copy-done.8
  438.1 7.1 convolution_convert_fusion
  445.9 8.8 %convolution_convert_fusion.2 = bf16[768,1600]{1,0:T(8,128)(2,1)S(1)} fusion(bf16[1600,1600]{1,0:T(8,128)(2,1)} %all-gather.9.cloned.1.call-done, f32[768,1600]{1,0:T(8,128)} %copy-done.8), kind=kOutput, calls=%fused_computation.24 | convolution fusion | flops 3934617600 | bytes 12492800 | tf_op jit(solution)/shard_map/dot_general | solution.py:26
  457.6 1.9 pad_maximum_fusion.grad_ref
  460.3 1.5 slice-done.4
  461.8 21.7 %convolution_convert_fusion.1.refs_5_ = bf16[1600,1600]{1,0:T(8,128)(2,1)} fusion(bf16[3072,1600]{1,0:T(8,128)(2,1)S(1)} %bitcast.138, bf16[3072,1600]{1,0:T(8,128)(2,1)S(1)} %bitcast.141), kind=kOutput, calls=%fused_computation.4 | convolution fusion | flops 15731200000 | bytes 24780800 | tf_op jit(solution)/shard_map/dot_general | solution.py:26
  483.5 147.2 %attend_backward.1 = (bf16[3,1024,1536]{2,1,0:T(8,128)(2,1)}, f32[768,1600]{1,0:T(8,128)}, bf16[1600,1536]{1,0:T(8,128)(2,1)}, f32[1,1536]{1,0:T(1,128)}) custom-call(s32[3,8]{1,0:T(4,128)} %copy-done.2, s32[3,8]{1,0:T(4,128)} %copy-done.3, bf16[3,1024,1536]{2,1,0:T(8,128)(2,1)} %get-tuple-element.59.qkv_ref, bf16[4,768,512]{2,1,0:T(8,128)(2,1)} %pad_maximum_fusion.grad_ref, ...), custom_call_target="tpu_custom_call" | custom-call | flops 60196651008 | bytes 83886080 | tf_op jit(solution)/shard_map/attend_backward/pallas_call | solution.py:665
  631.5 70.6 %group_forward.1 = (bf16[1600,1600]{1,0:T(8,128)(2,1)}, bf16[768,1600]{1,0:T(8,128)(2,1)}) custom-call(bf16[4,3,256,1600]{3,2,1,0:T(8,128)(2,1)} %get-tuple-element.49.refs_0_, bf16[1600,1600]{1,0:T(8,128)(2,1)} %all-gather.11.cloned.1.call-done.block_ref.refs_2_.refs_1_, bf16[1600,1600]{1,0:T(8,128)(2,1)} %copy-done.4, f32[768,1600]{1,0:T(8,128)} %copy-done.6, ...), custom_call_target="tpu_custom_call" | custom-call | flops 15728640000 | bytes 167772160 | tf_op jit(solution)/shard_map/group_forward/pallas_call | solution.py:998
  702.1 1.6 copy-done.13
  704.8 1.7 select_select_fusion.6
  707.3 2.2 select_select_fusion.4
  709.5 2.8 collective-permute-start.16
  712.4 4.7 copy.86
  718.6 3.6 slice_reduce_fusion.2
  723.3 5.2 multiply_reduce_fusion
  729.4 1.3 convert_add_fusion
  732.2 2.0 collective-permute-start.12
  734.4 9.1 %collective-permute-done.7 = f32[19200]{0:T(1024)S(1)} collective-permute-done((f32[19200]{0:T(1024)S(1)}, f32[19200]{0:T(1024)S(1)}, u32[]{:S(2)}, u32[]{:S(2)}) %collective-permute-start.7) | collective-permute-done | bytes 76832 | tf_op jit(solution)/shard_map/ppermute | solution.py:1072
  744.9 6.5 add_convert_fusion
  751.4 2.7 copy.87
  754.2 1.6 collective-permute-start.10
  755.8 4.7 fusion.5
  760.5 2.2 collective-permute-done.10
  764.7 2.2 convert_element_type.149
  (278 shorter events, 28.4 us)
Async XLA Ops:
  7.2 128.8 %all-gather.5.cloned.1.call-start = ((), (), s32[]{:S(2)}) async-start(), calls=%async_computation.4 | async-start | bytes 5529600 | tf_op jit(solution)/shard_map/all_gather | solution.py:1150
  11.8 14.3 %collective-permute-start.3 = (bf16[200,512]{1,0:T(8,128)(2,1)S(1)}, bf16[200,512]{1,0:T(8,128)(2,1)S(1)}, u32[]{:S(2)}, u32[]{:S(2)}) collective-permute-start(bf16[200,512]{1,0:T(8,128)(2,1)S(1)} %get-tuple-element.158), channel_id=1, source_target_pairs={{0,3},{1,2},{2,1},{3,0},{4,7},{5,6},{6,5},{7,4},{8,11},{9,10},{10,... | collective-permute-start | bytes 614408 | tf_op jit(solution)/shard_map/ppermute | solution.py:1072
  15.7 10.4 %collective-permute-start.4 = (bf16[200,512]{1,0:T(8,128)(2,1)S(1)}, bf16[200,512]{1,0:T(8,128)(2,1)}, u32[]{:S(2)}, u32[]{:S(2)}) collective-permute-start(bf16[200,512]{1,0:T(8,128)(2,1)S(1)} %get-tuple-element.157), channel_id=1, source_target_pairs={{0,2},{1,3},{2,0},{3,1},{4,6},{5,7},{6,4},{7,5},{8,10},{9,11},{10,... | collective-permute-start | bytes 614408 | tf_op jit(solution)/shard_map/ppermute | solution.py:1072
  16.2 9.9 %collective-permute-start.5 = (bf16[200,512]{1,0:T(8,128)(2,1)S(1)}, bf16[200,512]{1,0:T(8,128)(2,1)}, u32[]{:S(2)}, u32[]{:S(2)}) collective-permute-start(bf16[200,512]{1,0:T(8,128)(2,1)S(1)} %get-tuple-element.156), channel_id=1, source_target_pairs={{0,1},{1,0},{2,3},{3,2},{4,5},{5,4},{6,7},{7,6},{8,9},{9,8},{10,11... | collective-permute-start | bytes 614408 | tf_op jit(solution)/shard_map/ppermute | solution.py:1072
  26.0 19.0 %copy-start.35 = (pred[512]{0:T(512)(128)(4,1)}, pred[512]{0:T(512)(128)(4,1)S(1)}, u32[]{:S(2)}) copy-start(pred[512]{0:T(512)(128)(4,1)S(1)} %get-tuple-element.191) | copy-start | bytes 1540
  26.0 19.0 %copy-start.37 = (pred[512]{0:T(512)(128)(4,1)}, pred[512]{0:T(512)(128)(4,1)S(1)}, u32[]{:S(2)}) copy-start(pred[512]{0:T(512)(128)(4,1)S(1)} %get-tuple-element.192) | copy-start | bytes 1540
  26.0 19.0 %copy-start.39 = (pred[512]{0:T(512)(128)(4,1)}, pred[512]{0:T(512)(128)(4,1)S(1)}, u32[]{:S(2)}) copy-start(pred[512]{0:T(512)(128)(4,1)S(1)} %get-tuple-element.193) | copy-start | bytes 1540
  26.0 19.0 %copy-start.41 = (pred[512]{0:T(512)(128)(4,1)}, pred[512]{0:T(512)(128)(4,1)S(1)}, u32[]{:S(2)}) copy-start(pred[512]{0:T(512)(128)(4,1)S(1)} %get-tuple-element.194) | copy-start | bytes 1540
  30.6 112.4 %all-gather.7.cloned.1.call-start = ((), (), s32[]{:S(2)}) async-start(), calls=%async_computation.5 | async-start | bytes 5990400 | tf_op jit(solution)/shard_map/all_gather | solution.py:1181
  31.4 218.2 %all-gather.9.cloned.1.call-start = ((), (), s32[]{:S(2)}) async-start(), calls=%async_computation.6 | async-start | bytes 5990400 | tf_op jit(solution)/shard_map/all_gather | solution.py:1181
  31.4 9.0 %collective-permute-start = (bf16[200,400]{1,0:T(8,128)(2,1)S(1)}, bf16[200,400]{1,0:T(8,128)(2,1)S(1)}, u32[]{:S(2)}, u32[]{:S(2)}) collective-permute-start(bf16[200,400]{1,0:T(8,128)(2,1)S(1)} %copy-done.20), channel_id=1, source_target_pairs={{0,3},{1,2},{2,1},{3,0},{4,7},{5,6},{6,5},{7,4},{8,11},{9,10},{10,... | collective-permute-start | bytes 480008 | tf_op jit(solution)/shard_map/ppermute | solution.py:1072
  34.4 8.6 %collective-permute-start.1 = (bf16[200,400]{1,0:T(8,128)(2,1)S(1)}, bf16[200,400]{1,0:T(8,128)(2,1)S(1)}, u32[]{:S(2)}, u32[]{:S(2)}) collective-permute-start(bf16[200,400]{1,0:T(8,128)(2,1)S(1)} %copy-done.20), channel_id=1, source_target_pairs={{0,2},{1,3},{2,0},{3,1},{4,6},{5,7},{6,4},{7,5},{8,10},{9,11},{10,... | collective-permute-start | bytes 480008 | tf_op jit(solution)/shard_map/ppermute | solution.py:1072
  34.9 8.4 %collective-permute-start.2 = (bf16[200,400]{1,0:T(8,128)(2,1)S(1)}, bf16[200,400]{1,0:T(8,128)(2,1)S(1)}, u32[]{:S(2)}, u32[]{:S(2)}) collective-permute-start(bf16[200,400]{1,0:T(8,128)(2,1)S(1)} %copy-done.20), channel_id=1, source_target_pairs={{0,1},{1,0},{2,3},{3,2},{4,5},{5,4},{6,7},{7,6},{8,9},{9,8},{10,11... | collective-permute-start | bytes 480008 | tf_op jit(solution)/shard_map/ppermute | solution.py:1072
  45.0 85.3 %copy-start.28 = (s32[3,1024]{1,0:T(4,128)S(1)}, s32[3,1024]{1,0:T(4,128)}, u32[]{:S(2)}) copy-start(s32[3,1024]{1,0:T(4,128)} %param.16) | copy-start | bytes 36868
  45.0 86.5 %copy-start.27 = (bf16[2,1600]{1,0:T(2,128)(2,1)S(1)}, bf16[2,1600]{1,0:T(2,128)(2,1)}, u32[]{:S(2)}) copy-start(bf16[2,1600]{1,0:T(2,128)(2,1)} %param.20) | copy-start | bytes 19204
  45.1 86.8 %copy-start.12 = (bf16[3,256,1600]{1,2,0:T(8,128)(2,1)S(1)}, bf16[3,256,1600]{1,2,0:T(8,128)(2,1)}, u32[]{:S(2)}) copy-start(bf16[3,256,1600]{1,2,0:T(8,128)(2,1)} %param.29) | copy-start | bytes 7372804
  130.2 131.7 %all-gather.11.cloned.1.call-start = ((), (), s32[]{:S(2)}) async-start(), calls=%async_computation.7 | async-start | bytes 5990400 | tf_op jit(solution)/shard_map/all_gather | solution.py:1181
  131.3 499.4 %reduce-scatter.15.cloned.1.call-start = ((), (), s32[]{:S(2)}) async-start(), calls=%async_computation.10 | async-start | bytes 5990400
  136.0 104.4 %copy-start.2 = (s32[3,8]{1,0:T(4,128)}, s32[3,8]{1,0:T(4,128)S(1)}, u32[]{:S(2)}) copy-start(s32[3,8]{1,0:T(4,128)S(1)} %get-tuple-element.197.order_ref) | copy-start | bytes 292
  136.0 104.5 %copy-start.3 = (s32[3,8]{1,0:T(4,128)}, s32[3,8]{1,0:T(4,128)S(1)}, u32[]{:S(2)}) copy-start(s32[3,8]{1,0:T(4,128)S(1)} %get-tuple-element.198.place_ref) | copy-start | bytes 292
  327.3 28.9 %copy-start.4 = (bf16[1600,1600]{1,0:T(8,128)(2,1)}, bf16[1600,1600]{1,0:T(8,128)(2,1)S(1)}, u32[]{:S(2)}) copy-start(bf16[1600,1600]{1,0:T(8,128)(2,1)S(1)} %get-tuple-element.50.refs_3_.refs_2_) | copy-start | bytes 15360004
  327.3 101.3 %slice-start = ((s8[5111808]{0:T(1024)(128)(4,1)}), s8[4194304]{0:T(1024)(128)(4,1)S(1)}, s32[]{:S(2)}) async-start(s8[5111808]{0:T(1024)(128)(4,1)} %bitcast.123), calls=%async_computation.12 | async-start | bytes 8388608
  356.2 72.4 %slice-start.1 = ((s8[5111808]{0:T(1024)(128)(4,1)}), s8[917504]{0:T(1024)(128)(4,1)S(1)}, s32[]{:S(2)}) async-start(s8[5111808]{0:T(1024)(128)(4,1)} %bitcast.123), calls=%async_computation.13 | async-start | bytes 1835008
  445.2 185.6 %reduce-scatter.13.cloned.1.call-start = ((), (), s32[]{:S(2)}) async-start(), calls=%async_computation.9 | async-start | bytes 5990400
  445.8 256.3 %reduce-scatter.11.cloned.1.call-start = ((), (), s32[]{:S(2)}) async-start(), calls=%async_computation.8 | async-start | bytes 5529600 | tf_op jit(solution)/shard_map/reduce_scatter | solution.py:1313
  445.8 13.6 %slice-start.5 = ((s8[10223616]{0:T(1024)(128)(4,1)}), s8[4194304]{0:T(1024)(128)(4,1)S(1)}, s32[]{:S(2)}) async-start(s8[10223616]{0:T(1024)(128)(4,1)} %bitcast.139), calls=%async_computation.17 | async-start | bytes 8388608
  445.9 13.6 %slice-start.6 = ((s8[10223616]{0:T(1024)(128)(4,1)}), s8[4194304]{0:T(1024)(128)(4,1)S(1)}, s32[]{:S(2)}) async-start(s8[10223616]{0:T(1024)(128)(4,1)} %bitcast.139), calls=%async_computation.18 | async-start | bytes 8388608
  483.5 147.4 %copy-start.60 = (bf16[1600]{0:T(1024)(128)(2,1)S(1)}, bf16[1600]{0:T(1024)(128)(2,1)}, u32[]{:S(2)}) copy-start(bf16[1600]{0:T(1024)(128)(2,1)} %param.28) | copy-start | bytes 9604
  630.8 133.8 %reduce-scatter.17.cloned.1.call-start = ((), (), s32[]{:S(2)}) async-start(), calls=%async_computation.11 | async-start | bytes 5990400
  704.2 12.9 %copy-start.18 = (bf16[200,1600]{1,0:T(8,128)(2,1)S(1)}, bf16[200,1600]{1,0:T(8,128)(2,1)}, u32[]{:S(2)}) copy-start(bf16[200,1600]{1,0:T(8,128)(2,1)} %reduce-scatter.13.cloned.1.call-done) | copy-start | bytes 1920004
  704.2 14.1 %copy-start.19 = (bf16[200,1536]{1,0:T(8,128)(2,1)S(1)}, bf16[200,1536]{1,0:T(8,128)(2,1)}, u32[]{:S(2)}) copy-start(bf16[200,1536]{1,0:T(8,128)(2,1)} %reduce-scatter.11.cloned.1.call-done) | copy-start | bytes 1843204
  706.5 22.9 %collective-permute-start.14 = (bf16[200,400]{1,0:T(8,128)(2,1)S(1)}, bf16[200,400]{1,0:T(8,128)(2,1)S(1)}, u32[]{:S(2)}, u32[]{:S(2)}) collective-permute-start(bf16[200,400]{1,0:T(8,128)(2,1)S(1)} %get-tuple-element.163), channel_id=1, source_target_pairs={{0,1},{1,0},{2,3},{3,2},{4,5},{5,4},{6,7},{7,6},{8,9},{9,8},{10,11... | collective-permute-start | bytes 480008 | tf_op jit(solution)/shard_map/ppermute | solution.py:1072
  707.3 22.2 %collective-permute-start.15 = (bf16[200,400]{1,0:T(8,128)(2,1)S(1)}, bf16[200,400]{1,0:T(8,128)(2,1)S(1)}, u32[]{:S(2)}, u32[]{:S(2)}) collective-permute-start(bf16[200,400]{1,0:T(8,128)(2,1)S(1)} %get-tuple-element.164), channel_id=1, source_target_pairs={{0,2},{1,3},{2,0},{3,1},{4,6},{5,7},{6,4},{7,5},{8,10},{9,11},{10,... | collective-permute-start | bytes 480008 | tf_op jit(solution)/shard_map/ppermute | solution.py:1072
  709.5 20.0 %collective-permute-start.16 = (bf16[200,400]{1,0:T(8,128)(2,1)}, bf16[200,400]{1,0:T(8,128)(2,1)S(1)}, u32[]{:S(2)}, u32[]{:S(2)}) collective-permute-start(bf16[200,400]{1,0:T(8,128)(2,1)} %select_select_fusion.4), channel_id=1, source_target_pairs={{0,3},{1,2},{2,1},{3,0},{4,7},{5,6},{6,5},{7,4},{8,11},{9,10},{10,... | collective-permute-start | bytes 480008 | tf_op jit(solution)/shard_map/ppermute | solution.py:1072
  712.3 10.0 %copy-start.40 = (pred[512]{0:T(512)(128)(4,1)S(1)}, pred[512]{0:T(512)(128)(4,1)}, u32[]{:S(2)}) copy-start(pred[512]{0:T(512)(128)(4,1)} %copy-done.39) | copy-start | bytes 1540
  712.3 10.0 %copy-start.42 = (pred[512]{0:T(512)(128)(4,1)S(1)}, pred[512]{0:T(512)(128)(4,1)}, u32[]{:S(2)}) copy-start(pred[512]{0:T(512)(128)(4,1)} %copy-done.41) | copy-start | bytes 1540
  712.4 10.9 %copy-start.22 = (f32[1600]{0:T(1024)S(1)}, f32[1600]{0:T(1024)}, u32[]{:S(2)}) copy-start(f32[1600]{0:T(1024)} %copy-done.21) | copy-start | bytes 19204
  712.4 10.9 %copy-start.24 = (f32[768]{0:T(1024)S(1)}, f32[768]{0:T(1024)}, u32[]{:S(2)}) copy-start(f32[768]{0:T(1024)} %copy-done.23) | copy-start | bytes 9220
  712.4 10.9 %copy-start.26 = (f32[768]{0:T(1024)S(1)}, f32[768]{0:T(1024)}, u32[]{:S(2)}) copy-start(f32[768]{0:T(1024)} %copy-done.25) | copy-start | bytes 9220
  728.6 5.6 collective-permute-start.6
  730.8 25.0 %collective-permute-start.13 = (bf16[200,512]{1,0:T(8,128)(2,1)S(1)}, bf16[200,512]{1,0:T(8,128)(2,1)}, u32[]{:S(2)}, u32[]{:S(2)}) collective-permute-start(bf16[200,512]{1,0:T(8,128)(2,1)S(1)} %get-tuple-element.168), channel_id=1, source_target_pairs={{0,3},{1,2},{2,1},{3,0},{4,7},{5,6},{6,5},{7,4},{8,11},{9,10},{10,... | collective-permute-start | bytes 614408 | tf_op jit(solution)/shard_map/ppermute | solution.py:1072
  731.5 24.2 %collective-permute-start.11 = (bf16[200,512]{1,0:T(8,128)(2,1)}, bf16[200,512]{1,0:T(8,128)(2,1)}, u32[]{:S(2)}, u32[]{:S(2)}) collective-permute-start(bf16[200,512]{1,0:T(8,128)(2,1)} %get-tuple-element.167), channel_id=1, source_target_pairs={{0,1},{1,0},{2,3},{3,2},{4,5},{5,4},{6,7},{7,6},{8,9},{9,8},{10,11... | collective-permute-start | bytes 614408 | tf_op jit(solution)/shard_map/ppermute | solution.py:1072
  732.2 23.5 %collective-permute-start.12 = (bf16[200,512]{1,0:T(8,128)(2,1)}, bf16[200,512]{1,0:T(8,128)(2,1)}, u32[]{:S(2)}, u32[]{:S(2)}) collective-permute-start(bf16[200,512]{1,0:T(8,128)(2,1)} %get-tuple-element.166), channel_id=1, source_target_pairs={{0,2},{1,3},{2,0},{3,1},{4,6},{5,7},{6,4},{7,5},{8,10},{9,11},{10,... | collective-permute-start | bytes 614408 | tf_op jit(solution)/shard_map/ppermute | solution.py:1072
  734.3 9.2 %collective-permute-start.7 = (f32[19200]{0:T(1024)S(1)}, f32[19200]{0:T(1024)S(1)}, u32[]{:S(2)}, u32[]{:S(2)}) collective-permute-start(f32[19200]{0:T(1024)S(1)} %add.540), channel_id=1, source_target_pairs={{0,2},{1,3},{2,0},{3,1},{4,6},{5,7},{6,4},{7,5},{8,10},{9,11},{10,... | collective-permute-start | bytes 230408 | tf_op jit(solution)/shard_map/ppermute | solution.py:1072
  743.5 1.3 collective-permute-start.8
  744.9 9.3 %collective-permute-start.9 = (f32[19200]{0:T(1024)S(1)}, f32[19200]{0:T(1024)S(1)}, u32[]{:S(2)}, u32[]{:S(2)}) collective-permute-start(f32[19200]{0:T(1024)S(1)} %add.542), channel_id=1, source_target_pairs={{0,8},{1,9},{2,10},{3,11},{4,12},{5,13},{6,14},{7,15},{8,0},{9,1},... | collective-permute-start | bytes 230408 | tf_op jit(solution)/shard_map/ppermute | solution.py:1072
  754.2 8.5 %collective-permute-start.10 = (f32[19200]{0:T(1024)S(1)}, f32[19200]{0:T(1024)S(1)}, u32[]{:S(2)}, u32[]{:S(2)}) collective-permute-start(f32[19200]{0:T(1024)S(1)} %add.543), channel_id=1, source_target_pairs={{0,16},{1,17},{2,18},{3,19},{4,20},{5,21},{6,22},{7,23},{8,24},{9,... | collective-permute-start | bytes 230408 | tf_op jit(solution)/shard_map/ppermute | solution.py:1072
  755.8 11.2 %copy-start.1 = (bf16[200,1200]{1,0:T(8,128)(2,1)S(1)}, bf16[200,1200]{1,0:T(8,128)(2,1)}, u32[]{:S(2)}) copy-start(bf16[200,1200]{1,0:T(8,128)(2,1)} %param.19) | copy-start | bytes 1440004
  (46 other events, 272.4 us)
Sparse Core Ops, SparseCore 0:
  30.7 55.0 all-gather.4
  87.5 55.5 all-gather.6
  145.2 55.4 all-gather.8
  202.3 55.4 all-gather.10
  445.3 60.0 reduce-scatter.14
  507.6 60.0 reduce-scatter.12
  630.9 54.1 reduce-scatter.10
  702.2 61.1 reduce-scatter.16
